TPU v7x, 32 devices: a whole 2x2x4 slice. The times are simulated.
32 devices in a mesh: groups: 2 (over y), res: 4 (over z), col: 2 (over x), seq: 2 (over core).
Axes of the slice: x: 2, y: 2, z: 4, core: 2. Of those that a mesh axis runs over, the one named last changes fastest.
Arguments:
- alignment_states: bfloat16 [128, 128, 256], P(('groups', 'res', 'seq'), 'col'), parts along dimension 0, may hold values from -6 to 6
- standardize_scale: float32 [256], replicated, may hold values from 0.5 to 1.5
- standardize_shift: float32 [256], replicated, may hold values from -3 to 3
- first_factor_coeffs: bfloat16 [256, 32], replicated, may hold values from -0.375 to 0.375
- first_factor_offset: float32 [32], replicated, may hold values from -3 to 3
- second_factor_coeffs: bfloat16 [256, 32], replicated, may hold values from -0.375 to 0.375
- second_factor_offset: float32 [32], replicated, may hold values from -3 to 3
- final_coeffs: bfloat16 [1024, 128], replicated, may hold values from -0.1875 to 0.1875
- final_offset: float32 [128], replicated, may hold values from -3 to 3
Outputs:
- pair: bfloat16 [4, 64, 128, 128], P('groups', ('res', 'seq'), 'col'), parts along dimension 0
There are 2 independent parts, one for each index of `groups`. A program takes and returns all parts, laid end to end along the dimension named above; an argument that names none is the same for every part. Nothing has to cross between parts.
All inputs are finite; a program needn't handle non-finite values.
Results may differ from a plain program's by a relative error of at most 0.0037.
Values may be sent and summed in bfloat16 or wider, within the bound.
No kernel may reach another device: no remote copies, remote signals or barrier semaphores. Data moves between devices by JAX's collectives and lax.ppermute only.
A program may use at most 64 MiB of HBM per device.

v0:
```python
import jax
import jax.numpy as jnp
from jax import lax
from jax.sharding import PartitionSpec as P


def project_both(rows, standardize_scale, standardize_shift, w_both, bias_both):
    input_tensor = rows.astype(jnp.float32)
    mean = jnp.mean(input_tensor, axis=-1, keepdims=True)
    centred = input_tensor - mean
    variance = jnp.mean(centred * centred, axis=-1, keepdims=True)
    normed = (centred * lax.rsqrt(variance + 1e-05) * standardize_scale + standardize_shift).astype(
        jnp.bfloat16
    )
    return (jnp.dot(normed, w_both, preferred_element_type=jnp.float32) + bias_both).astype(
        jnp.bfloat16
    )


def per_device(
    alignment_states,
    standardize_scale,
    standardize_shift,
    first_factor_coeffs,
    first_factor_offset,
    second_factor_coeffs,
    second_factor_offset,
    final_coeffs,
    final_offset,
):
    aligned_rows_each_shard, position_span, hidden_dimension = alignment_states.shape
    position_number = lax.axis_size("res")
    n_seq = lax.axis_size("seq")
    n_col = lax.axis_size("col")
    positions_each_shard = position_span // position_number
    chans = first_factor_coeffs.shape[1]
    seq_loc = aligned_rows_each_shard * position_number
    w_both = jnp.concatenate([first_factor_coeffs, second_factor_coeffs], axis=1)
    bias_both = jnp.concatenate([first_factor_offset, second_factor_offset])
    raw = lax.all_to_all(
        alignment_states.reshape(
            aligned_rows_each_shard, position_number, positions_each_shard * hidden_dimension
        ),
        "res",
        split_axis=1,
        concat_axis=0,
        tiled=True,
    )
    both = project_both(
        raw.reshape(seq_loc * positions_each_shard, hidden_dimension),
        standardize_scale,
        standardize_shift,
        w_both,
        bias_both,
    )
    both = both.reshape(seq_loc, positions_each_shard, 2 * chans)
    left_loc = both[:, :, :chans].reshape(seq_loc, positions_each_shard * chans)
    right_three = both[:, :, chans:]
    right_loc = right_three.transpose(1, 0, 2).reshape(positions_each_shard, seq_loc * chans)
    left_use = lax.all_to_all(left_loc, "seq", split_axis=1, concat_axis=0, tiled=True)
    right_use = lax.all_gather(right_loc, "seq", axis=1, tiled=True)
    rows_all = lax.all_gather(left_use, "col", axis=1, tiled=True)
    seqs = rows_all.shape[0]
    per_group = seqs // n_seq
    n_rows = rows_all.shape[1] // chans
    left_four = rows_all.reshape(n_seq, per_group, n_rows, chans)
    pair_width = final_coeffs.shape[1]
    w_deep = jnp.concatenate([final_coeffs] * n_seq, axis=0)

    def one_block(block):
        sub = block.shape[0]
        block = block.reshape(sub, n_seq, per_group, chans)
        outer = jnp.einsum("gsic,jgse->ijgce", left_four, block, preferred_element_type=jnp.float32)
        outer = outer.astype(jnp.bfloat16).reshape(n_rows * sub, n_seq * chans * chans)
        summed = jnp.dot(outer, w_deep, preferred_element_type=jnp.float32)
        return summed.reshape(n_rows, sub, pair_width)

    piece = lax.all_gather(right_use, "res", axis=0, tiled=True)
    count = piece.shape[0]
    sub = 1
    for option in range(1, 17):
        if count % option == 0:
            sub = option
    blocks = piece.reshape(count // sub, sub, piece.shape[1])
    results = lax.map(one_block, blocks)
    summed = results.transpose(1, 0, 2, 3).reshape(n_rows, count, pair_width)
    summed = summed.reshape(n_col, n_rows // n_col, summed.shape[1], pair_width)
    total = float(aligned_rows_each_shard * position_number * n_seq)
    return (summed / total + final_offset).astype(jnp.bfloat16)


def solution(mesh):
    return jax.shard_map(
        per_device,
        mesh=mesh,
        in_specs=(P(("groups", "res", "seq"), "col", None), P(), P(), P(), P(), P(), P(), P(), P()),
        out_specs=P("groups", ("res", "seq"), "col", None),
        check_vma=False,
    )
```

profile of v0, /device:TPU:0, one launch (start us, length us, event | category | flops | bytes accessed | tf_op | source)
XLA Modules:
  0.0 109.3 jit_solution(5657845986276746612)
XLA Ops:
  0.0 1.2 %reshape.58 = bf16[8,4,4096]{2,1,0:T(4,128)(2,1)S(1)} reshape(bf16[8,64,256]{2,1,0:T(8,128)(2,1)} %param.11) | data formatting | bytes 524288 | tf_op jit(solution)/shard_map/reshape | solution.py:41
  1.2 0.9 copy.21
  2.0 6.3 %all-to-all-start = ((bf16[8,4,4096]{2,0,1:T(8,128)(2,1)}), bf16[8,4,4096]{2,0,1:T(8,128)(2,1)S(1)}, u32[]{:S(2)}, u32[]{:S(2)}) async-start(bf16[8,4,4096]{2,0,1:T(8,128)(2,1)} %copy.21), calls=%async_computation | async-start | bytes 524288 | tf_op jit(solution)/shard_map/all_to_all | solution.py:40
  8.4 0.7 pad_maximum_fusion.1
  9.1 1.1 pad_maximum_fusion
  10.2 7.1 %all-to-all-done = bf16[8,4,4096]{2,0,1:T(8,128)(2,1)S(1)} async-done(((bf16[8,4,4096]{2,0,1:T(8,128)(2,1)}), bf16[8,4,4096]{2,0,1:T(8,128)(2,1)S(1)}, u32[]{:S(2)}, u32[]{:S(2)}) %all-to-all-start) | async-done | bytes 262176 | tf_op jit(solution)/shard_map/all_to_all | solution.py:40
  17.6 0.2 multiply_reduce_fusion
  17.9 0.3 fusion.4
  18.6 3.7 %all_to_all.28 = bf16[32,2,256]{2,0,1:T(8,128)(2,1)S(1)} all-to-all(bf16[32,2,256]{2,0,1:T(8,128)(2,1)S(1)} %copy.24), channel_id=1, replica_groups=mesh['groups'=2,'res'=4,'col'=2,'seq'=2] {'seq'}, dimensions={1} | all-to-all | bytes 65536 | tf_op jit(solution)/shard_map/all_to_all | solution.py:60
  22.4 4.6 %all_gather.11 = bf16[64,512]{1,0:T(8,128)(2,1)S(1)} all-gather(bf16[64,256]{1,0:T(8,128)(2,1)S(1)} %bitcast.55), channel_id=1, replica_groups=mesh['groups'=2,'res'=4,'col'=2,'seq'=2] {'col'}, dimensions={1}, use_global_device_ids=true | all-gather | bytes 98304 | tf_op jit(solution)/shard_map/all_gather | solution.py:62
  27.4 1.9 %all_gather.9 = bf16[16,2048]{1,0:T(8,128)(2,1)S(1)} all-gather(bf16[16,1024]{1,0:T(8,128)(2,1)S(1)} %reshape.60), channel_id=1, replica_groups=mesh['groups'=2,'res'=4,'col'=2,'seq'=2] {'seq'}, dimensions={1}, use_global_device_ids=true | all-gather | bytes 98304 | tf_op jit(solution)/shard_map/all_gather | solution.py:61
  29.3 13.8 %all_gather.10 = bf16[64,2048]{1,0:T(8,128)(2,1)S(1)} all-gather(bf16[16,2048]{1,0:T(8,128)(2,1)S(1)} %all_gather.9), channel_id=1, replica_groups=mesh['groups'=2,'res'=4,'col'=2,'seq'=2] {'res'}, dimensions={0}, use_global_device_ids=true | all-gather | bytes 327680 | tf_op jit(solution)/shard_map/all_gather | solution.py:78
  43.1 65.3 %while.10 = (s32[]{:T(128)}, f32[4,16,16,128]{3,2,1,0:T(8,128)S(1)}, bf16[4,16,2048]{2,1,0:T(8,128)(2,1)S(1)}, bf16[2,32,16,32]{3,1,2,0:T(8,128)(2,1)S(1)}, bf16[2048,128]{1,0:T(8,128)(2,1)S(1)}, /*index=5*/s32[]{:T(128)}) while((s32[]{:T(128)}, f32[4,16,16,128]{3,2,1,0:T(8,128)S(1)}, bf16[4,16,2048]{2,1,0:T(8,128)(2,1)S(1)}, ...), condition=%wide.region_3.4_spmd, body=%wide.region_2.3_spmd.sunk | while | flops 168296448 | bytes 7340109 | solution.py:85
  43.1 0.2 reshape.70
  43.3 3.2 %convert_bitcast_fusion.3 = bf16[16,16,2,32,32]{3,4,0,1,2:T(8,128)(2,1)} fusion(bf16[2,32,16,32]{3,1,2,0:T(8,128)(2,1)S(1)} %get-tuple-element.101, bf16[16,2,32,32]{3,2,1,0:T(8,128)(2,1)S(1)} %reshape.70), kind=kOutput, calls=%fused_computation.clone.1 | convolution fusion | flops 34078720 | bytes 1179648 | tf_op jit(solution)/shard_map/while/body/eval_jaxpr/gsic,jgse->ijgce/dot_general | solution.py:73
  46.5 6.4 %copy.36 = bf16[16,16,2,32,32]{4,3,2,1,0:T(8,128)(2,1)} copy(bf16[16,16,2,32,32]{3,4,0,1,2:T(8,128)(2,1)} %convert_bitcast_fusion.3) | data formatting | bytes 2097152 | tf_op jit(solution)/shard_map/while/body/eval_jaxpr/convert_element_type | solution.py:74
  52.9 6.0 %reshape.71 = bf16[16,16,2048]{2,1,0:T(8,128)(2,1)S(1)} reshape(bf16[16,16,2,32,32]{4,3,2,1,0:T(8,128)(2,1)} %copy.36) | data formatting | bytes 2097152 | tf_op jit(solution)/shard_map/reshape.23
  59.0 0.4 fusion.27
  59.4 0.2 reshape.70
  59.6 3.2 %convert_bitcast_fusion.3 = bf16[16,16,2,32,32]{3,4,0,1,2:T(8,128)(2,1)} fusion(bf16[2,32,16,32]{3,1,2,0:T(8,128)(2,1)S(1)} %get-tuple-element.101, bf16[16,2,32,32]{3,2,1,0:T(8,128)(2,1)S(1)} %reshape.70), kind=kOutput, calls=%fused_computation.clone.1 | convolution fusion | flops 34078720 | bytes 1179648 | tf_op jit(solution)/shard_map/while/body/eval_jaxpr/gsic,jgse->ijgce/dot_general | solution.py:73
  62.8 6.4 %copy.36 = bf16[16,16,2,32,32]{4,3,2,1,0:T(8,128)(2,1)} copy(bf16[16,16,2,32,32]{3,4,0,1,2:T(8,128)(2,1)} %convert_bitcast_fusion.3) | data formatting | bytes 2097152 | tf_op jit(solution)/shard_map/while/body/eval_jaxpr/convert_element_type | solution.py:74
  69.3 6.0 %reshape.71 = bf16[16,16,2048]{2,1,0:T(8,128)(2,1)S(1)} reshape(bf16[16,16,2,32,32]{4,3,2,1,0:T(8,128)(2,1)} %copy.36) | data formatting | bytes 2097152 | tf_op jit(solution)/shard_map/reshape.23
  75.3 0.4 fusion.27
  76.0 3.2 %convert_bitcast_fusion.3 = bf16[16,16,2,32,32]{3,4,0,1,2:T(8,128)(2,1)} fusion(bf16[2,32,16,32]{3,1,2,0:T(8,128)(2,1)S(1)} %get-tuple-element.101, bf16[16,2,32,32]{3,2,1,0:T(8,128)(2,1)S(1)} %reshape.70), kind=kOutput, calls=%fused_computation.clone.1 | convolution fusion | flops 34078720 | bytes 1179648 | tf_op jit(solution)/shard_map/while/body/eval_jaxpr/gsic,jgse->ijgce/dot_general | solution.py:73
  79.2 6.4 %copy.36 = bf16[16,16,2,32,32]{4,3,2,1,0:T(8,128)(2,1)} copy(bf16[16,16,2,32,32]{3,4,0,1,2:T(8,128)(2,1)} %convert_bitcast_fusion.3) | data formatting | bytes 2097152 | tf_op jit(solution)/shard_map/while/body/eval_jaxpr/convert_element_type | solution.py:74
  85.6 6.0 %reshape.71 = bf16[16,16,2048]{2,1,0:T(8,128)(2,1)S(1)} reshape(bf16[16,16,2,32,32]{4,3,2,1,0:T(8,128)(2,1)} %copy.36) | data formatting | bytes 2097152 | tf_op jit(solution)/shard_map/reshape.23
  91.6 0.4 fusion.27
  92.3 3.2 %convert_bitcast_fusion.3 = bf16[16,16,2,32,32]{3,4,0,1,2:T(8,128)(2,1)} fusion(bf16[2,32,16,32]{3,1,2,0:T(8,128)(2,1)S(1)} %get-tuple-element.101, bf16[16,2,32,32]{3,2,1,0:T(8,128)(2,1)S(1)} %reshape.70), kind=kOutput, calls=%fused_computation.clone.1 | convolution fusion | flops 34078720 | bytes 1179648 | tf_op jit(solution)/shard_map/while/body/eval_jaxpr/gsic,jgse->ijgce/dot_general | solution.py:73
  95.5 6.4 %copy.36 = bf16[16,16,2,32,32]{4,3,2,1,0:T(8,128)(2,1)} copy(bf16[16,16,2,32,32]{3,4,0,1,2:T(8,128)(2,1)} %convert_bitcast_fusion.3) | data formatting | bytes 2097152 | tf_op jit(solution)/shard_map/while/body/eval_jaxpr/convert_element_type | solution.py:74
  102.0 6.0 %reshape.71 = bf16[16,16,2048]{2,1,0:T(8,128)(2,1)S(1)} reshape(bf16[16,16,2,32,32]{4,3,2,1,0:T(8,128)(2,1)} %copy.36) | data formatting | bytes 2097152 | tf_op jit(solution)/shard_map/reshape.23
  108.0 0.4 fusion.27
  108.5 0.8 add_convert_fusion
  (32 shorter events, 1.6 us)
Async XLA Ops:
  0.0 17.8 %copy-start.4 = (f32[256]{0:T(256)S(1)}, f32[256]{0:T(256)}, u32[]{:S(2)}) copy-start(f32[256]{0:T(256)} %param.12) | copy-start | bytes 3076
  0.0 17.8 %copy-start.3 = (f32[256]{0:T(256)S(1)}, f32[256]{0:T(256)}, u32[]{:S(2)}) copy-start(f32[256]{0:T(256)} %param.13) | copy-start | bytes 3076
  0.0 17.8 %copy-start.2 = (bf16[256,32]{0,1:T(8,128)(2,1)S(1)}, bf16[256,32]{0,1:T(8,128)(2,1)}, u32[]{:S(2)}) copy-start(bf16[256,32]{0,1:T(8,128)(2,1)} %param.14) | copy-start | bytes 49156
  0.0 17.9 %copy-start.1 = (bf16[256,32]{0,1:T(8,128)(2,1)S(1)}, bf16[256,32]{0,1:T(8,128)(2,1)}, u32[]{:S(2)}) copy-start(bf16[256,32]{0,1:T(8,128)(2,1)} %param.16) | copy-start | bytes 49156
  2.0 15.2 %all-to-all-start = ((bf16[8,4,4096]{2,0,1:T(8,128)(2,1)}), bf16[8,4,4096]{2,0,1:T(8,128)(2,1)S(1)}, u32[]{:S(2)}, u32[]{:S(2)}) async-start(bf16[8,4,4096]{2,0,1:T(8,128)(2,1)} %copy.21), calls=%async_computation | async-start | bytes 524288 | tf_op jit(solution)/shard_map/all_to_all | solution.py:40
  43.1 65.4 %copy-start = (f32[128]{0:T(128)S(1)}, f32[128]{0:T(128)}, u32[]{:S(2)}) copy-start(f32[128]{0:T(128)} %param.19) | copy-start | bytes 1540
where the time goes:
time: 110 us; the launch traced here: 109 us
  local copies, waits for them, and re-layouts  53.6 us (49%)
  blocking collectives  24 us (22%)
  matrix products  15 us (14%)
  waiting for transfers between devices  7.1 us (6%)
  starting transfers between devices  6.33 us (6%)
  other arithmetic  3.04 us (3%)
    convert_element_type x4, local copies, waits for them, and re-layouts, one_block(): outer.astype(jnp.bfloat16).reshape(n_rows * sub, n_seq * chans * chans)  25.8 us
    another operation x4, local copies, waits for them, and re-layouts  24 us
    all_gather x1, blocking collectives, per_device(): piece = lax.all_gather(right_use, 'res', axis=0, tiled=True)  13.8 us
    dot_general x4, matrix products, one_block(): jnp.einsum('gsic,jgse->ijgce', left_four, block, preferred_element_type=j...  12.9 us
    all_to_all x1, waiting for transfers between devices, per_device(): lax.all_to_all(alignment_states.reshape(aligned_rows_each_shard, position...  7.1 us
    all_to_all x1, starting transfers between devices, per_device(): lax.all_to_all(alignment_states.reshape(aligned_rows_each_shard, position...  6.33 us
    all_gather x1, blocking collectives, per_device(): rows_all = lax.all_gather(left_use, 'col', axis=1, tiled=True)  4.58 us
    all_to_all x1, blocking collectives, per_device(): lax.all_to_all(left_loc, 'seq', split_axis=1, concat_axis=0, tiled=True)  3.75 us
  transfers between devices with their start and end apart: 1, of which 1 were waited for; matrix products, arithmetic and copies ran while one was open for 2% of the time, Pallas kernels for 0%

commit v1 on v0

v1 whole, which is shorter than its diff:
```python
import functools

import jax
import jax.numpy as jnp
from jax import lax
from jax.experimental import pallas as pl
from jax.experimental.pallas import tpu as pltpu
from jax.sharding import PartitionSpec as P

LANES = 128
SUBLANES = 8
VMEM = pl.BlockSpec(memory_space=pltpu.VMEM)


def partner(index, step, size):
    return index ^ step if size & (size - 1) == 0 else (index + step) % size


def lane_index(shape):
    return lax.broadcasted_iota(jnp.int32, shape, len(shape) - 1)


def project_kernel(dims, x_ref, scale_ref, shift_ref, w1_ref, b1_ref, w2_ref, b2_ref, *refs):
    n_res, n_col, _, _ = dims
    outs, (rows_scr, lane_scr, right_scr) = refs[:-3], refs[-3:]
    right_out, left_out = outs[0], outs[1]
    z_outs = outs[2 : 2 + n_res - 1]
    x_outs = outs[2 + n_res - 1 :]
    n_s, span, width = x_ref.shape
    chans = w1_ref.shape[1]
    fold = LANES // chans
    half = LANES // 2
    x = x_ref[...].reshape(n_s * span, width).astype(jnp.float32)
    mean = jnp.mean(x, axis=-1, keepdims=True)
    centred = x - mean
    variance = jnp.mean(centred * centred, axis=-1, keepdims=True)
    normed = (centred * lax.rsqrt(variance + 1e-05) * scale_ref[...] + shift_ref[...]).astype(jnp.bfloat16)

    spread = lax.broadcasted_iota(jnp.int32, (chans, LANES), 1) % chans
    spread = (spread == lax.broadcasted_iota(jnp.int32, (chans, LANES), 0)).astype(jnp.bfloat16)
    w1 = jnp.dot(w1_ref[...], spread, preferred_element_type=jnp.float32).astype(jnp.bfloat16)
    b1 = jnp.concatenate([b1_ref[...]] * fold, axis=1)
    rows_scr[...] = jnp.dot(normed, w1, preferred_element_type=jnp.float32) + b1
    n_rows = n_s * span // fold
    owner = lane_index((n_rows, LANES)) // chans
    merged = rows_scr[pl.ds(0, n_rows, stride=fold), :]
    for turn in range(1, fold):
        merged = jnp.where(owner == turn, rows_scr[pl.ds(turn, n_rows, stride=fold), :], merged)
    groups = span // fold
    for s in range(n_s):
        lane_scr[pl.ds(s, groups, stride=n_s), :] = merged[s * groups : (s + 1) * groups]
    left_out[...] = lane_scr[...].astype(jnp.bfloat16)

    eye = lax.broadcasted_iota(jnp.int32, (chans, chans), 0) == lane_index((chans, chans))
    w2 = lax.dot_general(
        eye.astype(jnp.bfloat16), w2_ref[...], (((1,), (1,)), ((), ())), preferred_element_type=jnp.float32
    ).astype(jnp.bfloat16)
    b2 = jnp.sum(jnp.where(eye, b2_ref[...], 0.0), axis=1, keepdims=True)
    right = lax.dot_general(w2, normed, (((1,), (1,)), ((), ())), preferred_element_type=jnp.float32) + b2
    pairs = chans // 2
    low = lane_index((pairs, LANES)) < half
    blocks = span // half
    for tile in range(n_s * span // LANES):
        here = right[:, tile * LANES : (tile + 1) * LANES]
        there = pltpu.roll(here, half, 1)
        for side in range(2):
            s, block = divmod(2 * tile + side, blocks)
            first, second = (here, there) if side == 0 else (there, here)
            right_scr[pl.ds(block * pairs * n_s + s, pairs, stride=n_s), :] = jnp.where(
                low, first[:pairs], second[pairs:]
            )
    right_slab = right_scr[...].astype(jnp.bfloat16)
    right_out[...] = right_slab

    here = lax.axis_index("res")
    n_right = right_slab.shape[0]
    part = left_out.shape[0] // n_res
    for k, out in enumerate(z_outs):
        out[:n_right] = right_slab
        out[n_right:] = left_out[pl.ds(pl.multiple_of(partner(here, k + 1, n_res) * part, part), part), :]
    for k, out in enumerate(x_outs):
        out[...] = left_out[pl.ds(pl.multiple_of(partner(here, k % n_res, n_res) * part, part), part), :]


def pack_kernel(dims, right_ref, left_ref, *refs):
    n_res, n_col, n_seq, step = dims
    ins, out = refs[:-1], refs[-1]
    z_ins, x_ins = ins[: n_res - 1], ins[n_res - 1 :]
    n_right = right_ref.shape[0]
    part = left_ref.shape[0] // n_res
    own = part // n_seq
    other = partner(lax.axis_index("seq"), step, n_seq)
    out[:n_right] = right_ref[...]
    for k, ref in enumerate(z_ins):
        out[(k + 1) * n_right : (k + 2) * n_right] = ref[:n_right]
    base = n_res * n_right
    start = pl.multiple_of(lax.axis_index("res") * part + other * own, own)
    out[base : base + own] = left_ref[pl.ds(start, own), :]
    for k, ref in enumerate(z_ins):
        at = base + (k + 1) * own
        out[at : at + own] = ref[pl.ds(pl.multiple_of(n_right + other * own, own), own), :]
    for k, ref in enumerate(x_ins):
        at = base + (n_res + k) * own
        out[at : at + own] = ref[pl.ds(pl.multiple_of(other * own, own), own), :]


def weight_kernel(w_ref, out_ref, scr):
    chans_sq, width = w_ref.shape
    chans = int(round(chans_sq**0.5))
    scr[...] = w_ref[...].astype(jnp.float32)
    pairs = chans // 2
    fold = LANES // chans
    order = [side * pairs + pair for pair in range(pairs) for side in range(2)]
    for tile in range(chans // fold):
        piece = jnp.concatenate(
            [scr[pl.ds(e, chans, stride=chans), :] for e in order[tile * fold : (tile + 1) * fold]], axis=0
        )
        out_ref[:, tile * LANES : (tile + 1) * LANES] = piece.T.astype(jnp.bfloat16)


def pair_kernel(dims, total, offset_ref, w_ref, right_ref, left_ref, *refs):
    n_res, n_col, n_seq, chans = dims
    out_ref, left_scr, outer_scr = refs[-3], refs[-2], refs[-1]
    ins = refs[:-3]
    z_ins = ins[: n_res - 1]
    x_ins = ins[n_res - 1 : n_res - 1 + (n_col - 1) * n_res]
    s_ins = ins[n_res - 1 + (n_col - 1) * n_res :]
    n_right = right_ref.shape[0]
    part = left_ref.shape[0] // n_res
    own = part // n_seq
    me = lax.axis_index("seq")
    half = LANES // 2
    fold = LANES // chans
    pairs = chans // 2
    rows_dev = out_ref.shape[1]
    turns = rows_dev // fold
    n_s = own // turns

    start = pl.multiple_of(lax.axis_index("res") * part + me * own, own)
    mine = pl.multiple_of(me * own, own)
    rights = [(right_ref, 0)] + [(ref, 0) for ref in z_ins]
    lefts = [[(left_ref, start)] + [(ref, pl.multiple_of(n_right + mine, own)) for ref in z_ins]]
    for u in range(n_col - 1):
        lefts.append([(x_ins[u * n_res + k], mine) for k in range(n_res)])
    for ref in s_ins:
        rights += [(ref, k * n_right) for k in range(n_res)]
        base = n_res * n_right
        for u in range(n_col):
            lefts[u] += [(ref, base + (u * n_res + k) * own) for k in range(n_res)]

    for u in range(n_col):
        slabs = [ref[pl.ds(at, own), :].astype(jnp.float32) for ref, at in lefts[u]]
        for turn in range(turns):
            column = jnp.concatenate([slab[turn * n_s : (turn + 1) * n_s] for slab in slabs], axis=0)
            depth = column.shape[0]
            left_scr[u * LANES : (u + 1) * LANES, turn * depth : (turn + 1) * depth] = column.T.astype(jnp.bfloat16)

    n_blocks = n_right // (pairs * n_s)
    offset = offset_ref[...]
    col = lax.axis_index("col")

    def block_of_columns(block):
        at_block = block * pairs * n_s
        slabs = [ref[pl.ds(at + at_block, pairs * n_s), :].astype(jnp.float32) for ref, at in rights]
        left = left_scr[...]
        for pair in range(pairs):
            here = jnp.concatenate([slab[pair * n_s : (pair + 1) * n_s] for slab in slabs], axis=0)
            there = pltpu.roll(here, half, 1)
            low = lane_index(here.shape) < half
            weights = jnp.concatenate(
                [
                    jnp.concatenate([jnp.where(low, here, 0.0), jnp.where(low, 0.0, there)], axis=0),
                    jnp.concatenate([jnp.where(low, there, 0.0), jnp.where(low, 0.0, here)], axis=0),
                ],
                axis=1,
            ).astype(jnp.bfloat16)
            outer = jnp.dot(left, weights, preferred_element_type=jnp.float32).astype(jnp.bfloat16)
            for side in range(2):
                at = (2 * pair + side) * chans
                for tile in range(n_col * fold):
                    outer_scr[at : at + chans, tile * LANES : (tile + 1) * LANES] = outer[
                        tile * chans : (tile + 1) * chans, side * LANES : (side + 1) * LANES
                    ]
        for u in range(n_col):
            summed = jnp.dot(
                w_ref[...],
                outer_scr[:, u * fold * LANES : (u + 1) * fold * LANES],
                preferred_element_type=jnp.float32,
            )
            to = partner(col, u, n_col) if n_col & (n_col - 1) == 0 else (col - u + n_col) % n_col
            for residue in range(fold):
                piece = summed[:, residue * LANES : (residue + 1) * LANES].T
                piece = (piece / total + offset).astype(jnp.bfloat16)
                for turn in range(turns):
                    out_ref[to, turn * fold + residue, pl.ds(block * half, half), :] = piece[
                        turn * half : (turn + 1) * half
                    ]

    if n_blocks == 1:
        block_of_columns(0)
    else:
        pl.loop(0, n_blocks)(block_of_columns)


def per_device(alignment, scale, shift, w1, b1, w2, b2, w_final, offset):
    n_s, span, width = alignment.shape
    n_res, n_col, n_seq = lax.axis_size("res"), lax.axis_size("col"), lax.axis_size("seq")
    chans, pair_width = w1.shape[1], w_final.shape[1]
    bf16 = jnp.bfloat16
    n_right = span * chans * n_s // LANES
    n_left = span * chans * n_s // LANES
    part = n_left // n_res
    own = part // n_seq
    rows_dev = span // (n_res * n_seq)
    slab = jax.ShapeDtypeStruct((n_right, LANES), bf16)
    z_slab = jax.ShapeDtypeStruct((n_right + part, LANES), bf16)
    x_slab = jax.ShapeDtypeStruct((part, LANES), bf16)
    n_x = (n_col - 1) * n_res
    dims = (n_res, n_col, n_seq)
    params = functools.partial(pltpu.CompilerParams, vmem_limit_bytes=32 * 1024 * 1024)

    made = pl.pallas_call(
        functools.partial(project_kernel, dims + (chans,)),
        out_shape=[slab, slab] + [z_slab] * (n_res - 1) + [x_slab] * n_x,
        in_specs=[VMEM] * 7,
        out_specs=[VMEM] * (2 + n_res - 1 + n_x),
        scratch_shapes=[
            pltpu.VMEM((n_s * span, LANES), jnp.float32),
            pltpu.VMEM((n_left, LANES), jnp.float32),
            pltpu.VMEM((n_right, LANES), jnp.float32),
        ],
        compiler_params=params(),
        name="project",
    )(alignment, scale.reshape(1, -1), shift.reshape(1, -1), w1, b1.reshape(1, -1), w2, b2.reshape(1, -1))
    right, left = made[0], made[1]

    def to_chip(array, step_col, step_res):
        pairs = []
        for r in range(n_res):
            for c in range(n_col):
                to = partner(r, step_res, n_res) * n_col + partner(c, step_col, n_col)
                pairs.append((r * n_col + c, to))
        return lax.ppermute(array, ("res", "col"), pairs)

    z_in = [to_chip(made[2 + k], 0, k + 1) for k in range(n_res - 1)]
    x_in = [to_chip(made[1 + n_res + k], 1 + k // n_res, k % n_res) for k in range(n_x)]

    weights = pl.pallas_call(
        weight_kernel,
        out_shape=jax.ShapeDtypeStruct((pair_width, chans * chans), bf16),
        in_specs=[VMEM],
        out_specs=VMEM,
        scratch_shapes=[pltpu.VMEM((chans * chans, pair_width), jnp.float32)],
        compiler_params=params(),
        name="weights",
    )(w_final)

    s_in = []
    for step in range(1, n_seq):
        packed = pl.pallas_call(
            functools.partial(pack_kernel, dims + (step,)),
            out_shape=jax.ShapeDtypeStruct((n_res * n_right + n_res * n_col * own, LANES), bf16),
            in_specs=[VMEM] * (2 + len(z_in) + len(x_in)),
            out_specs=VMEM,
            compiler_params=params(),
            name="pack",
        )(right, left, *z_in, *x_in)
        s_in.append(lax.ppermute(packed, "seq", [(q, partner(q, step, n_seq)) for q in range(n_seq)]))

    turns = rows_dev * chans // LANES
    depth = turns * n_s * n_res * n_seq
    return pl.pallas_call(
        functools.partial(pair_kernel, dims + (chans,), float(n_s * n_res * n_seq)),
        out_shape=jax.ShapeDtypeStruct((n_col, rows_dev, span, pair_width), bf16),
        in_specs=[VMEM] * (4 + len(z_in) + len(x_in) + len(s_in)),
        out_specs=VMEM,
        scratch_shapes=[
            pltpu.VMEM((n_col * LANES, depth), bf16),
            pltpu.VMEM((chans * chans, n_col * (LANES // chans) * LANES), bf16),
        ],
        compiler_params=params(),
        name="pair",
    )(offset.reshape(1, -1), weights, right, left, *z_in, *x_in, *s_in)


def solution(mesh):
    return jax.shard_map(
        per_device,
        mesh=mesh,
        in_specs=(P(("groups", "res", "seq"), "col", None), P(), P(), P(), P(), P(), P(), P(), P()),
        out_specs=P("groups", ("res", "seq"), "col", None),
        check_vma=False,
    )
```

time: 110 us -> 26 us (0.24)
  local copies, waits for them, and re-layouts: 53.6 us -> 2.62 us
  blocking collectives: 24 us -> 0 us
  matrix products: 15 us -> 0 us
  starting transfers between devices: 6.33 us -> 14.3 us
  Pallas kernels: 0 us -> 3.16 us
  other arithmetic: 3.04 us -> 0 us
  waiting for transfers between devices: 7.1 us -> 5.55 us
    convert_element_type x6 -> x0, local copies, waits for them, and re-layouts: 26 us -> none  [the longest x4 25.8 us: one_block(): outer.astype(jnp.bfloat16).reshape(n_rows * sub, n_seq * chans * chans)]
    another operation x4 -> x0, local copies, waits for them, and re-layouts: 24 us -> none
    all_gather x3 -> x0, blocking collectives: 20.2 us -> none  [the longest x1 13.8 us: per_device(): piece = lax.all_gather(right_use, 'res', axis=0, tiled=True)]
    dot_general x9 -> x0, matrix products: 15 us -> none  [the longest x4 12.9 us: one_block(): jnp.einsum('gsic,jgse->ijgce', left_four, block, preferred_element_type=j...]
    ppermute x0 -> x8, starting transfers between devices: none -> 14.3 us  [the longest x7 14.2 us: to_chip(): return lax.ppermute(array, ('res', 'col'), pairs)]
    all_to_all x1 -> x0, waiting for transfers between devices: 7.1 us -> none  [per_device(): lax.all_to_all(alignment_states.reshape(aligned_rows_each_shard, position...]
    all_to_all x1 -> x0, starting transfers between devices: 6.33 us -> none  [per_device(): lax.all_to_all(alignment_states.reshape(aligned_rows_each_shard, position...]
    ppermute x0 -> x8, waiting for transfers between devices: none -> 5.55 us  [the longest x7 4.6 us: to_chip(): return lax.ppermute(array, ('res', 'col'), pairs)]
  transfers between devices with their start and end apart: 1 -> 8, of which waited for: 1 -> 3; matrix products, arithmetic and copies ran while one was open for 2% -> 0% of each run, Pallas kernels for 0% -> 2%
where the time goes in v1:
time: 26 us; the launch traced here: 25.7 us
  starting transfers between devices  14.3 us (55%)
  waiting for transfers between devices  5.55 us (21%)
  Pallas kernels  3.16 us (12%)
  local copies, waits for them, and re-layouts  2.62 us (10%)
    ppermute x7, starting transfers between devices, to_chip(): return lax.ppermute(array, ('res', 'col'), pairs)  14.2 us
    ppermute x7, waiting for transfers between devices, to_chip(): return lax.ppermute(array, ('res', 'col'), pairs)  4.6 us
    unnamed x18, local copies, waits for them, and re-layouts  2.62 us
    pallas_call x1, Pallas kernels, per_device(): pl.pallas_call(functools.partial(pair_kernel, dims + (chans,), float(n_s...  2.14 us
    ppermute x1, waiting for transfers between devices, per_device(): lax.ppermute(packed, 'seq', [(q, partner(q, step, n_seq)) for q in range(...  0.95 us
    pallas_call x1, Pallas kernels, per_device(): pl.pallas_call(functools.partial(project_kernel, dims + (chans,)), out_sh...  0.61 us
  transfers between devices with their start and end apart: 8, of which 3 were waited for; matrix products, arithmetic and copies ran while one was open for 0% of the time, Pallas kernels for 2%

profile of v1, /device:TPU:0, one launch (start us, length us, event | category | flops | bytes accessed | tf_op | source)
XLA Modules:
  0.0 25.7 jit_solution(3153841031022878028)
XLA Ops:
  0.0 0.8 %copy.10.w1_ref = bf16[256,32]{1,0:T(8,128)(2,1)S(1)} copy(bf16[256,32]{0,1:T(8,128)(2,1)} %param.12) | data formatting | bytes 32768 | tf_op args[3]
  0.9 0.0 copy-done.7
  0.9 0.1 copy.11.w2_ref
  1.0 0.0 copy-start.3
  1.0 0.0 copy-start.5
  1.0 0.0 copy-start.2
  1.0 0.0 copy-start.4
  1.0 0.6 %copy-done.3 = f32[256]{0:T(256)S(1)} copy-done((f32[256]{0:T(256)S(1)}, f32[256]{0:T(256)}, u32[]{:S(2)}) %copy-start.3) | copy-done | bytes 1048
  1.7 0.0 copy-done.5
  1.7 0.0 copy-done.2
  1.7 0.9 %copy-done = bf16[8,64,256]{2,1,0:T(8,128)(2,1)S(1)} copy-done((bf16[8,64,256]{2,1,0:T(8,128)(2,1)S(1)}, bf16[8,64,256]{2,1,0:T(8,128)(2,1)}, u32[]{:S(2)}) %copy-start) | copy-done | bytes 262168
  2.6 0.6 %project.1 = (bf16[128,128]{1,0:T(8,128)(2,1)S(1)}, bf16[128,128]{1,0:T(8,128)(2,1)S(1)}, bf16[160,128]{1,0:T(8,128)(2,1)S(1)}, bf16[160,128]{1,0:T(8,128)(2,1)S...) custom-call(bf16[8,64,256]{2,1,0:T(8,128)(2,1)S(1)} %copy-done, ...), custom_call_target="tpu_custom_call" | custom-call | tf_op jit(solution)/shard_map/project/pallas_call | solution.py:222
  3.3 0.0 copy-start.1
  3.3 3.1 %collective-permute-start = (bf16[160,128]{1,0:T(8,128)(2,1)S(1)}, bf16[160,128]{1,0:T(8,128)(2,1)S(1)}, u32[]{:S(2)}, u32[]{:S(2)}) collective-permute-start(bf16[160,128]{1,0:T(8,128)(2,1)S(1)} %get-tuple-element.16), channel_id=1, source_target_pairs={{0,4},{2,6},{4,0},{6,2},{8,12},{10,14},{12,8},{14,10},{1,5},{3,7},... | collective-permute-start | bytes 122888 | tf_op jit(solution)/shard_map/ppermute | solution.py:243
  6.4 2.6 %collective-permute-start.1 = (bf16[160,128]{1,0:T(8,128)(2,1)S(1)}, bf16[160,128]{1,0:T(8,128)(2,1)S(1)}, u32[]{:S(2)}, u32[]{:S(2)}) collective-permute-start(bf16[160,128]{1,0:T(8,128)(2,1)S(1)} %get-tuple-element.17), channel_id=1, source_target_pairs={{0,8},{2,10},{4,12},{6,14},{8,0},{10,2},{12,4},{14,6},{1,9},{3,11}... | collective-permute-start | bytes 122888 | tf_op jit(solution)/shard_map/ppermute | solution.py:243
  9.0 0.0 collective-permute-start.2
  9.0 1.7 %collective-permute-start.3 = (bf16[32,128]{1,0:T(8,128)(2,1)S(1)}, bf16[32,128]{1,0:T(8,128)(2,1)S(1)}, u32[]{:S(2)}, u32[]{:S(2)}) collective-permute-start(bf16[32,128]{1,0:T(8,128)(2,1)S(1)} %get-tuple-element.19), channel_id=1, source_target_pairs={{0,2},{2,0},{4,6},{6,4},{8,10},{10,8},{12,14},{14,12},{1,3},{3,1},... | collective-permute-start | bytes 24584 | tf_op jit(solution)/shard_map/ppermute | solution.py:243
  10.7 0.7 %collective-permute-start.4 = (bf16[32,128]{1,0:T(8,128)(2,1)S(1)}, bf16[32,128]{1,0:T(8,128)(2,1)S(1)}, u32[]{:S(2)}, u32[]{:S(2)}) collective-permute-start(bf16[32,128]{1,0:T(8,128)(2,1)S(1)} %get-tuple-element.20), channel_id=1, source_target_pairs={{0,6},{2,4},{4,2},{6,0},{8,14},{10,12},{12,10},{14,8},{1,7},{3,5},... | collective-permute-start | bytes 24584 | tf_op jit(solution)/shard_map/ppermute | solution.py:243
  11.3 1.3 %collective-permute-done.3.refs_3_ = bf16[32,128]{1,0:T(8,128)(2,1)S(1)} collective-permute-done((bf16[32,128]{1,0:T(8,128)(2,1)S(1)}, bf16[32,128]{1,0:T(8,128)(2,1)S(1)}, u32[]{:S(2)}, u32[]{:S(2)}) %collective-permute-start.3) | collective-permute-done | bytes 8224 | tf_op jit(solution)/shard_map/ppermute | solution.py:243
  12.6 3.1 %collective-permute-start.5 = (bf16[32,128]{1,0:T(8,128)(2,1)S(1)}, bf16[32,128]{1,0:T(8,128)(2,1)S(1)}, u32[]{:S(2)}, u32[]{:S(2)}) collective-permute-start(bf16[32,128]{1,0:T(8,128)(2,1)S(1)} %get-tuple-element.21), channel_id=1, source_target_pairs={{0,10},{2,8},{4,14},{6,12},{8,2},{10,0},{12,6},{14,4},{1,11},{3,9}... | collective-permute-start | bytes 24584 | tf_op jit(solution)/shard_map/ppermute | solution.py:243
  15.7 0.0 collective-permute-done.4.refs_4_
  15.7 3.1 %collective-permute-start.6 = (bf16[32,128]{1,0:T(8,128)(2,1)S(1)}, bf16[32,128]{1,0:T(8,128)(2,1)S(1)}, u32[]{:S(2)}, u32[]{:S(2)}) collective-permute-start(bf16[32,128]{1,0:T(8,128)(2,1)S(1)} %get-tuple-element.22), channel_id=1, source_target_pairs={{0,14},{2,12},{4,10},{6,8},{8,6},{10,4},{12,2},{14,0},{1,15},{3,13... | collective-permute-start | bytes 24584 | tf_op jit(solution)/shard_map/ppermute | solution.py:243
  18.8 0.0 collective-permute-done.5.refs_5_
  18.8 3.3 %collective-permute-done.6.refs_6_ = bf16[32,128]{1,0:T(8,128)(2,1)S(1)} collective-permute-done((bf16[32,128]{1,0:T(8,128)(2,1)S(1)}, bf16[32,128]{1,0:T(8,128)(2,1)S(1)}, u32[]{:S(2)}, u32[]{:S(2)}) %collective-permute-start.6) | collective-permute-done | bytes 8224 | tf_op jit(solution)/shard_map/ppermute | solution.py:243
  22.1 0.0 collective-permute-done.refs_0_
  22.1 0.0 collective-permute-done.1.refs_1_
  22.1 0.0 collective-permute-done.2.refs_2_
  22.1 0.1 collective-permute-start.7
  22.2 0.4 %weights.1.w_ref = bf16[128,1024]{1,0:T(8,128)(2,1)S(1)} custom-call(bf16[1024,128]{1,0:T(8,128)(2,1)S(1)} %copy-done.1), custom_call_target="tpu_custom_call" | custom-call | tf_op jit(solution)/shard_map/weights/pallas_call | solution.py:248
  22.6 0.0 copy-start.6
  22.6 1.0 %collective-permute-done.7.refs_7_ = bf16[640,128]{1,0:T(8,128)(2,1)S(1)} collective-permute-done((bf16[640,128]{1,0:T(8,128)(2,1)S(1)}, bf16[640,128]{1,0:T(8,128)(2,1)S(1)}, u32[]{:S(2)}, u32[]{:S(2)}) %collective-permute-start.7) | collective-permute-done | bytes 163872 | tf_op jit(solution)/shard_map/ppermute | solution.py:268
  23.6 2.1 %pair.1 = bf16[2,8,64,128]{3,2,1,0:T(8,128)(2,1)} custom-call(f32[1,128]{1,0:T(1,128)S(1)} %bitcast.9, bf16[128,1024]{1,0:T(8,128)(2,1)S(1)} %weights.1.w_ref, bf16[128,128]{1,0:T(8,128)(2,1)S(1)} %get-tuple-element.14.right_ref, bf16[128,128]{1,0:T(8,128)(2,1)S(1)} %get-tuple-element.15.left_ref, bf16[160,128]{1,0:T(8,128)(2,1)S(1)} %collective-permute-done.refs_0_, ...), custom_call_target="tpu_custom_call" | custom-call | tf_op jit(solution)/shard_map/pair/pallas_call | solution.py:272
  (6 shorter events, 0.0 us)
Async XLA Ops:
  0.0 0.9 %copy-start.7 = (bf16[256,32]{0,1:T(8,128)(2,1)S(1)}, bf16[256,32]{0,1:T(8,128)(2,1)}, u32[]{:S(2)}) copy-start(bf16[256,32]{0,1:T(8,128)(2,1)} %param.14) | copy-start | bytes 49156
  1.0 0.7 %copy-start.3 = (f32[256]{0:T(256)S(1)}, f32[256]{0:T(256)}, u32[]{:S(2)}) copy-start(f32[256]{0:T(256)} %param.11) | copy-start | bytes 3076
  1.0 0.7 %copy-start.5 = (f32[32]{0:T(128)S(1)}, f32[32]{0:T(128)}, u32[]{:S(2)}) copy-start(f32[32]{0:T(128)} %param.15) | copy-start | bytes 388
  1.0 0.7 %copy-start.2 = (f32[256]{0:T(256)S(1)}, f32[256]{0:T(256)}, u32[]{:S(2)}) copy-start(f32[256]{0:T(256)} %param.10) | copy-start | bytes 3076
  1.0 0.7 %copy-start.4 = (f32[32]{0:T(128)S(1)}, f32[32]{0:T(128)}, u32[]{:S(2)}) copy-start(f32[32]{0:T(128)} %param.13) | copy-start | bytes 388
  1.7 1.0 %copy-start = (bf16[8,64,256]{2,1,0:T(8,128)(2,1)S(1)}, bf16[8,64,256]{2,1,0:T(8,128)(2,1)}, u32[]{:S(2)}) copy-start(bf16[8,64,256]{2,1,0:T(8,128)(2,1)} %x_ref.1) | copy-start | bytes 786436
  3.3 18.9 %copy-start.1 = (bf16[1024,128]{1,0:T(8,128)(2,1)S(1)}, bf16[1024,128]{1,0:T(8,128)(2,1)}, u32[]{:S(2)}) copy-start(bf16[1024,128]{1,0:T(8,128)(2,1)} %w_ref.1) | copy-start | bytes 786436
  3.3 18.8 %collective-permute-start = (bf16[160,128]{1,0:T(8,128)(2,1)S(1)}, bf16[160,128]{1,0:T(8,128)(2,1)S(1)}, u32[]{:S(2)}, u32[]{:S(2)}) collective-permute-start(bf16[160,128]{1,0:T(8,128)(2,1)S(1)} %get-tuple-element.16), channel_id=1, source_target_pairs={{0,4},{2,6},{4,0},{6,2},{8,12},{10,14},{12,8},{14,10},{1,5},{3,7},... | collective-permute-start | bytes 122888 | tf_op jit(solution)/shard_map/ppermute | solution.py:243
  6.4 15.7 %collective-permute-start.1 = (bf16[160,128]{1,0:T(8,128)(2,1)S(1)}, bf16[160,128]{1,0:T(8,128)(2,1)S(1)}, u32[]{:S(2)}, u32[]{:S(2)}) collective-permute-start(bf16[160,128]{1,0:T(8,128)(2,1)S(1)} %get-tuple-element.17), channel_id=1, source_target_pairs={{0,8},{2,10},{4,12},{6,14},{8,0},{10,2},{12,4},{14,6},{1,9},{3,11}... | collective-permute-start | bytes 122888 | tf_op jit(solution)/shard_map/ppermute | solution.py:243
  9.0 13.1 %collective-permute-start.2 = (bf16[160,128]{1,0:T(8,128)(2,1)S(1)}, bf16[160,128]{1,0:T(8,128)(2,1)S(1)}, u32[]{:S(2)}, u32[]{:S(2)}) collective-permute-start(bf16[160,128]{1,0:T(8,128)(2,1)S(1)} %get-tuple-element.18), channel_id=1, source_target_pairs={{0,12},{2,14},{4,8},{6,10},{8,4},{10,6},{12,0},{14,2},{1,13},{3,15... | collective-permute-start | bytes 122888 | tf_op jit(solution)/shard_map/ppermute | solution.py:243
  9.0 3.7 %collective-permute-start.3 = (bf16[32,128]{1,0:T(8,128)(2,1)S(1)}, bf16[32,128]{1,0:T(8,128)(2,1)S(1)}, u32[]{:S(2)}, u32[]{:S(2)}) collective-permute-start(bf16[32,128]{1,0:T(8,128)(2,1)S(1)} %get-tuple-element.19), channel_id=1, source_target_pairs={{0,2},{2,0},{4,6},{6,4},{8,10},{10,8},{12,14},{14,12},{1,3},{3,1},... | collective-permute-start | bytes 24584 | tf_op jit(solution)/shard_map/ppermute | solution.py:243
  10.7 5.1 %collective-permute-start.4 = (bf16[32,128]{1,0:T(8,128)(2,1)S(1)}, bf16[32,128]{1,0:T(8,128)(2,1)S(1)}, u32[]{:S(2)}, u32[]{:S(2)}) collective-permute-start(bf16[32,128]{1,0:T(8,128)(2,1)S(1)} %get-tuple-element.20), channel_id=1, source_target_pairs={{0,6},{2,4},{4,2},{6,0},{8,14},{10,12},{12,10},{14,8},{1,7},{3,5},... | collective-permute-start | bytes 24584 | tf_op jit(solution)/shard_map/ppermute | solution.py:243
  12.6 6.2 %collective-permute-start.5 = (bf16[32,128]{1,0:T(8,128)(2,1)S(1)}, bf16[32,128]{1,0:T(8,128)(2,1)S(1)}, u32[]{:S(2)}, u32[]{:S(2)}) collective-permute-start(bf16[32,128]{1,0:T(8,128)(2,1)S(1)} %get-tuple-element.21), channel_id=1, source_target_pairs={{0,10},{2,8},{4,14},{6,12},{8,2},{10,0},{12,6},{14,4},{1,11},{3,9}... | collective-permute-start | bytes 24584 | tf_op jit(solution)/shard_map/ppermute | solution.py:243
  15.7 6.3 %collective-permute-start.6 = (bf16[32,128]{1,0:T(8,128)(2,1)S(1)}, bf16[32,128]{1,0:T(8,128)(2,1)S(1)}, u32[]{:S(2)}, u32[]{:S(2)}) collective-permute-start(bf16[32,128]{1,0:T(8,128)(2,1)S(1)} %get-tuple-element.22), channel_id=1, source_target_pairs={{0,14},{2,12},{4,10},{6,8},{8,6},{10,4},{12,2},{14,0},{1,15},{3,13... | collective-permute-start | bytes 24584 | tf_op jit(solution)/shard_map/ppermute | solution.py:243
  22.1 1.5 %collective-permute-start.7 = (bf16[640,128]{1,0:T(8,128)(2,1)S(1)}, bf16[640,128]{1,0:T(8,128)(2,1)S(1)}, u32[]{:S(2)}, u32[]{:S(2)}) collective-permute-start(bf16[640,128]{1,0:T(8,128)(2,1)S(1)} %pack.1), channel_id=1, source_target_pairs={{0,1},{1,0},{2,3},{3,2},{4,5},{5,4},{6,7},{7,6},{8,9},{9,8},{10,11... | collective-permute-start | bytes 491528 | tf_op jit(solution)/shard_map/ppermute | solution.py:268
  22.6 1.0 %copy-start.6 = (f32[128]{0:T(128)S(1)}, f32[128]{0:T(128)}, u32[]{:S(2)}) copy-start(f32[128]{0:T(128)} %param.17) | copy-start | bytes 1540

commit v2 on v1

--- a/solution.py
+++ b/solution.py
@@ -10,6 +10,8 @@
 LANES = 128
 SUBLANES = 8
 VMEM = pl.BlockSpec(memory_space=pltpu.VMEM)
+ANY = pl.BlockSpec(memory_space=pl.ANY)
+ACROSS = (((1,), (1,)), ((), ()))
 
 
 def partner(index, step, size):
@@ -20,14 +22,22 @@
     return lax.broadcasted_iota(jnp.int32, shape, len(shape) - 1)
 
 
-def project_kernel(dims, x_ref, scale_ref, shift_ref, w1_ref, b1_ref, w2_ref, b2_ref, *refs):
+def project_kernel(dims, *refs):
     n_res, n_col, _, _ = dims
-    outs, (rows_scr, lane_scr, right_scr) = refs[:-3], refs[-3:]
+    n_in = 7
+    sources, outs, scratch = refs[:n_in], refs[n_in : -n_in - 4], refs[-n_in - 4 :]
+    landed, (rows_scr, lane_scr, right_scr, sems) = scratch[:n_in], scratch[n_in:]
+    copies = [pltpu.make_async_copy(a, b, sems.at[i]) for i, (a, b) in enumerate(zip(sources, landed))]
+    for copy in copies:
+        copy.start()
+    for copy in copies:
+        copy.wait()
+    x_ref, scale_ref, shift_ref, w1_ref, b1_ref, w2_ref, b2_ref = landed
     right_out, left_out = outs[0], outs[1]
     z_outs = outs[2 : 2 + n_res - 1]
     x_outs = outs[2 + n_res - 1 :]
     n_s, span, width = x_ref.shape
-    chans = w1_ref.shape[1]
+    chans = w1_ref.shape[0]
     fold = LANES // chans
     half = LANES // 2
     x = x_ref[...].reshape(n_s * span, width).astype(jnp.float32)
@@ -36,11 +46,9 @@
     variance = jnp.mean(centred * centred, axis=-1, keepdims=True)
     normed = (centred * lax.rsqrt(variance + 1e-05) * scale_ref[...] + shift_ref[...]).astype(jnp.bfloat16)
 
-    spread = lax.broadcasted_iota(jnp.int32, (chans, LANES), 1) % chans
-    spread = (spread == lax.broadcasted_iota(jnp.int32, (chans, LANES), 0)).astype(jnp.bfloat16)
-    w1 = jnp.dot(w1_ref[...], spread, preferred_element_type=jnp.float32).astype(jnp.bfloat16)
+    w1 = jnp.concatenate([w1_ref[...]] * fold, axis=0)
     b1 = jnp.concatenate([b1_ref[...]] * fold, axis=1)
-    rows_scr[...] = jnp.dot(normed, w1, preferred_element_type=jnp.float32) + b1
+    rows_scr[...] = lax.dot_general(normed, w1, ACROSS, preferred_element_type=jnp.float32) + b1
     n_rows = n_s * span // fold
     owner = lane_index((n_rows, LANES)) // chans
     merged = rows_scr[pl.ds(0, n_rows, stride=fold), :]
@@ -52,11 +60,8 @@
     left_out[...] = lane_scr[...].astype(jnp.bfloat16)
 
     eye = lax.broadcasted_iota(jnp.int32, (chans, chans), 0) == lane_index((chans, chans))
-    w2 = lax.dot_general(
-        eye.astype(jnp.bfloat16), w2_ref[...], (((1,), (1,)), ((), ())), preferred_element_type=jnp.float32
-    ).astype(jnp.bfloat16)
     b2 = jnp.sum(jnp.where(eye, b2_ref[...], 0.0), axis=1, keepdims=True)
-    right = lax.dot_general(w2, normed, (((1,), (1,)), ((), ())), preferred_element_type=jnp.float32) + b2
+    right = lax.dot_general(w2_ref[...], normed, ACROSS, preferred_element_type=jnp.float32) + b2
     pairs = chans // 2
     low = lane_index((pairs, LANES)) < half
     blocks = span // half
@@ -219,19 +224,22 @@
     dims = (n_res, n_col, n_seq)
     params = functools.partial(pltpu.CompilerParams, vmem_limit_bytes=32 * 1024 * 1024)
 
+    taken = (alignment, scale.reshape(1, -1), shift.reshape(1, -1), w1.T, b1.reshape(1, -1), w2.T, b2.reshape(1, -1))
     made = pl.pallas_call(
         functools.partial(project_kernel, dims + (chans,)),
         out_shape=[slab, slab] + [z_slab] * (n_res - 1) + [x_slab] * n_x,
-        in_specs=[VMEM] * 7,
+        in_specs=[ANY] * len(taken),
         out_specs=[VMEM] * (2 + n_res - 1 + n_x),
-        scratch_shapes=[
+        scratch_shapes=[pltpu.VMEM(a.shape, a.dtype) for a in taken]
+        + [
             pltpu.VMEM((n_s * span, LANES), jnp.float32),
             pltpu.VMEM((n_left, LANES), jnp.float32),
             pltpu.VMEM((n_right, LANES), jnp.float32),
+            pltpu.SemaphoreType.DMA((len(taken),)),
         ],
         compiler_params=params(),
         name="project",
-    )(alignment, scale.reshape(1, -1), shift.reshape(1, -1), w1, b1.reshape(1, -1), w2, b2.reshape(1, -1))
+    )(*taken)
     right, left = made[0], made[1]
 
     def to_chip(array, step_col, step_res):

time: 26 us -> 26.7 us (1.027)
  local copies, waits for them, and re-layouts: 2.62 us -> 3.11 us
    unnamed x18, local copies, waits for them, and re-layouts: 2.62 us -> 3.11 us
where the time goes in v2:
time: 26.7 us; the launch traced here: 26.3 us
  starting transfers between devices  14.3 us (54%)
  waiting for transfers between devices  5.55 us (21%)
  Pallas kernels  3.29 us (12%)
  local copies, waits for them, and re-layouts  3.11 us (12%)
    ppermute x7, starting transfers between devices, to_chip(): return lax.ppermute(array, ('res', 'col'), pairs)  14.2 us
    ppermute x7, waiting for transfers between devices, to_chip(): return lax.ppermute(array, ('res', 'col'), pairs)  4.6 us
    unnamed x18, local copies, waits for them, and re-layouts  3.11 us
    pallas_call x1, Pallas kernels, per_device(): pl.pallas_call(functools.partial(pair_kernel, dims + (chans,), float(n_s...  2.14 us
    ppermute x1, waiting for transfers between devices, per_device(): lax.ppermute(packed, 'seq', [(q, partner(q, step, n_seq)) for q in range(...  0.95 us
    pallas_call x1, Pallas kernels, per_device(): pl.pallas_call(functools.partial(project_kernel, dims + (chans,)), out_sh...  0.73 us
  transfers between devices with their start and end apart: 8, of which 3 were waited for; matrix products, arithmetic and copies ran while one was open for 0% of the time, Pallas kernels for 2%

profile of v2, /device:TPU:0, one launch (start us, length us, event | category | flops | bytes accessed | tf_op | source)
XLA Modules:
  0.0 26.3 jit_solution(10655919943468452540)
XLA Ops:
  0.0 0.0 copy-start.5
  0.0 0.0 copy-start.7
  0.0 0.7 %copy-done.5 = f32[256]{0:T(256)S(1)} copy-done((f32[256]{0:T(256)S(1)}, f32[256]{0:T(256)}, u32[]{:S(2)}) %copy-start.5) | copy-done | bytes 1048
  0.7 0.0 copy-done.7
  0.7 0.0 copy-done.4
  0.7 0.0 copy-done.6
  0.7 0.9 %copy-done = bf16[8,64,256]{2,1,0:T(8,128)(2,1)S(1)} copy-done((bf16[8,64,256]{2,1,0:T(8,128)(2,1)S(1)}, bf16[8,64,256]{2,1,0:T(8,128)(2,1)}, u32[]{:S(2)}) %copy-start) | copy-done | bytes 262168
  1.7 0.7 %copy-done.2 = bf16[256,32]{0,1:T(8,128)(2,1)S(1)} copy-done((bf16[256,32]{0,1:T(8,128)(2,1)S(1)}, bf16[256,32]{0,1:T(8,128)(2,1)}, u32[]{:S(2)}) %copy-start.2) | copy-done | bytes 16408
  2.4 0.7 %copy-done.3 = bf16[256,32]{0,1:T(8,128)(2,1)S(1)} copy-done((bf16[256,32]{0,1:T(8,128)(2,1)S(1)}, bf16[256,32]{0,1:T(8,128)(2,1)}, u32[]{:S(2)}) %copy-start.3) | copy-done | bytes 16408
  3.1 0.7 %project.1 = (bf16[128,128]{1,0:T(8,128)(2,1)S(1)}, bf16[128,128]{1,0:T(8,128)(2,1)S(1)}, bf16[160,128]{1,0:T(8,128)(2,1)S(1)}, bf16[160,128]{1,0:T(8,128)(2,1)S...) custom-call(bf16[8,64,256]{2,1,0:T(8,128)(2,1)S(1)} %copy-done, ...), custom_call_target="tpu_custom_call" | custom-call | tf_op jit(solution)/shard_map/project/pallas_call | solution.py:228
  3.8 0.0 copy-start.1
  3.9 3.1 %collective-permute-start = (bf16[160,128]{1,0:T(8,128)(2,1)S(1)}, bf16[160,128]{1,0:T(8,128)(2,1)S(1)}, u32[]{:S(2)}, u32[]{:S(2)}) collective-permute-start(bf16[160,128]{1,0:T(8,128)(2,1)S(1)} %get-tuple-element.16), channel_id=1, source_target_pairs={{0,4},{2,6},{4,0},{6,2},{8,12},{10,14},{12,8},{14,10},{1,5},{3,7},... | collective-permute-start | bytes 122888 | tf_op jit(solution)/shard_map/ppermute | solution.py:251
  6.9 2.6 %collective-permute-start.1 = (bf16[160,128]{1,0:T(8,128)(2,1)S(1)}, bf16[160,128]{1,0:T(8,128)(2,1)S(1)}, u32[]{:S(2)}, u32[]{:S(2)}) collective-permute-start(bf16[160,128]{1,0:T(8,128)(2,1)S(1)} %get-tuple-element.17), channel_id=1, source_target_pairs={{0,8},{2,10},{4,12},{6,14},{8,0},{10,2},{12,4},{14,6},{1,9},{3,11}... | collective-permute-start | bytes 122888 | tf_op jit(solution)/shard_map/ppermute | solution.py:251
  9.5 0.0 collective-permute-start.2
  9.5 1.7 %collective-permute-start.3 = (bf16[32,128]{1,0:T(8,128)(2,1)S(1)}, bf16[32,128]{1,0:T(8,128)(2,1)S(1)}, u32[]{:S(2)}, u32[]{:S(2)}) collective-permute-start(bf16[32,128]{1,0:T(8,128)(2,1)S(1)} %get-tuple-element.19), channel_id=1, source_target_pairs={{0,2},{2,0},{4,6},{6,4},{8,10},{10,8},{12,14},{14,12},{1,3},{3,1},... | collective-permute-start | bytes 24584 | tf_op jit(solution)/shard_map/ppermute | solution.py:251
  11.2 0.6 %collective-permute-start.4 = (bf16[32,128]{1,0:T(8,128)(2,1)S(1)}, bf16[32,128]{1,0:T(8,128)(2,1)S(1)}, u32[]{:S(2)}, u32[]{:S(2)}) collective-permute-start(bf16[32,128]{1,0:T(8,128)(2,1)S(1)} %get-tuple-element.20), channel_id=1, source_target_pairs={{0,6},{2,4},{4,2},{6,0},{8,14},{10,12},{12,10},{14,8},{1,7},{3,5},... | collective-permute-start | bytes 24584 | tf_op jit(solution)/shard_map/ppermute | solution.py:251
  11.9 1.3 %collective-permute-done.3.refs_3_ = bf16[32,128]{1,0:T(8,128)(2,1)S(1)} collective-permute-done((bf16[32,128]{1,0:T(8,128)(2,1)S(1)}, bf16[32,128]{1,0:T(8,128)(2,1)S(1)}, u32[]{:S(2)}, u32[]{:S(2)}) %collective-permute-start.3) | collective-permute-done | bytes 8224 | tf_op jit(solution)/shard_map/ppermute | solution.py:251
  13.2 3.1 %collective-permute-start.5 = (bf16[32,128]{1,0:T(8,128)(2,1)S(1)}, bf16[32,128]{1,0:T(8,128)(2,1)S(1)}, u32[]{:S(2)}, u32[]{:S(2)}) collective-permute-start(bf16[32,128]{1,0:T(8,128)(2,1)S(1)} %get-tuple-element.21), channel_id=1, source_target_pairs={{0,10},{2,8},{4,14},{6,12},{8,2},{10,0},{12,6},{14,4},{1,11},{3,9}... | collective-permute-start | bytes 24584 | tf_op jit(solution)/shard_map/ppermute | solution.py:251
  16.3 0.0 collective-permute-done.4.refs_4_
  16.3 3.1 %collective-permute-start.6 = (bf16[32,128]{1,0:T(8,128)(2,1)S(1)}, bf16[32,128]{1,0:T(8,128)(2,1)S(1)}, u32[]{:S(2)}, u32[]{:S(2)}) collective-permute-start(bf16[32,128]{1,0:T(8,128)(2,1)S(1)} %get-tuple-element.22), channel_id=1, source_target_pairs={{0,14},{2,12},{4,10},{6,8},{8,6},{10,4},{12,2},{14,0},{1,15},{3,13... | collective-permute-start | bytes 24584 | tf_op jit(solution)/shard_map/ppermute | solution.py:251
  19.4 0.0 collective-permute-done.5.refs_5_
  19.4 3.3 %collective-permute-done.6.refs_6_ = bf16[32,128]{1,0:T(8,128)(2,1)S(1)} collective-permute-done((bf16[32,128]{1,0:T(8,128)(2,1)S(1)}, bf16[32,128]{1,0:T(8,128)(2,1)S(1)}, u32[]{:S(2)}, u32[]{:S(2)}) %collective-permute-start.6) | collective-permute-done | bytes 8224 | tf_op jit(solution)/shard_map/ppermute | solution.py:251
  22.7 0.0 collective-permute-done.refs_0_
  22.7 0.0 collective-permute-done.1.refs_1_
  22.7 0.0 collective-permute-done.2.refs_2_
  22.7 0.1 collective-permute-start.7
  22.8 0.0 copy-done.1
  22.8 0.4 %weights.1.w_ref = bf16[128,1024]{1,0:T(8,128)(2,1)S(1)} custom-call(bf16[1024,128]{1,0:T(8,128)(2,1)S(1)} %copy-done.1), custom_call_target="tpu_custom_call" | custom-call | tf_op jit(solution)/shard_map/weights/pallas_call | solution.py:256
  23.2 0.0 copy-start.8
  23.2 1.0 %collective-permute-done.7.refs_7_ = bf16[640,128]{1,0:T(8,128)(2,1)S(1)} collective-permute-done((bf16[640,128]{1,0:T(8,128)(2,1)S(1)}, bf16[640,128]{1,0:T(8,128)(2,1)S(1)}, u32[]{:S(2)}, u32[]{:S(2)}) %collective-permute-start.7) | collective-permute-done | bytes 163872 | tf_op jit(solution)/shard_map/ppermute | solution.py:276
  24.2 0.0 copy-done.8
  24.2 2.1 %pair.1 = bf16[2,8,64,128]{3,2,1,0:T(8,128)(2,1)} custom-call(f32[1,128]{1,0:T(1,128)S(1)} %bitcast.13, bf16[128,1024]{1,0:T(8,128)(2,1)S(1)} %weights.1.w_ref, bf16[128,128]{1,0:T(8,128)(2,1)S(1)} %get-tuple-element.14.right_ref, bf16[128,128]{1,0:T(8,128)(2,1)S(1)} %get-tuple-element.15.left_ref, bf16[160,128]{1,0:T(8,128)(2,1)S(1)} %collective-permute-done.refs_0_, ...), custom_call_target="tpu_custom_call" | custom-call | tf_op jit(solution)/shard_map/pair/pallas_call | solution.py:280
  (6 shorter events, 0.0 us)
Async XLA Ops:
  0.0 0.7 %copy-start.5 = (f32[256]{0:T(256)S(1)}, f32[256]{0:T(256)}, u32[]{:S(2)}) copy-start(f32[256]{0:T(256)} %param.11) | copy-start | bytes 3076
  0.0 0.7 %copy-start.7 = (f32[32]{0:T(128)S(1)}, f32[32]{0:T(128)}, u32[]{:S(2)}) copy-start(f32[32]{0:T(128)} %param.15) | copy-start | bytes 388
  0.0 0.7 %copy-start.4 = (f32[256]{0:T(256)S(1)}, f32[256]{0:T(256)}, u32[]{:S(2)}) copy-start(f32[256]{0:T(256)} %param.10) | copy-start | bytes 3076
  0.0 0.7 %copy-start.6 = (f32[32]{0:T(128)S(1)}, f32[32]{0:T(128)}, u32[]{:S(2)}) copy-start(f32[32]{0:T(128)} %param.13) | copy-start | bytes 388
  0.7 1.0 %copy-start = (bf16[8,64,256]{2,1,0:T(8,128)(2,1)S(1)}, bf16[8,64,256]{2,1,0:T(8,128)(2,1)}, u32[]{:S(2)}) copy-start(bf16[8,64,256]{2,1,0:T(8,128)(2,1)} %refs_0_.1) | copy-start | bytes 786436
  1.7 0.7 %copy-start.2 = (bf16[256,32]{0,1:T(8,128)(2,1)S(1)}, bf16[256,32]{0,1:T(8,128)(2,1)}, u32[]{:S(2)}) copy-start(bf16[256,32]{0,1:T(8,128)(2,1)} %param.12) | copy-start | bytes 49156
  2.4 0.7 %copy-start.3 = (bf16[256,32]{0,1:T(8,128)(2,1)S(1)}, bf16[256,32]{0,1:T(8,128)(2,1)}, u32[]{:S(2)}) copy-start(bf16[256,32]{0,1:T(8,128)(2,1)} %param.14) | copy-start | bytes 49156
  3.8 18.9 %copy-start.1 = (bf16[1024,128]{1,0:T(8,128)(2,1)S(1)}, bf16[1024,128]{1,0:T(8,128)(2,1)}, u32[]{:S(2)}) copy-start(bf16[1024,128]{1,0:T(8,128)(2,1)} %w_ref.1) | copy-start | bytes 786436
  3.9 18.8 %collective-permute-start = (bf16[160,128]{1,0:T(8,128)(2,1)S(1)}, bf16[160,128]{1,0:T(8,128)(2,1)S(1)}, u32[]{:S(2)}, u32[]{:S(2)}) collective-permute-start(bf16[160,128]{1,0:T(8,128)(2,1)S(1)} %get-tuple-element.16), channel_id=1, source_target_pairs={{0,4},{2,6},{4,0},{6,2},{8,12},{10,14},{12,8},{14,10},{1,5},{3,7},... | collective-permute-start | bytes 122888 | tf_op jit(solution)/shard_map/ppermute | solution.py:251
  6.9 15.7 %collective-permute-start.1 = (bf16[160,128]{1,0:T(8,128)(2,1)S(1)}, bf16[160,128]{1,0:T(8,128)(2,1)S(1)}, u32[]{:S(2)}, u32[]{:S(2)}) collective-permute-start(bf16[160,128]{1,0:T(8,128)(2,1)S(1)} %get-tuple-element.17), channel_id=1, source_target_pairs={{0,8},{2,10},{4,12},{6,14},{8,0},{10,2},{12,4},{14,6},{1,9},{3,11}... | collective-permute-start | bytes 122888 | tf_op jit(solution)/shard_map/ppermute | solution.py:251
  9.5 13.1 %collective-permute-start.2 = (bf16[160,128]{1,0:T(8,128)(2,1)S(1)}, bf16[160,128]{1,0:T(8,128)(2,1)S(1)}, u32[]{:S(2)}, u32[]{:S(2)}) collective-permute-start(bf16[160,128]{1,0:T(8,128)(2,1)S(1)} %get-tuple-element.18), channel_id=1, source_target_pairs={{0,12},{2,14},{4,8},{6,10},{8,4},{10,6},{12,0},{14,2},{1,13},{3,15... | collective-permute-start | bytes 122888 | tf_op jit(solution)/shard_map/ppermute | solution.py:251
  9.5 3.7 %collective-permute-start.3 = (bf16[32,128]{1,0:T(8,128)(2,1)S(1)}, bf16[32,128]{1,0:T(8,128)(2,1)S(1)}, u32[]{:S(2)}, u32[]{:S(2)}) collective-permute-start(bf16[32,128]{1,0:T(8,128)(2,1)S(1)} %get-tuple-element.19), channel_id=1, source_target_pairs={{0,2},{2,0},{4,6},{6,4},{8,10},{10,8},{12,14},{14,12},{1,3},{3,1},... | collective-permute-start | bytes 24584 | tf_op jit(solution)/shard_map/ppermute | solution.py:251
  11.2 5.1 %collective-permute-start.4 = (bf16[32,128]{1,0:T(8,128)(2,1)S(1)}, bf16[32,128]{1,0:T(8,128)(2,1)S(1)}, u32[]{:S(2)}, u32[]{:S(2)}) collective-permute-start(bf16[32,128]{1,0:T(8,128)(2,1)S(1)} %get-tuple-element.20), channel_id=1, source_target_pairs={{0,6},{2,4},{4,2},{6,0},{8,14},{10,12},{12,10},{14,8},{1,7},{3,5},... | collective-permute-start | bytes 24584 | tf_op jit(solution)/shard_map/ppermute | solution.py:251
  13.2 6.2 %collective-permute-start.5 = (bf16[32,128]{1,0:T(8,128)(2,1)S(1)}, bf16[32,128]{1,0:T(8,128)(2,1)S(1)}, u32[]{:S(2)}, u32[]{:S(2)}) collective-permute-start(bf16[32,128]{1,0:T(8,128)(2,1)S(1)} %get-tuple-element.21), channel_id=1, source_target_pairs={{0,10},{2,8},{4,14},{6,12},{8,2},{10,0},{12,6},{14,4},{1,11},{3,9}... | collective-permute-start | bytes 24584 | tf_op jit(solution)/shard_map/ppermute | solution.py:251
  16.3 6.3 %collective-permute-start.6 = (bf16[32,128]{1,0:T(8,128)(2,1)S(1)}, bf16[32,128]{1,0:T(8,128)(2,1)S(1)}, u32[]{:S(2)}, u32[]{:S(2)}) collective-permute-start(bf16[32,128]{1,0:T(8,128)(2,1)S(1)} %get-tuple-element.22), channel_id=1, source_target_pairs={{0,14},{2,12},{4,10},{6,8},{8,6},{10,4},{12,2},{14,0},{1,15},{3,13... | collective-permute-start | bytes 24584 | tf_op jit(solution)/shard_map/ppermute | solution.py:251
  22.7 1.5 %collective-permute-start.7 = (bf16[640,128]{1,0:T(8,128)(2,1)S(1)}, bf16[640,128]{1,0:T(8,128)(2,1)S(1)}, u32[]{:S(2)}, u32[]{:S(2)}) collective-permute-start(bf16[640,128]{1,0:T(8,128)(2,1)S(1)} %pack.1), channel_id=1, source_target_pairs={{0,1},{1,0},{2,3},{3,2},{4,5},{5,4},{6,7},{7,6},{8,9},{9,8},{10,11... | collective-permute-start | bytes 491528 | tf_op jit(solution)/shard_map/ppermute | solution.py:276
  23.2 1.0 %copy-start.8 = (f32[128]{0:T(128)S(1)}, f32[128]{0:T(128)}, u32[]{:S(2)}) copy-start(f32[128]{0:T(128)} %param.17) | copy-start | bytes 1540

commit v3 on v2

--- a/solution.py
+++ b/solution.py
@@ -10,7 +10,7 @@
 LANES = 128
 SUBLANES = 8
 VMEM = pl.BlockSpec(memory_space=pltpu.VMEM)
-ANY = pl.BlockSpec(memory_space=pl.ANY)
+HBM = pl.BlockSpec(memory_space=pltpu.HBM)
 ACROSS = (((1,), (1,)), ((), ()))
 
 
@@ -228,7 +228,7 @@
     made = pl.pallas_call(
         functools.partial(project_kernel, dims + (chans,)),
         out_shape=[slab, slab] + [z_slab] * (n_res - 1) + [x_slab] * n_x,
-        in_specs=[ANY] * len(taken),
+        in_specs=[HBM] * len(taken),
         out_specs=[VMEM] * (2 + n_res - 1 + n_x),
         scratch_shapes=[pltpu.VMEM(a.shape, a.dtype) for a in taken]
         + [
@@ -239,7 +239,7 @@
         ],
         compiler_params=params(),
         name="project",
-    )(*taken)
+    )(*[pltpu.with_memory_space_constraint(a, pltpu.HBM) for a in taken])
     right, left = made[0], made[1]
 
     def to_chip(array, step_col, step_res):

time: 26.7 us -> 24.2 us (0.906); the launches traced: 26.3 us -> 24.1 us
  local copies, waits for them, and re-layouts: 3.11 us -> 0.01 us
  Pallas kernels: 3.29 us -> 4.18 us
    unnamed x18 -> x4, local copies, waits for them, and re-layouts: 3.11 us -> 0.01 us
    pallas_call x1, Pallas kernels: 0.73 us -> 1.62 us  [per_device(): pl.pallas_call(functools.partial(project_kernel, dims + (chans,)), out_sh...]
where the time goes in v3:
time: 24.2 us; the launch traced here: 24.1 us
  starting transfers between devices  14.3 us (59%)
  waiting for transfers between devices  5.55 us (23%)
  Pallas kernels  4.18 us (17%)
    ppermute x7, starting transfers between devices, to_chip(): return lax.ppermute(array, ('res', 'col'), pairs)  14.2 us
    ppermute x7, waiting for transfers between devices, to_chip(): return lax.ppermute(array, ('res', 'col'), pairs)  4.6 us
    pallas_call x1, Pallas kernels, per_device(): pl.pallas_call(functools.partial(pair_kernel, dims + (chans,), float(n_s...  2.14 us
    pallas_call x1, Pallas kernels, per_device(): pl.pallas_call(functools.partial(project_kernel, dims + (chans,)), out_sh...  1.62 us
    ppermute x1, waiting for transfers between devices, per_device(): lax.ppermute(packed, 'seq', [(q, partner(q, step, n_seq)) for q in range(...  0.95 us
  transfers between devices with their start and end apart: 8, of which 3 were waited for; matrix products, arithmetic and copies ran while one was open for 0% of the time, Pallas kernels for 2%

profile of v3, /device:TPU:0, one launch (start us, length us, event | category | flops | bytes accessed | tf_op | source)
XLA Modules:
  0.0 24.1 jit_solution(13152442666734555003)
XLA Ops:
  0.0 1.6 %project.1 = (bf16[128,128]{1,0:T(8,128)(2,1)S(1)}, bf16[128,128]{1,0:T(8,128)(2,1)S(1)}, bf16[160,128]{1,0:T(8,128)(2,1)S(1)}, bf16[160,128]{1,0:T(8,128)(2,1)S...) custom-call(bf16[8,64,256]{2,1,0:T(8,128)(2,1)} %refs_0_.1, ...), custom_call_target="tpu_custom_call" | custom-call | tf_op jit(solution)/shard_map/project/pallas_call | solution.py:228
  1.6 0.0 copy-start
  1.6 3.1 %collective-permute-start = (bf16[160,128]{1,0:T(8,128)(2,1)S(1)}, bf16[160,128]{1,0:T(8,128)(2,1)S(1)}, u32[]{:S(2)}, u32[]{:S(2)}) collective-permute-start(bf16[160,128]{1,0:T(8,128)(2,1)S(1)} %get-tuple-element.16), channel_id=1, source_target_pairs={{0,4},{2,6},{4,0},{6,2},{8,12},{10,14},{12,8},{14,10},{1,5},{3,7},... | collective-permute-start | bytes 122888 | tf_op jit(solution)/shard_map/ppermute | solution.py:251
  4.7 2.6 %collective-permute-start.1 = (bf16[160,128]{1,0:T(8,128)(2,1)S(1)}, bf16[160,128]{1,0:T(8,128)(2,1)S(1)}, u32[]{:S(2)}, u32[]{:S(2)}) collective-permute-start(bf16[160,128]{1,0:T(8,128)(2,1)S(1)} %get-tuple-element.17), channel_id=1, source_target_pairs={{0,8},{2,10},{4,12},{6,14},{8,0},{10,2},{12,4},{14,6},{1,9},{3,11}... | collective-permute-start | bytes 122888 | tf_op jit(solution)/shard_map/ppermute | solution.py:251
  7.3 0.0 collective-permute-start.2
  7.3 1.7 %collective-permute-start.3 = (bf16[32,128]{1,0:T(8,128)(2,1)S(1)}, bf16[32,128]{1,0:T(8,128)(2,1)S(1)}, u32[]{:S(2)}, u32[]{:S(2)}) collective-permute-start(bf16[32,128]{1,0:T(8,128)(2,1)S(1)} %get-tuple-element.19), channel_id=1, source_target_pairs={{0,2},{2,0},{4,6},{6,4},{8,10},{10,8},{12,14},{14,12},{1,3},{3,1},... | collective-permute-start | bytes 24584 | tf_op jit(solution)/shard_map/ppermute | solution.py:251
  9.0 0.6 %collective-permute-start.4 = (bf16[32,128]{1,0:T(8,128)(2,1)S(1)}, bf16[32,128]{1,0:T(8,128)(2,1)S(1)}, u32[]{:S(2)}, u32[]{:S(2)}) collective-permute-start(bf16[32,128]{1,0:T(8,128)(2,1)S(1)} %get-tuple-element.20), channel_id=1, source_target_pairs={{0,6},{2,4},{4,2},{6,0},{8,14},{10,12},{12,10},{14,8},{1,7},{3,5},... | collective-permute-start | bytes 24584 | tf_op jit(solution)/shard_map/ppermute | solution.py:251
  9.7 1.3 %collective-permute-done.3.refs_3_ = bf16[32,128]{1,0:T(8,128)(2,1)S(1)} collective-permute-done((bf16[32,128]{1,0:T(8,128)(2,1)S(1)}, bf16[32,128]{1,0:T(8,128)(2,1)S(1)}, u32[]{:S(2)}, u32[]{:S(2)}) %collective-permute-start.3) | collective-permute-done | bytes 8224 | tf_op jit(solution)/shard_map/ppermute | solution.py:251
  11.0 3.1 %collective-permute-start.5 = (bf16[32,128]{1,0:T(8,128)(2,1)S(1)}, bf16[32,128]{1,0:T(8,128)(2,1)S(1)}, u32[]{:S(2)}, u32[]{:S(2)}) collective-permute-start(bf16[32,128]{1,0:T(8,128)(2,1)S(1)} %get-tuple-element.21), channel_id=1, source_target_pairs={{0,10},{2,8},{4,14},{6,12},{8,2},{10,0},{12,6},{14,4},{1,11},{3,9}... | collective-permute-start | bytes 24584 | tf_op jit(solution)/shard_map/ppermute | solution.py:251
  14.1 0.0 collective-permute-done.4.refs_4_
  14.1 3.1 %collective-permute-start.6 = (bf16[32,128]{1,0:T(8,128)(2,1)S(1)}, bf16[32,128]{1,0:T(8,128)(2,1)S(1)}, u32[]{:S(2)}, u32[]{:S(2)}) collective-permute-start(bf16[32,128]{1,0:T(8,128)(2,1)S(1)} %get-tuple-element.22), channel_id=1, source_target_pairs={{0,14},{2,12},{4,10},{6,8},{8,6},{10,4},{12,2},{14,0},{1,15},{3,13... | collective-permute-start | bytes 24584 | tf_op jit(solution)/shard_map/ppermute | solution.py:251
  17.2 0.0 collective-permute-done.5.refs_5_
  17.2 3.3 %collective-permute-done.6.refs_6_ = bf16[32,128]{1,0:T(8,128)(2,1)S(1)} collective-permute-done((bf16[32,128]{1,0:T(8,128)(2,1)S(1)}, bf16[32,128]{1,0:T(8,128)(2,1)S(1)}, u32[]{:S(2)}, u32[]{:S(2)}) %collective-permute-start.6) | collective-permute-done | bytes 8224 | tf_op jit(solution)/shard_map/ppermute | solution.py:251
  20.5 0.0 collective-permute-done.refs_0_
  20.5 0.0 collective-permute-done.1.refs_1_
  20.5 0.0 collective-permute-done.2.refs_2_
  20.5 0.1 collective-permute-start.7
  20.6 0.0 copy-done
  20.6 0.4 %weights.1.w_ref = bf16[128,1024]{1,0:T(8,128)(2,1)S(1)} custom-call(bf16[1024,128]{1,0:T(8,128)(2,1)S(1)} %copy-done), custom_call_target="tpu_custom_call" | custom-call | tf_op jit(solution)/shard_map/weights/pallas_call | solution.py:256
  21.0 0.0 copy-start.1
  21.0 1.0 %collective-permute-done.7.refs_7_ = bf16[640,128]{1,0:T(8,128)(2,1)S(1)} collective-permute-done((bf16[640,128]{1,0:T(8,128)(2,1)S(1)}, bf16[640,128]{1,0:T(8,128)(2,1)S(1)}, u32[]{:S(2)}, u32[]{:S(2)}) %collective-permute-start.7) | collective-permute-done | bytes 163872 | tf_op jit(solution)/shard_map/ppermute | solution.py:276
  22.0 0.0 copy-done.1
  22.0 2.1 %pair.1 = bf16[2,8,64,128]{3,2,1,0:T(8,128)(2,1)} custom-call(f32[1,128]{1,0:T(1,128)S(1)} %bitcast.7, bf16[128,1024]{1,0:T(8,128)(2,1)S(1)} %weights.1.w_ref, bf16[128,128]{1,0:T(8,128)(2,1)S(1)} %get-tuple-element.14.right_ref, bf16[128,128]{1,0:T(8,128)(2,1)S(1)} %get-tuple-element.15.left_ref, bf16[160,128]{1,0:T(8,128)(2,1)S(1)} %collective-permute-done.refs_0_, ...), custom_call_target="tpu_custom_call" | custom-call | tf_op jit(solution)/shard_map/pair/pallas_call | solution.py:280
  (1 shorter events, 0.0 us)
Async XLA Ops:
  1.6 18.9 %copy-start = (bf16[1024,128]{1,0:T(8,128)(2,1)S(1)}, bf16[1024,128]{1,0:T(8,128)(2,1)}, u32[]{:S(2)}) copy-start(bf16[1024,128]{1,0:T(8,128)(2,1)} %w_ref.1) | copy-start | bytes 786436
  1.6 18.8 %collective-permute-start = (bf16[160,128]{1,0:T(8,128)(2,1)S(1)}, bf16[160,128]{1,0:T(8,128)(2,1)S(1)}, u32[]{:S(2)}, u32[]{:S(2)}) collective-permute-start(bf16[160,128]{1,0:T(8,128)(2,1)S(1)} %get-tuple-element.16), channel_id=1, source_target_pairs={{0,4},{2,6},{4,0},{6,2},{8,12},{10,14},{12,8},{14,10},{1,5},{3,7},... | collective-permute-start | bytes 122888 | tf_op jit(solution)/shard_map/ppermute | solution.py:251
  4.7 15.7 %collective-permute-start.1 = (bf16[160,128]{1,0:T(8,128)(2,1)S(1)}, bf16[160,128]{1,0:T(8,128)(2,1)S(1)}, u32[]{:S(2)}, u32[]{:S(2)}) collective-permute-start(bf16[160,128]{1,0:T(8,128)(2,1)S(1)} %get-tuple-element.17), channel_id=1, source_target_pairs={{0,8},{2,10},{4,12},{6,14},{8,0},{10,2},{12,4},{14,6},{1,9},{3,11}... | collective-permute-start | bytes 122888 | tf_op jit(solution)/shard_map/ppermute | solution.py:251
  7.3 13.1 %collective-permute-start.2 = (bf16[160,128]{1,0:T(8,128)(2,1)S(1)}, bf16[160,128]{1,0:T(8,128)(2,1)S(1)}, u32[]{:S(2)}, u32[]{:S(2)}) collective-permute-start(bf16[160,128]{1,0:T(8,128)(2,1)S(1)} %get-tuple-element.18), channel_id=1, source_target_pairs={{0,12},{2,14},{4,8},{6,10},{8,4},{10,6},{12,0},{14,2},{1,13},{3,15... | collective-permute-start | bytes 122888 | tf_op jit(solution)/shard_map/ppermute | solution.py:251
  7.3 3.7 %collective-permute-start.3 = (bf16[32,128]{1,0:T(8,128)(2,1)S(1)}, bf16[32,128]{1,0:T(8,128)(2,1)S(1)}, u32[]{:S(2)}, u32[]{:S(2)}) collective-permute-start(bf16[32,128]{1,0:T(8,128)(2,1)S(1)} %get-tuple-element.19), channel_id=1, source_target_pairs={{0,2},{2,0},{4,6},{6,4},{8,10},{10,8},{12,14},{14,12},{1,3},{3,1},... | collective-permute-start | bytes 24584 | tf_op jit(solution)/shard_map/ppermute | solution.py:251
  9.0 5.1 %collective-permute-start.4 = (bf16[32,128]{1,0:T(8,128)(2,1)S(1)}, bf16[32,128]{1,0:T(8,128)(2,1)S(1)}, u32[]{:S(2)}, u32[]{:S(2)}) collective-permute-start(bf16[32,128]{1,0:T(8,128)(2,1)S(1)} %get-tuple-element.20), channel_id=1, source_target_pairs={{0,6},{2,4},{4,2},{6,0},{8,14},{10,12},{12,10},{14,8},{1,7},{3,5},... | collective-permute-start | bytes 24584 | tf_op jit(solution)/shard_map/ppermute | solution.py:251
  11.0 6.2 %collective-permute-start.5 = (bf16[32,128]{1,0:T(8,128)(2,1)S(1)}, bf16[32,128]{1,0:T(8,128)(2,1)S(1)}, u32[]{:S(2)}, u32[]{:S(2)}) collective-permute-start(bf16[32,128]{1,0:T(8,128)(2,1)S(1)} %get-tuple-element.21), channel_id=1, source_target_pairs={{0,10},{2,8},{4,14},{6,12},{8,2},{10,0},{12,6},{14,4},{1,11},{3,9}... | collective-permute-start | bytes 24584 | tf_op jit(solution)/shard_map/ppermute | solution.py:251
  14.1 6.3 %collective-permute-start.6 = (bf16[32,128]{1,0:T(8,128)(2,1)S(1)}, bf16[32,128]{1,0:T(8,128)(2,1)S(1)}, u32[]{:S(2)}, u32[]{:S(2)}) collective-permute-start(bf16[32,128]{1,0:T(8,128)(2,1)S(1)} %get-tuple-element.22), channel_id=1, source_target_pairs={{0,14},{2,12},{4,10},{6,8},{8,6},{10,4},{12,2},{14,0},{1,15},{3,13... | collective-permute-start | bytes 24584 | tf_op jit(solution)/shard_map/ppermute | solution.py:251
  20.5 1.5 %collective-permute-start.7 = (bf16[640,128]{1,0:T(8,128)(2,1)S(1)}, bf16[640,128]{1,0:T(8,128)(2,1)S(1)}, u32[]{:S(2)}, u32[]{:S(2)}) collective-permute-start(bf16[640,128]{1,0:T(8,128)(2,1)S(1)} %pack.1), channel_id=1, source_target_pairs={{0,1},{1,0},{2,3},{3,2},{4,5},{5,4},{6,7},{7,6},{8,9},{9,8},{10,11... | collective-permute-start | bytes 491528 | tf_op jit(solution)/shard_map/ppermute | solution.py:276
  21.0 1.0 %copy-start.1 = (f32[128]{0:T(128)S(1)}, f32[128]{0:T(128)}, u32[]{:S(2)}) copy-start(f32[128]{0:T(128)} %param.17) | copy-start | bytes 1540

commit v4 on v3

--- a/solution.py
+++ b/solution.py
@@ -22,8 +22,7 @@
     return lax.broadcasted_iota(jnp.int32, shape, len(shape) - 1)
 
 
-def project_kernel(dims, *refs):
-    n_res, n_col, _, _ = dims
+def project_kernel(n_res, solo, *refs):
     n_in = 7
     sources, outs, scratch = refs[:n_in], refs[n_in : -n_in - 4], refs[-n_in - 4 :]
     landed, (rows_scr, lane_scr, right_scr, sems) = scratch[:n_in], scratch[n_in:]
@@ -33,9 +32,7 @@
     for copy in copies:
         copy.wait()
     x_ref, scale_ref, shift_ref, w1_ref, b1_ref, w2_ref, b2_ref = landed
-    right_out, left_out = outs[0], outs[1]
-    z_outs = outs[2 : 2 + n_res - 1]
-    x_outs = outs[2 + n_res - 1 :]
+    slab_out, solo_out = outs
     n_s, span, width = x_ref.shape
     chans = w1_ref.shape[0]
     fold = LANES // chans
@@ -57,7 +54,6 @@
     groups = span // fold
     for s in range(n_s):
         lane_scr[pl.ds(s, groups, stride=n_s), :] = merged[s * groups : (s + 1) * groups]
-    left_out[...] = lane_scr[...].astype(jnp.bfloat16)
 
     eye = lax.broadcasted_iota(jnp.int32, (chans, chans), 0) == lane_index((chans, chans))
     b2 = jnp.sum(jnp.where(eye, b2_ref[...], 0.0), axis=1, keepdims=True)
@@ -75,38 +71,42 @@
                 low, first[:pairs], second[pairs:]
             )
     right_slab = right_scr[...].astype(jnp.bfloat16)
-    right_out[...] = right_slab
-
-    here = lax.axis_index("res")
-    n_right = right_slab.shape[0]
-    part = left_out.shape[0] // n_res
-    for k, out in enumerate(z_outs):
-        out[:n_right] = right_slab
-        out[n_right:] = left_out[pl.ds(pl.multiple_of(partner(here, k + 1, n_res) * part, part), part), :]
-    for k, out in enumerate(x_outs):
-        out[...] = left_out[pl.ds(pl.multiple_of(partner(here, k % n_res, n_res) * part, part), part), :]
-
-
-def pack_kernel(dims, right_ref, left_ref, *refs):
-    n_res, n_col, n_seq, step = dims
+    n_right, n_left = right_scr.shape[0], lane_scr.shape[0]
+    part = n_left // n_res
+    slab_out[:n_right] = right_slab
+    slab_out[n_right:] = lane_scr[...].astype(jnp.bfloat16)
+    to = partner(lax.axis_index("res"), solo, n_res)
+    solo_out[:n_right] = right_slab
+    solo_out[n_right:] = lane_scr[pl.ds(pl.multiple_of(to * part, part), part), :].astype(jnp.bfloat16)
+
+
+def chip_kernel(n_res, steps, own_ref, other_ref, *outs):
+    n_right = own_ref.shape[0] // 2
+    part = n_right // n_res
+    me, here = lax.axis_index("seq"), lax.axis_index("res")
+    for (first, second), out in zip(steps, outs):
+        to = partner(here, jnp.where(me == 0, first, second), n_res)
+        start = pl.multiple_of(n_right + to * part, part)
+        at = out.shape[0] - 2 * part
+        if at:
+            out[:n_right] = own_ref[:n_right]
+            out[n_right:at] = other_ref[:n_right]
+        out[at : at + part] = own_ref[pl.ds(start, part), :]
+        out[at + part :] = other_ref[pl.ds(start, part), :]
+
+
+def core_kernel(parts, part, own, *refs):
     ins, out = refs[:-1], refs[-1]
-    z_ins, x_ins = ins[: n_res - 1], ins[n_res - 1 :]
-    n_right = right_ref.shape[0]
-    part = left_ref.shape[0] // n_res
-    own = part // n_seq
-    other = partner(lax.axis_index("seq"), step, n_seq)
-    out[:n_right] = right_ref[...]
-    for k, ref in enumerate(z_ins):
-        out[(k + 1) * n_right : (k + 2) * n_right] = ref[:n_right]
-    base = n_res * n_right
-    start = pl.multiple_of(lax.axis_index("res") * part + other * own, own)
-    out[base : base + own] = left_ref[pl.ds(start, own), :]
-    for k, ref in enumerate(z_ins):
-        at = base + (k + 1) * own
-        out[at : at + own] = ref[pl.ds(pl.multiple_of(n_right + other * own, own), own), :]
-    for k, ref in enumerate(x_ins):
-        at = base + (n_res + k) * own
-        out[at : at + own] = ref[pl.ds(pl.multiple_of(other * own, own), own), :]
+    mine = pl.multiple_of((1 - lax.axis_index("seq")) * own, own)
+    at = 0
+    for ref, n_parts in zip(ins, parts):
+        body = ref.shape[0] - n_parts * part
+        if body:
+            out[at : at + body] = ref[:body]
+            at += body
+        for k in range(n_parts):
+            out[at : at + own] = ref[pl.ds(pl.multiple_of(body + k * part + mine, own), own), :]
+            at += own
 
 
 def weight_kernel(w_ref, out_ref, scr):
@@ -123,16 +123,10 @@
         out_ref[:, tile * LANES : (tile + 1) * LANES] = piece.T.astype(jnp.bfloat16)
 
 
-def pair_kernel(dims, total, offset_ref, w_ref, right_ref, left_ref, *refs):
-    n_res, n_col, n_seq, chans = dims
+def pair_kernel(plan, total, offset_ref, w_ref, *refs):
     out_ref, left_scr, outer_scr = refs[-3], refs[-2], refs[-1]
-    ins = refs[:-3]
-    z_ins = ins[: n_res - 1]
-    x_ins = ins[n_res - 1 : n_res - 1 + (n_col - 1) * n_res]
-    s_ins = ins[n_res - 1 + (n_col - 1) * n_res :]
-    n_right = right_ref.shape[0]
-    part = left_ref.shape[0] // n_res
-    own = part // n_seq
+    n_col, chans, part, own = plan["n_col"], plan["chans"], plan["part"], plan["own"]
+    n_right = part * plan["n_res"]
     me = lax.axis_index("seq")
     half = LANES // 2
     fold = LANES // chans
@@ -141,22 +135,42 @@
     turns = rows_dev // fold
     n_s = own // turns
 
-    start = pl.multiple_of(lax.axis_index("res") * part + me * own, own)
+    own_ref, other_ref, solo_ref = refs[:3]
+    n_pairs = plan["n_pairs"]
+    b_refs = refs[3 : 3 + n_pairs]
+    x_refs = refs[3 + n_pairs : 3 + n_pairs + (n_col - 1) * (n_pairs + 1)]
+    z_other, x_other = refs[3 + n_pairs + (n_col - 1) * (n_pairs + 1) : -3]
     mine = pl.multiple_of(me * own, own)
-    rights = [(right_ref, 0)] + [(ref, 0) for ref in z_ins]
-    lefts = [[(left_ref, start)] + [(ref, pl.multiple_of(n_right + mine, own)) for ref in z_ins]]
+
+    def rows_of(ref, at):
+        return ref[pl.ds(at, own), :].astype(jnp.float32)
+
+    start = pl.multiple_of(n_right + lax.axis_index("res") * part + mine, own)
+    rights = [(own_ref, 0), (other_ref, 0), (solo_ref, 0), (z_other, 0)]
+    lefts = [[rows_of(own_ref, start), rows_of(other_ref, start)]]
+    lefts[0] += [rows_of(solo_ref, pl.multiple_of(n_right + mine, own)), rows_of(z_other, n_right)]
+    for k, ref in enumerate(b_refs):
+        at = n_right + own + k * 2 * (n_right + own)
+        rights += [(ref, 0), (ref, n_right), (z_other, at + n_right), (z_other, at)]
+        lefts[0] += [rows_of(ref, pl.multiple_of(2 * n_right + h * part + mine, own)) for h in range(2)]
+        lefts[0] += [rows_of(z_other, at + 2 * n_right + (1 - h) * own) for h in range(2)]
     for u in range(n_col - 1):
-        lefts.append([(x_ins[u * n_res + k], mine) for k in range(n_res)])
-    for ref in s_ins:
-        rights += [(ref, k * n_right) for k in range(n_res)]
-        base = n_res * n_right
-        for u in range(n_col):
-            lefts[u] += [(ref, base + (u * n_res + k) * own) for k in range(n_res)]
+        chunks = []
+        for k in range(n_pairs + 1):
+            place = u * (n_pairs + 1) + k
+            heard = [rows_of(x_refs[place], pl.multiple_of(h * part + mine, own)) for h in range(2)]
+            told = [rows_of(x_other, (2 * place + 1 - h) * own) for h in range(2)]
+            if k < n_pairs:
+                chunks += heard + told
+            else:
+                near = [jnp.where(me == 0, a, b) for a, b in zip(heard, told)]
+                far = [jnp.where(me == 0, b, a) for a, b in zip(heard, told)]
+                chunks = near + far + chunks
+        lefts.append(chunks)
 
     for u in range(n_col):
-        slabs = [ref[pl.ds(at, own), :].astype(jnp.float32) for ref, at in lefts[u]]
         for turn in range(turns):
-            column = jnp.concatenate([slab[turn * n_s : (turn + 1) * n_s] for slab in slabs], axis=0)
+            column = jnp.concatenate([slab[turn * n_s : (turn + 1) * n_s] for slab in lefts[u]], axis=0)
             depth = column.shape[0]
             left_scr[u * LANES : (u + 1) * LANES, turn * depth : (turn + 1) * depth] = column.T.astype(jnp.bfloat16)
 
@@ -217,19 +231,20 @@
     part = n_left // n_res
     own = part // n_seq
     rows_dev = span // (n_res * n_seq)
-    slab = jax.ShapeDtypeStruct((n_right, LANES), bf16)
-    z_slab = jax.ShapeDtypeStruct((n_right + part, LANES), bf16)
-    x_slab = jax.ShapeDtypeStruct((part, LANES), bf16)
-    n_x = (n_col - 1) * n_res
-    dims = (n_res, n_col, n_seq)
-    params = functools.partial(pltpu.CompilerParams, vmem_limit_bytes=32 * 1024 * 1024)
+    params = pltpu.CompilerParams(vmem_limit_bytes=32 * 1024 * 1024)
+
+    def rows(n):
+        return jax.ShapeDtypeStruct((n, LANES), bf16)
+
+    solo = n_res - 1
+    pairs = [(k, k + 1) for k in range(1, solo, 2)]
 
     taken = (alignment, scale.reshape(1, -1), shift.reshape(1, -1), w1.T, b1.reshape(1, -1), w2.T, b2.reshape(1, -1))
-    made = pl.pallas_call(
-        functools.partial(project_kernel, dims + (chans,)),
-        out_shape=[slab, slab] + [z_slab] * (n_res - 1) + [x_slab] * n_x,
+    slab, solo_out = pl.pallas_call(
+        functools.partial(project_kernel, n_res, solo),
+        out_shape=[rows(n_right + n_left), rows(n_right + part)],
         in_specs=[HBM] * len(taken),
-        out_specs=[VMEM] * (2 + n_res - 1 + n_x),
+        out_specs=[VMEM] * 2,
         scratch_shapes=[pltpu.VMEM(a.shape, a.dtype) for a in taken]
         + [
             pltpu.VMEM((n_s * span, LANES), jnp.float32),
@@ -237,21 +252,35 @@
             pltpu.VMEM((n_right, LANES), jnp.float32),
             pltpu.SemaphoreType.DMA((len(taken),)),
         ],
-        compiler_params=params(),
+        compiler_params=params,
         name="project",
     )(*[pltpu.with_memory_space_constraint(a, pltpu.HBM) for a in taken])
-    right, left = made[0], made[1]
-
-    def to_chip(array, step_col, step_res):
-        pairs = []
+
+    def to_core(array):
+        return lax.ppermute(array, "seq", [(q, 1 - q) for q in range(n_seq)])
+
+    def to_chip(array, step_col, steps):
+        route = []
         for r in range(n_res):
             for c in range(n_col):
-                to = partner(r, step_res, n_res) * n_col + partner(c, step_col, n_col)
-                pairs.append((r * n_col + c, to))
-        return lax.ppermute(array, ("res", "col"), pairs)
-
-    z_in = [to_chip(made[2 + k], 0, k + 1) for k in range(n_res - 1)]
-    x_in = [to_chip(made[1 + n_res + k], 1 + k // n_res, k % n_res) for k in range(n_x)]
+                for q in range(n_seq):
+                    to = partner(r, steps[q], n_res) * n_col + partner(c, step_col, n_col)
+                    route.append(((r * n_col + c) * n_seq + q, to * n_seq + q))
+        return lax.ppermute(array, ("res", "col", "seq"), route)
+
+    slab_in = to_core(slab)
+    solo_in = to_chip(solo_out, 0, (solo, solo))
+    sends = [(0, steps) for steps in pairs]
+    sends += [(u, steps) for u in range(1, n_col) for steps in pairs + [(0, solo)]]
+    messages = pl.pallas_call(
+        functools.partial(chip_kernel, n_res, [steps for _, steps in sends]),
+        out_shape=[rows(2 * part + (0 if u else 2 * n_right)) for u, _ in sends],
+        in_specs=[VMEM] * 2,
+        out_specs=[VMEM] * len(sends),
+        compiler_params=params,
+        name="chip",
+    )(slab, slab_in)
+    heard = [to_chip(message, u, steps) for message, (u, steps) in zip(messages, sends)]
 
     weights = pl.pallas_call(
         weight_kernel,
@@ -259,36 +288,41 @@
         in_specs=[VMEM],
         out_specs=VMEM,
         scratch_shapes=[pltpu.VMEM((chans * chans, pair_width), jnp.float32)],
-        compiler_params=params(),
+        compiler_params=params,
         name="weights",
     )(w_final)
 
-    s_in = []
-    for step in range(1, n_seq):
+    def share(arrays, parts, n_rows):
         packed = pl.pallas_call(
-            functools.partial(pack_kernel, dims + (step,)),
-            out_shape=jax.ShapeDtypeStruct((n_res * n_right + n_res * n_col * own, LANES), bf16),
-            in_specs=[VMEM] * (2 + len(z_in) + len(x_in)),
+            functools.partial(core_kernel, parts, part, own),
+            out_shape=rows(n_rows),
+            in_specs=[VMEM] * len(arrays),
             out_specs=VMEM,
-            compiler_params=params(),
-            name="pack",
-        )(right, left, *z_in, *x_in)
-        s_in.append(lax.ppermute(packed, "seq", [(q, partner(q, step, n_seq)) for q in range(n_seq)]))
+            compiler_params=params,
+            name="core",
+        )(*arrays)
+        return to_core(packed)
+
+    z_in, x_in = heard[: len(pairs)], heard[len(pairs) :]
+    z_other = share([solo_in] + z_in, [1] + [2] * len(z_in), (2 * len(pairs) + 1) * (n_right + own))
+    x_other = share(x_in, [2] * len(x_in), 2 * own * len(x_in))
 
     turns = rows_dev * chans // LANES
     depth = turns * n_s * n_res * n_seq
+    plan = dict(n_res=n_res, n_col=n_col, chans=chans, part=part, own=own, n_pairs=len(pairs))
+    operands = (offset.reshape(1, -1), weights, slab, slab_in, solo_in, *heard, z_other, x_other)
     return pl.pallas_call(
-        functools.partial(pair_kernel, dims + (chans,), float(n_s * n_res * n_seq)),
+        functools.partial(pair_kernel, plan, float(n_s * n_res * n_seq)),
         out_shape=jax.ShapeDtypeStruct((n_col, rows_dev, span, pair_width), bf16),
-        in_specs=[VMEM] * (4 + len(z_in) + len(x_in) + len(s_in)),
+        in_specs=[VMEM] * len(operands),
         out_specs=VMEM,
         scratch_shapes=[
             pltpu.VMEM((n_col * LANES, depth), bf16),
             pltpu.VMEM((chans * chans, n_col * (LANES // chans) * LANES), bf16),
         ],
-        compiler_params=params(),
+        compiler_params=params,
         name="pair",
-    )(offset.reshape(1, -1), weights, right, left, *z_in, *x_in, *s_in)
+    )(*operands)
 
 
 def solution(mesh):

time: 24.2 us -> 24.1 us (level)
  starting transfers between devices: 14.3 us -> 11.2 us
  waiting for transfers between devices: 5.55 us -> 8.23 us
    ppermute x8 -> x7, starting transfers between devices: 14.3 us -> 11.2 us  [the longest x4 7.21 us: to_chip(): return lax.ppermute(array, ('res', 'col', 'seq'), route)]
    ppermute x8 -> x7, waiting for transfers between devices: 5.55 us -> 8.23 us  [the longest x4 6.9 us: to_chip(): return lax.ppermute(array, ('res', 'col', 'seq'), route)]
    pallas_call x3 -> x5, Pallas kernels: 3.78 us -> 3.78 us  [the longest x1 2.14 us: per_device(): pl.pallas_call(functools.partial(pair_kernel, plan, float(n_s * n_res * n...]
  transfers between devices with their start and end apart: 8 -> 7, of which waited for: 3 -> 5; matrix products, arithmetic and copies ran while one was open for 0% -> 0% of each run, Pallas kernels for 2% -> 2%
where the time goes in v4:
time: 24.1 us; the launch traced here: 23.9 us
  starting transfers between devices  11.2 us (46%)
  waiting for transfers between devices  8.23 us (34%)
  Pallas kernels  4.18 us (17%)
    ppermute x4, starting transfers between devices, to_chip(): return lax.ppermute(array, ('res', 'col', 'seq'), route)  7.21 us
    ppermute x4, waiting for transfers between devices, to_chip(): return lax.ppermute(array, ('res', 'col', 'seq'), route)  6.9 us
    ppermute x3, starting transfers between devices, to_core(): return lax.ppermute(array, 'seq', [(q, 1 - q) for q in range(n_seq)])  4.02 us
    pallas_call x1, Pallas kernels, per_device(): pl.pallas_call(functools.partial(pair_kernel, plan, float(n_s * n_res * n...  2.14 us
    pallas_call x1, Pallas kernels, per_device(): pl.pallas_call(functools.partial(project_kernel, n_res, solo), out_shape=...  1.62 us
    ppermute x3, waiting for transfers between devices, to_core(): return lax.ppermute(array, 'seq', [(q, 1 - q) for q in range(n_seq)])  1.33 us
  transfers between devices with their start and end apart: 7, of which 5 were waited for; matrix products, arithmetic and copies ran while one was open for 0% of the time, Pallas kernels for 2%

profile of v4, /device:TPU:0, one launch (start us, length us, event | category | flops | bytes accessed | tf_op | source)
XLA Modules:
  0.0 23.9 jit_solution(13487049618034224517)
XLA Ops:
  0.0 1.6 %project.1 = (bf16[256,128]{1,0:T(8,128)(2,1)S(1)}, bf16[160,128]{1,0:T(8,128)(2,1)S(1)}) custom-call(bf16[8,64,256]{2,1,0:T(8,128)(2,1)} %refs_0_.1, f32[1,256]{1,0:T(1,128)} %bitcast.10, f32[1,256]{1,0:T(1,128)} %bitcast.11, bf16[32,256]{1,0:T(8,128)(2,1)} %bitcast.8, f32[1,32]{1,0:T(1,128)} %bitcast.12, bf16[32,256]{1,0:T(8,128)(2,1)} %bitcast.9, ...), custom_call_target="tpu_custom_call" | custom-call | tf_op jit(solution)/shard_map/project/pallas_call | solution.py:243
  1.6 0.0 copy-start
  1.6 0.5 %collective-permute-start = (bf16[256,128]{1,0:T(8,128)(2,1)S(1)}, bf16[256,128]{1,0:T(8,128)(2,1)S(1)}, u32[]{:S(2)}, u32[]{:S(2)}) collective-permute-start(bf16[256,128]{1,0:T(8,128)(2,1)S(1)} %get-tuple-element.10.own_ref.refs_0_), channel_id=1, source_target_pairs={{0,1},{1,0},{2,3},{3,2},{4,5},{5,4},{6,7},{7,6},{8,9},{9,8},{10,11... | collective-permute-start | bytes 196616 | tf_op jit(solution)/shard_map/ppermute | solution.py:260
  2.2 0.9 %collective-permute-done.other_ref.refs_1_ = bf16[256,128]{1,0:T(8,128)(2,1)S(1)} collective-permute-done((bf16[256,128]{1,0:T(8,128)(2,1)S(1)}, bf16[256,128]{1,0:T(8,128)(2,1)S(1)}, u32[]{:S(2)}, u32[]{:S(2)}) %collective-permute-start) | collective-permute-done | bytes 65568 | tf_op jit(solution)/shard_map/ppermute | solution.py:260
  3.1 3.0 %collective-permute-start.2 = (bf16[320,128]{1,0:T(8,128)(2,1)S(1)}, bf16[320,128]{1,0:T(8,128)(2,1)S(1)}, u32[]{:S(2)}, u32[]{:S(2)}) collective-permute-start(bf16[320,128]{1,0:T(8,128)(2,1)S(1)} %get-tuple-element.12), channel_id=1, source_target_pairs={{0,4},{1,9},{2,6},{3,11},{4,0},{5,13},{6,2},{7,15},{8,12},{9,1},{1... | collective-permute-start | bytes 245768 | tf_op jit(solution)/shard_map/ppermute | solution.py:269
  6.1 2.5 %collective-permute-start.1 = (bf16[160,128]{1,0:T(8,128)(2,1)S(1)}, bf16[160,128]{1,0:T(8,128)(2,1)S(1)}, u32[]{:S(2)}, u32[]{:S(2)}) collective-permute-start(bf16[160,128]{1,0:T(8,128)(2,1)S(1)} %get-tuple-element.11), channel_id=1, source_target_pairs={{0,12},{1,13},{2,14},{3,15},{4,8},{5,9},{6,10},{7,11},{8,4},{9,5},... | collective-permute-start | bytes 122888 | tf_op jit(solution)/shard_map/ppermute | solution.py:269
  8.5 3.7 %collective-permute-done.1.refs_0_.refs_2_ = bf16[160,128]{1,0:T(8,128)(2,1)S(1)} collective-permute-done((bf16[160,128]{1,0:T(8,128)(2,1)S(1)}, bf16[160,128]{1,0:T(8,128)(2,1)S(1)}, u32[]{:S(2)}, u32[]{:S(2)}) %collective-permute-start.1) | collective-permute-done | bytes 40992 | tf_op jit(solution)/shard_map/ppermute | solution.py:269
  12.2 0.0 collective-permute-done.2.refs_1_.refs_3_
  12.2 0.1 collective-permute-start.5
  12.3 1.2 %collective-permute-start.3 = (bf16[64,128]{1,0:T(8,128)(2,1)S(1)}, bf16[64,128]{1,0:T(8,128)(2,1)S(1)}, u32[]{:S(2)}, u32[]{:S(2)}) collective-permute-start(bf16[64,128]{1,0:T(8,128)(2,1)S(1)} %get-tuple-element.13), channel_id=1, source_target_pairs={{0,6},{1,11},{2,4},{3,9},{4,2},{5,15},{6,0},{7,13},{8,14},{9,3},{1... | collective-permute-start | bytes 49160 | tf_op jit(solution)/shard_map/ppermute | solution.py:269
  13.6 0.5 %collective-permute-start.4 = (bf16[64,128]{1,0:T(8,128)(2,1)S(1)}, bf16[64,128]{1,0:T(8,128)(2,1)S(1)}, u32[]{:S(2)}, u32[]{:S(2)}) collective-permute-start(bf16[64,128]{1,0:T(8,128)(2,1)S(1)} %get-tuple-element.14), channel_id=1, source_target_pairs={{0,2},{1,15},{2,0},{3,13},{4,6},{5,11},{6,4},{7,9},{8,10},{9,7},{1... | collective-permute-start | bytes 49160 | tf_op jit(solution)/shard_map/ppermute | solution.py:269
  14.1 2.9 %collective-permute-done.3.refs_0_.refs_4_ = bf16[64,128]{1,0:T(8,128)(2,1)S(1)} collective-permute-done((bf16[64,128]{1,0:T(8,128)(2,1)S(1)}, bf16[64,128]{1,0:T(8,128)(2,1)S(1)}, u32[]{:S(2)}, u32[]{:S(2)}) %collective-permute-start.3) | collective-permute-done | bytes 16416 | tf_op jit(solution)/shard_map/ppermute | solution.py:269
  17.0 0.3 %collective-permute-done.4.refs_1_.refs_5_ = bf16[64,128]{1,0:T(8,128)(2,1)S(1)} collective-permute-done((bf16[64,128]{1,0:T(8,128)(2,1)S(1)}, bf16[64,128]{1,0:T(8,128)(2,1)S(1)}, u32[]{:S(2)}, u32[]{:S(2)}) %collective-permute-start.4) | collective-permute-done | bytes 16416 | tf_op jit(solution)/shard_map/ppermute | solution.py:269
  17.3 3.4 %collective-permute-start.6 = (bf16[64,128]{1,0:T(8,128)(2,1)S(1)}, bf16[64,128]{1,0:T(8,128)(2,1)S(1)}, u32[]{:S(2)}, u32[]{:S(2)}) collective-permute-start(bf16[64,128]{1,0:T(8,128)(2,1)S(1)} %core.3), channel_id=1, source_target_pairs={{0,1},{1,0},{2,3},{3,2},{4,5},{5,4},{6,7},{7,6},{8,9},{9,8},{10,11... | collective-permute-start | bytes 49160 | tf_op jit(solution)/shard_map/ppermute | solution.py:260
  20.7 0.0 copy-done
  20.7 0.4 %weights.1.w_ref = bf16[128,1024]{1,0:T(8,128)(2,1)S(1)} custom-call(bf16[1024,128]{1,0:T(8,128)(2,1)S(1)} %copy-done), custom_call_target="tpu_custom_call" | custom-call | tf_op jit(solution)/shard_map/weights/pallas_call | solution.py:285
  21.1 0.0 copy-start.1
  21.1 0.4 %collective-permute-done.6.refs_7_ = bf16[64,128]{1,0:T(8,128)(2,1)S(1)} collective-permute-done((bf16[64,128]{1,0:T(8,128)(2,1)S(1)}, bf16[64,128]{1,0:T(8,128)(2,1)S(1)}, u32[]{:S(2)}, u32[]{:S(2)}) %collective-permute-start.6) | collective-permute-done | bytes 16416 | tf_op jit(solution)/shard_map/ppermute | solution.py:260
  21.6 0.0 collective-permute-done.5.refs_6_
  21.6 0.2 copy-done.1
  21.8 2.1 %pair.1 = bf16[2,8,64,128]{3,2,1,0:T(8,128)(2,1)} custom-call(f32[1,128]{1,0:T(1,128)S(1)} %bitcast.7, bf16[128,1024]{1,0:T(8,128)(2,1)S(1)} %weights.1.w_ref, bf16[256,128]{1,0:T(8,128)(2,1)S(1)} %get-tuple-element.10.own_ref.refs_0_, bf16[256,128]{1,0:T(8,128)(2,1)S(1)} %collective-permute-done.other_ref.refs_1_, ...), custom_call_target="tpu_custom_call" | custom-call | tf_op jit(solution)/shard_map/pair/pallas_call | solution.py:314
  (3 shorter events, 0.0 us)
Async XLA Ops:
  1.6 19.1 %copy-start = (bf16[1024,128]{1,0:T(8,128)(2,1)S(1)}, bf16[1024,128]{1,0:T(8,128)(2,1)}, u32[]{:S(2)}) copy-start(bf16[1024,128]{1,0:T(8,128)(2,1)} %w_ref.1) | copy-start | bytes 786436
  1.6 1.4 %collective-permute-start = (bf16[256,128]{1,0:T(8,128)(2,1)S(1)}, bf16[256,128]{1,0:T(8,128)(2,1)S(1)}, u32[]{:S(2)}, u32[]{:S(2)}) collective-permute-start(bf16[256,128]{1,0:T(8,128)(2,1)S(1)} %get-tuple-element.10.own_ref.refs_0_), channel_id=1, source_target_pairs={{0,1},{1,0},{2,3},{3,2},{4,5},{5,4},{6,7},{7,6},{8,9},{9,8},{10,11... | collective-permute-start | bytes 196616 | tf_op jit(solution)/shard_map/ppermute | solution.py:260
  3.1 9.2 %collective-permute-start.2 = (bf16[320,128]{1,0:T(8,128)(2,1)S(1)}, bf16[320,128]{1,0:T(8,128)(2,1)S(1)}, u32[]{:S(2)}, u32[]{:S(2)}) collective-permute-start(bf16[320,128]{1,0:T(8,128)(2,1)S(1)} %get-tuple-element.12), channel_id=1, source_target_pairs={{0,4},{1,9},{2,6},{3,11},{4,0},{5,13},{6,2},{7,15},{8,12},{9,1},{1... | collective-permute-start | bytes 245768 | tf_op jit(solution)/shard_map/ppermute | solution.py:269
  6.1 6.2 %collective-permute-start.1 = (bf16[160,128]{1,0:T(8,128)(2,1)S(1)}, bf16[160,128]{1,0:T(8,128)(2,1)S(1)}, u32[]{:S(2)}, u32[]{:S(2)}) collective-permute-start(bf16[160,128]{1,0:T(8,128)(2,1)S(1)} %get-tuple-element.11), channel_id=1, source_target_pairs={{0,12},{1,13},{2,14},{3,15},{4,8},{5,9},{6,10},{7,11},{8,4},{9,5},... | collective-permute-start | bytes 122888 | tf_op jit(solution)/shard_map/ppermute | solution.py:269
  12.2 9.3 %collective-permute-start.5 = (bf16[432,128]{1,0:T(8,128)(2,1)S(1)}, bf16[432,128]{1,0:T(8,128)(2,1)S(1)}, u32[]{:S(2)}, u32[]{:S(2)}) collective-permute-start(bf16[432,128]{1,0:T(8,128)(2,1)S(1)} %core.2), channel_id=1, source_target_pairs={{0,1},{1,0},{2,3},{3,2},{4,5},{5,4},{6,7},{7,6},{8,9},{9,8},{10,11... | collective-permute-start | bytes 331784 | tf_op jit(solution)/shard_map/ppermute | solution.py:260
  12.3 4.7 %collective-permute-start.3 = (bf16[64,128]{1,0:T(8,128)(2,1)S(1)}, bf16[64,128]{1,0:T(8,128)(2,1)S(1)}, u32[]{:S(2)}, u32[]{:S(2)}) collective-permute-start(bf16[64,128]{1,0:T(8,128)(2,1)S(1)} %get-tuple-element.13), channel_id=1, source_target_pairs={{0,6},{1,11},{2,4},{3,9},{4,2},{5,15},{6,0},{7,13},{8,14},{9,3},{1... | collective-permute-start | bytes 49160 | tf_op jit(solution)/shard_map/ppermute | solution.py:269
  13.6 3.8 %collective-permute-start.4 = (bf16[64,128]{1,0:T(8,128)(2,1)S(1)}, bf16[64,128]{1,0:T(8,128)(2,1)S(1)}, u32[]{:S(2)}, u32[]{:S(2)}) collective-permute-start(bf16[64,128]{1,0:T(8,128)(2,1)S(1)} %get-tuple-element.14), channel_id=1, source_target_pairs={{0,2},{1,15},{2,0},{3,13},{4,6},{5,11},{6,4},{7,9},{8,10},{9,7},{1... | collective-permute-start | bytes 49160 | tf_op jit(solution)/shard_map/ppermute | solution.py:269
  17.3 4.2 %collective-permute-start.6 = (bf16[64,128]{1,0:T(8,128)(2,1)S(1)}, bf16[64,128]{1,0:T(8,128)(2,1)S(1)}, u32[]{:S(2)}, u32[]{:S(2)}) collective-permute-start(bf16[64,128]{1,0:T(8,128)(2,1)S(1)} %core.3), channel_id=1, source_target_pairs={{0,1},{1,0},{2,3},{3,2},{4,5},{5,4},{6,7},{7,6},{8,9},{9,8},{10,11... | collective-permute-start | bytes 49160 | tf_op jit(solution)/shard_map/ppermute | solution.py:260
  21.1 0.7 %copy-start.1 = (f32[128]{0:T(128)S(1)}, f32[128]{0:T(128)}, u32[]{:S(2)}) copy-start(f32[128]{0:T(128)} %param.17) | copy-start | bytes 1540

commit v5 on v4

--- a/solution.py
+++ b/solution.py
@@ -22,9 +22,9 @@
     return lax.broadcasted_iota(jnp.int32, shape, len(shape) - 1)
 
 
-def project_kernel(n_res, solo, *refs):
+def project_kernel(n_res, steps, *refs):
     n_in = 7
-    sources, outs, scratch = refs[:n_in], refs[n_in : -n_in - 4], refs[-n_in - 4 :]
+    sources, (slab_out, *z_outs), scratch = refs[:n_in], refs[n_in : -n_in - 4], refs[-n_in - 4 :]
     landed, (rows_scr, lane_scr, right_scr, sems) = scratch[:n_in], scratch[n_in:]
     copies = [pltpu.make_async_copy(a, b, sems.at[i]) for i, (a, b) in enumerate(zip(sources, landed))]
     for copy in copies:
@@ -32,7 +32,6 @@
     for copy in copies:
         copy.wait()
     x_ref, scale_ref, shift_ref, w1_ref, b1_ref, w2_ref, b2_ref = landed
-    slab_out, solo_out = outs
     n_s, span, width = x_ref.shape
     chans = w1_ref.shape[0]
     fold = LANES // chans
@@ -75,9 +74,10 @@
     part = n_left // n_res
     slab_out[:n_right] = right_slab
     slab_out[n_right:] = lane_scr[...].astype(jnp.bfloat16)
-    to = partner(lax.axis_index("res"), solo, n_res)
-    solo_out[:n_right] = right_slab
-    solo_out[n_right:] = lane_scr[pl.ds(pl.multiple_of(to * part, part), part), :].astype(jnp.bfloat16)
+    for step, out in zip(steps, z_outs):
+        to = partner(lax.axis_index("res"), step, n_res)
+        out[:n_right] = right_slab
+        out[n_right:] = lane_scr[pl.ds(pl.multiple_of(to * part, part), part), :].astype(jnp.bfloat16)
 
 
 def chip_kernel(n_res, steps, own_ref, other_ref, *outs):
@@ -87,25 +87,21 @@
     for (first, second), out in zip(steps, outs):
         to = partner(here, jnp.where(me == 0, first, second), n_res)
         start = pl.multiple_of(n_right + to * part, part)
-        at = out.shape[0] - 2 * part
-        if at:
-            out[:n_right] = own_ref[:n_right]
-            out[n_right:at] = other_ref[:n_right]
-        out[at : at + part] = own_ref[pl.ds(start, part), :]
-        out[at + part :] = other_ref[pl.ds(start, part), :]
-
-
-def core_kernel(parts, part, own, *refs):
+        out[:part] = own_ref[pl.ds(start, part), :]
+        out[part:] = other_ref[pl.ds(start, part), :]
+
+
+def core_kernel(n_z, part, own, *refs):
     ins, out = refs[:-1], refs[-1]
-    mine = pl.multiple_of((1 - lax.axis_index("seq")) * own, own)
+    mine = (1 - lax.axis_index("seq")) * own
     at = 0
-    for ref, n_parts in zip(ins, parts):
-        body = ref.shape[0] - n_parts * part
+    for k, ref in enumerate(ins):
+        body = ref.shape[0] - part if k < n_z else 0
         if body:
             out[at : at + body] = ref[:body]
             at += body
-        for k in range(n_parts):
-            out[at : at + own] = ref[pl.ds(pl.multiple_of(body + k * part + mine, own), own), :]
+        for start in range(body, ref.shape[0], part):
+            out[at : at + own] = ref[pl.ds(pl.multiple_of(start + mine, own), own), :]
             at += own
 
 
@@ -126,7 +122,8 @@
 def pair_kernel(plan, total, offset_ref, w_ref, *refs):
     out_ref, left_scr, outer_scr = refs[-3], refs[-2], refs[-1]
     n_col, chans, part, own = plan["n_col"], plan["chans"], plan["part"], plan["own"]
-    n_right = part * plan["n_res"]
+    n_res, pairs_of = plan["n_res"], plan["pairs"]
+    n_right = part * n_res
     me = lax.axis_index("seq")
     half = LANES // 2
     fold = LANES // chans
@@ -135,38 +132,33 @@
     turns = rows_dev // fold
     n_s = own // turns
 
-    own_ref, other_ref, solo_ref = refs[:3]
-    n_pairs = plan["n_pairs"]
-    b_refs = refs[3 : 3 + n_pairs]
-    x_refs = refs[3 + n_pairs : 3 + n_pairs + (n_col - 1) * (n_pairs + 1)]
-    z_other, x_other = refs[3 + n_pairs + (n_col - 1) * (n_pairs + 1) : -3]
+    own_ref, other_ref = refs[:2]
+    z_refs = refs[2 : 1 + n_res]
+    x_refs = refs[1 + n_res : 1 + n_res + (n_col - 1) * len(pairs_of)]
+    other_in = refs[-4]
     mine = pl.multiple_of(me * own, own)
 
     def rows_of(ref, at):
         return ref[pl.ds(at, own), :].astype(jnp.float32)
 
     start = pl.multiple_of(n_right + lax.axis_index("res") * part + mine, own)
-    rights = [(own_ref, 0), (other_ref, 0), (solo_ref, 0), (z_other, 0)]
+    rights = [(own_ref, 0), (other_ref, 0)]
     lefts = [[rows_of(own_ref, start), rows_of(other_ref, start)]]
-    lefts[0] += [rows_of(solo_ref, pl.multiple_of(n_right + mine, own)), rows_of(z_other, n_right)]
-    for k, ref in enumerate(b_refs):
-        at = n_right + own + k * 2 * (n_right + own)
-        rights += [(ref, 0), (ref, n_right), (z_other, at + n_right), (z_other, at)]
-        lefts[0] += [rows_of(ref, pl.multiple_of(2 * n_right + h * part + mine, own)) for h in range(2)]
-        lefts[0] += [rows_of(z_other, at + 2 * n_right + (1 - h) * own) for h in range(2)]
+    for k, ref in enumerate(z_refs):
+        at = k * (n_right + own)
+        rights += [(ref, 0), (other_in, at)]
+        lefts[0] += [rows_of(ref, pl.multiple_of(n_right + mine, own)), rows_of(other_in, at + n_right)]
     for u in range(n_col - 1):
-        chunks = []
-        for k in range(n_pairs + 1):
-            place = u * (n_pairs + 1) + k
+        chunks = [None] * n_res
+        for k, (first, second) in enumerate(pairs_of):
+            place = u * len(pairs_of) + k
+            at = (n_res - 1) * (n_right + own) + 2 * place * own
             heard = [rows_of(x_refs[place], pl.multiple_of(h * part + mine, own)) for h in range(2)]
-            told = [rows_of(x_other, (2 * place + 1 - h) * own) for h in range(2)]
-            if k < n_pairs:
-                chunks += heard + told
-            else:
-                near = [jnp.where(me == 0, a, b) for a, b in zip(heard, told)]
-                far = [jnp.where(me == 0, b, a) for a, b in zip(heard, told)]
-                chunks = near + far + chunks
-        lefts.append(chunks)
+            told = [rows_of(other_in, at + (1 - h) * own) for h in range(2)]
+            chunks[first] = [jnp.where(me == 0, a, b) for a, b in zip(heard, told)]
+            chunks[second] = [jnp.where(me == 0, b, a) for a, b in zip(heard, told)]
+        order = [0] + plan["z_steps"]
+        lefts.append([slab for step in order for slab in chunks[step]])
 
     for u in range(n_col):
         for turn in range(turns):
@@ -236,15 +228,15 @@
     def rows(n):
         return jax.ShapeDtypeStruct((n, LANES), bf16)
 
-    solo = n_res - 1
-    pairs = [(k, k + 1) for k in range(1, solo, 2)]
+    z_steps = [k for k in range(1, n_res) if k > 1] + [1] * (n_res > 1)
+    pairs = [(k, k + 1) for k in range(1, n_res - 1, 2)] + [(0, n_res - 1)]
 
     taken = (alignment, scale.reshape(1, -1), shift.reshape(1, -1), w1.T, b1.reshape(1, -1), w2.T, b2.reshape(1, -1))
-    slab, solo_out = pl.pallas_call(
-        functools.partial(project_kernel, n_res, solo),
-        out_shape=[rows(n_right + n_left), rows(n_right + part)],
+    slab, *z_out = pl.pallas_call(
+        functools.partial(project_kernel, n_res, z_steps),
+        out_shape=[rows(n_right + n_left)] + [rows(n_right + part)] * len(z_steps),
         in_specs=[HBM] * len(taken),
-        out_specs=[VMEM] * 2,
+        out_specs=[VMEM] * n_res,
         scratch_shapes=[pltpu.VMEM(a.shape, a.dtype) for a in taken]
         + [
             pltpu.VMEM((n_s * span, LANES), jnp.float32),
@@ -269,18 +261,17 @@
         return lax.ppermute(array, ("res", "col", "seq"), route)
 
     slab_in = to_core(slab)
-    solo_in = to_chip(solo_out, 0, (solo, solo))
-    sends = [(0, steps) for steps in pairs]
-    sends += [(u, steps) for u in range(1, n_col) for steps in pairs + [(0, solo)]]
+    z_in = [to_chip(array, 0, (step, step)) for array, step in zip(z_out, z_steps)]
+    sends = [(u, steps) for u in range(1, n_col) for steps in pairs]
     messages = pl.pallas_call(
         functools.partial(chip_kernel, n_res, [steps for _, steps in sends]),
-        out_shape=[rows(2 * part + (0 if u else 2 * n_right)) for u, _ in sends],
+        out_shape=[rows(2 * part)] * len(sends),
         in_specs=[VMEM] * 2,
         out_specs=[VMEM] * len(sends),
         compiler_params=params,
         name="chip",
     )(slab, slab_in)
-    heard = [to_chip(message, u, steps) for message, (u, steps) in zip(messages, sends)]
+    x_in = [to_chip(message, u, steps) for message, (u, steps) in zip(messages, sends)]
 
     weights = pl.pallas_call(
         weight_kernel,
@@ -292,10 +283,10 @@
         name="weights",
     )(w_final)
 
-    def share(arrays, parts, n_rows):
+    def share(n_z, arrays):
         packed = pl.pallas_call(
-            functools.partial(core_kernel, parts, part, own),
-            out_shape=rows(n_rows),
+            functools.partial(core_kernel, n_z, part, own),
+            out_shape=rows(n_z * (n_right + own) + (len(arrays) - n_z) * 2 * own),
             in_specs=[VMEM] * len(arrays),
             out_specs=VMEM,
             compiler_params=params,
@@ -303,14 +294,12 @@
         )(*arrays)
         return to_core(packed)
 
-    z_in, x_in = heard[: len(pairs)], heard[len(pairs) :]
-    z_other = share([solo_in] + z_in, [1] + [2] * len(z_in), (2 * len(pairs) + 1) * (n_right + own))
-    x_other = share(x_in, [2] * len(x_in), 2 * own * len(x_in))
+    other_in = share(len(z_in), z_in + x_in)
 
     turns = rows_dev * chans // LANES
     depth = turns * n_s * n_res * n_seq
-    plan = dict(n_res=n_res, n_col=n_col, chans=chans, part=part, own=own, n_pairs=len(pairs))
-    operands = (offset.reshape(1, -1), weights, slab, slab_in, solo_in, *heard, z_other, x_other)
+    plan = dict(n_res=n_res, n_col=n_col, chans=chans, part=part, own=own, pairs=pairs, z_steps=z_steps)
+    operands = (offset.reshape(1, -1), weights, slab, slab_in, *z_in, *x_in, other_in)
     return pl.pallas_call(
         functools.partial(pair_kernel, plan, float(n_s * n_res * n_seq)),
         out_shape=jax.ShapeDtypeStruct((n_col, rows_dev, span, pair_width), bf16),

time: 24.1 us -> 19.2 us (0.80)
  waiting for transfers between devices: 8.23 us -> 3.77 us
    ppermute x4 -> x5, waiting for transfers between devices: 6.9 us -> 3.2 us  [to_chip(): return lax.ppermute(array, ('res', 'col', 'seq'), route)]
    ppermute x3 -> x2, starting transfers between devices: 4.02 us -> 2.47 us  [to_core(): return lax.ppermute(array, 'seq', [(q, 1 - q) for q in range(n_seq)])]
    ppermute x4 -> x5, starting transfers between devices: 7.21 us -> 8.5 us  [to_chip(): return lax.ppermute(array, ('res', 'col', 'seq'), route)]
    ppermute x3 -> x2, waiting for transfers between devices: 1.33 us -> 0.57 us  [to_core(): return lax.ppermute(array, 'seq', [(q, 1 - q) for q in range(n_seq)])]
    pallas_call x3 -> x2, Pallas kernels: 1.63 us -> 1.63 us  [the longest x1 1.62 us: per_device(): pl.pallas_call(functools.partial(project_kernel, n_res, z_steps), out_sha...]
  transfers between devices with their start and end apart: 7 -> 7, of which waited for: 5 -> 4; matrix products, arithmetic and copies ran while one was open for 0% -> 0% of each run, Pallas kernels for 2% -> 2%
where the time goes in v5:
time: 19.2 us; the launch traced here: 19 us
  starting transfers between devices  11 us (57%)
  Pallas kernels  4.17 us (22%)
  waiting for transfers between devices  3.77 us (20%)
    ppermute x5, starting transfers between devices, to_chip(): return lax.ppermute(array, ('res', 'col', 'seq'), route)  8.5 us
    ppermute x5, waiting for transfers between devices, to_chip(): return lax.ppermute(array, ('res', 'col', 'seq'), route)  3.2 us
    ppermute x2, starting transfers between devices, to_core(): return lax.ppermute(array, 'seq', [(q, 1 - q) for q in range(n_seq)])  2.47 us
    pallas_call x1, Pallas kernels, per_device(): pl.pallas_call(functools.partial(pair_kernel, plan, float(n_s * n_res * n...  2.14 us
    pallas_call x1, Pallas kernels, per_device(): pl.pallas_call(functools.partial(project_kernel, n_res, z_steps), out_sha...  1.62 us
    ppermute x2, waiting for transfers between devices, to_core(): return lax.ppermute(array, 'seq', [(q, 1 - q) for q in range(n_seq)])  0.57 us
    pallas_call x1, Pallas kernels, per_device(): pl.pallas_call(weight_kernel, out_shape=jax.ShapeDtypeStruct((pair_width,...  0.39 us
  transfers between devices with their start and end apart: 7, of which 4 were waited for; matrix products, arithmetic and copies ran while one was open for 0% of the time, Pallas kernels for 2%

profile of v5, /device:TPU:0, one launch (start us, length us, event | category | flops | bytes accessed | tf_op | source)
XLA Modules:
  0.0 19.0 jit_solution(18332413799203441248)
XLA Ops:
  0.0 1.6 %project.1 = (bf16[256,128]{1,0:T(8,128)(2,1)S(1)}, bf16[160,128]{1,0:T(8,128)(2,1)S(1)}, bf16[160,128]{1,0:T(8,128)(2,1)S(1)}, bf16[160,128]{1,0:T(8,128)(2,1)S(1)}) custom-call(bf16[8,64,256]{2,1,0:T(8,128)(2,1)} %refs_0_.1, f32[1,256]{1,0:T(1,128)} %bitcast.10, f32[1,256]{1,0:T(1,128)} %bitcast.11, bf16[32,256]{1,0:T(8,128)(2,1)} %bitcast.8, ...), custom_call_target="tpu_custom_call" | custom-call | tf_op jit(solution)/shard_map/project/pallas_call | solution.py:235
  1.6 0.0 copy-start
  1.6 0.5 %collective-permute-start = (bf16[256,128]{1,0:T(8,128)(2,1)S(1)}, bf16[256,128]{1,0:T(8,128)(2,1)S(1)}, u32[]{:S(2)}, u32[]{:S(2)}) collective-permute-start(bf16[256,128]{1,0:T(8,128)(2,1)S(1)} %get-tuple-element.11.own_ref.refs_0_), channel_id=1, source_target_pairs={{0,1},{1,0},{2,3},{3,2},{4,5},{5,4},{6,7},{7,6},{8,9},{9,8},{10,11... | collective-permute-start | bytes 196616 | tf_op jit(solution)/shard_map/ppermute | solution.py:252
  2.2 3.7 %collective-permute-start.1 = (bf16[160,128]{1,0:T(8,128)(2,1)S(1)}, bf16[160,128]{1,0:T(8,128)(2,1)S(1)}, u32[]{:S(2)}, u32[]{:S(2)}) collective-permute-start(bf16[160,128]{1,0:T(8,128)(2,1)S(1)} %get-tuple-element.12), channel_id=1, source_target_pairs={{0,8},{1,9},{2,10},{3,11},{4,12},{5,13},{6,14},{7,15},{8,0},{9,1},... | collective-permute-start | bytes 122888 | tf_op jit(solution)/shard_map/ppermute | solution.py:261
  5.8 1.3 %collective-permute-start.2 = (bf16[160,128]{1,0:T(8,128)(2,1)S(1)}, bf16[160,128]{1,0:T(8,128)(2,1)S(1)}, u32[]{:S(2)}, u32[]{:S(2)}) collective-permute-start(bf16[160,128]{1,0:T(8,128)(2,1)S(1)} %get-tuple-element.13), channel_id=1, source_target_pairs={{0,12},{1,13},{2,14},{3,15},{4,8},{5,9},{6,10},{7,11},{8,4},{9,5},... | collective-permute-start | bytes 122888 | tf_op jit(solution)/shard_map/ppermute | solution.py:261
  7.2 0.2 %collective-permute-start.3 = (bf16[160,128]{1,0:T(8,128)(2,1)S(1)}, bf16[160,128]{1,0:T(8,128)(2,1)S(1)}, u32[]{:S(2)}, u32[]{:S(2)}) collective-permute-start(bf16[160,128]{1,0:T(8,128)(2,1)S(1)} %get-tuple-element.14), channel_id=1, source_target_pairs={{0,4},{1,5},{2,6},{3,7},{4,0},{5,1},{6,2},{7,3},{8,12},{9,13},{10,... | collective-permute-start | bytes 122888 | tf_op jit(solution)/shard_map/ppermute | solution.py:261
  7.4 0.0 collective-permute-done.other_ref.refs_1_
  7.4 2.7 %collective-permute-start.4 = (bf16[64,128]{1,0:T(8,128)(2,1)S(1)}, bf16[64,128]{1,0:T(8,128)(2,1)S(1)}, u32[]{:S(2)}, u32[]{:S(2)}) collective-permute-start(bf16[64,128]{1,0:T(8,128)(2,1)S(1)} %get-tuple-element.15), channel_id=1, source_target_pairs={{0,6},{1,11},{2,4},{3,9},{4,2},{5,15},{6,0},{7,13},{8,14},{9,3},{1... | collective-permute-start | bytes 49160 | tf_op jit(solution)/shard_map/ppermute | solution.py:261
  10.1 0.5 %collective-permute-start.5 = (bf16[64,128]{1,0:T(8,128)(2,1)S(1)}, bf16[64,128]{1,0:T(8,128)(2,1)S(1)}, u32[]{:S(2)}, u32[]{:S(2)}) collective-permute-start(bf16[64,128]{1,0:T(8,128)(2,1)S(1)} %get-tuple-element.16), channel_id=1, source_target_pairs={{0,2},{1,15},{2,0},{3,13},{4,6},{5,11},{6,4},{7,9},{8,10},{9,7},{1... | collective-permute-start | bytes 49160 | tf_op jit(solution)/shard_map/ppermute | solution.py:261
  10.7 0.0 collective-permute-done.1.refs_0_.refs_2_
  10.7 1.1 %collective-permute-done.2.refs_1_.refs_3_ = bf16[160,128]{1,0:T(8,128)(2,1)S(1)} collective-permute-done((bf16[160,128]{1,0:T(8,128)(2,1)S(1)}, bf16[160,128]{1,0:T(8,128)(2,1)S(1)}, u32[]{:S(2)}, u32[]{:S(2)}) %collective-permute-start.2) | collective-permute-done | bytes 40992 | tf_op jit(solution)/shard_map/ppermute | solution.py:261
  11.7 0.0 collective-permute-done.3.refs_2_.refs_4_
  11.7 1.3 %collective-permute-done.4.refs_3_.refs_5_ = bf16[64,128]{1,0:T(8,128)(2,1)S(1)} collective-permute-done((bf16[64,128]{1,0:T(8,128)(2,1)S(1)}, bf16[64,128]{1,0:T(8,128)(2,1)S(1)}, u32[]{:S(2)}, u32[]{:S(2)}) %collective-permute-start.4) | collective-permute-done | bytes 16416 | tf_op jit(solution)/shard_map/ppermute | solution.py:261
  13.0 0.9 %collective-permute-done.5.refs_4_.refs_6_ = bf16[64,128]{1,0:T(8,128)(2,1)S(1)} collective-permute-done((bf16[64,128]{1,0:T(8,128)(2,1)S(1)}, bf16[64,128]{1,0:T(8,128)(2,1)S(1)}, u32[]{:S(2)}, u32[]{:S(2)}) %collective-permute-start.5) | collective-permute-done | bytes 16416 | tf_op jit(solution)/shard_map/ppermute | solution.py:261
  13.9 2.0 %collective-permute-start.6 = (bf16[496,128]{1,0:T(8,128)(2,1)S(1)}, bf16[496,128]{1,0:T(8,128)(2,1)S(1)}, u32[]{:S(2)}, u32[]{:S(2)}) collective-permute-start(bf16[496,128]{1,0:T(8,128)(2,1)S(1)} %core.1), channel_id=1, source_target_pairs={{0,1},{1,0},{2,3},{3,2},{4,5},{5,4},{6,7},{7,6},{8,9},{9,8},{10,11... | collective-permute-start | bytes 380936 | tf_op jit(solution)/shard_map/ppermute | solution.py:252
  15.8 0.0 copy-done
  15.8 0.4 %weights.1.w_ref = bf16[128,1024]{1,0:T(8,128)(2,1)S(1)} custom-call(bf16[1024,128]{1,0:T(8,128)(2,1)S(1)} %copy-done), custom_call_target="tpu_custom_call" | custom-call | tf_op jit(solution)/shard_map/weights/pallas_call | solution.py:276
  16.2 0.0 copy-start.1
  16.3 0.6 %collective-permute-done.6.refs_7_ = bf16[496,128]{1,0:T(8,128)(2,1)S(1)} collective-permute-done((bf16[496,128]{1,0:T(8,128)(2,1)S(1)}, bf16[496,128]{1,0:T(8,128)(2,1)S(1)}, u32[]{:S(2)}, u32[]{:S(2)}) %collective-permute-start.6) | collective-permute-done | bytes 127008 | tf_op jit(solution)/shard_map/ppermute | solution.py:252
  16.8 0.1 copy-done.1
  16.9 2.1 %pair.1 = bf16[2,8,64,128]{3,2,1,0:T(8,128)(2,1)} custom-call(f32[1,128]{1,0:T(1,128)S(1)} %bitcast.7, bf16[128,1024]{1,0:T(8,128)(2,1)S(1)} %weights.1.w_ref, bf16[256,128]{1,0:T(8,128)(2,1)S(1)} %get-tuple-element.11.own_ref.refs_0_, bf16[256,128]{1,0:T(8,128)(2,1)S(1)} %collective-permute-done.other_ref.refs_1_, ...), custom_call_target="tpu_custom_call" | custom-call | tf_op jit(solution)/shard_map/pair/pallas_call | solution.py:303
  (2 shorter events, 0.0 us)
Async XLA Ops:
  1.6 14.2 %copy-start = (bf16[1024,128]{1,0:T(8,128)(2,1)S(1)}, bf16[1024,128]{1,0:T(8,128)(2,1)}, u32[]{:S(2)}) copy-start(bf16[1024,128]{1,0:T(8,128)(2,1)} %w_ref.1) | copy-start | bytes 786436
  1.6 5.8 %collective-permute-start = (bf16[256,128]{1,0:T(8,128)(2,1)S(1)}, bf16[256,128]{1,0:T(8,128)(2,1)S(1)}, u32[]{:S(2)}, u32[]{:S(2)}) collective-permute-start(bf16[256,128]{1,0:T(8,128)(2,1)S(1)} %get-tuple-element.11.own_ref.refs_0_), channel_id=1, source_target_pairs={{0,1},{1,0},{2,3},{3,2},{4,5},{5,4},{6,7},{7,6},{8,9},{9,8},{10,11... | collective-permute-start | bytes 196616 | tf_op jit(solution)/shard_map/ppermute | solution.py:252
  2.2 8.5 %collective-permute-start.1 = (bf16[160,128]{1,0:T(8,128)(2,1)S(1)}, bf16[160,128]{1,0:T(8,128)(2,1)S(1)}, u32[]{:S(2)}, u32[]{:S(2)}) collective-permute-start(bf16[160,128]{1,0:T(8,128)(2,1)S(1)} %get-tuple-element.12), channel_id=1, source_target_pairs={{0,8},{1,9},{2,10},{3,11},{4,12},{5,13},{6,14},{7,15},{8,0},{9,1},... | collective-permute-start | bytes 122888 | tf_op jit(solution)/shard_map/ppermute | solution.py:261
  5.8 5.9 %collective-permute-start.2 = (bf16[160,128]{1,0:T(8,128)(2,1)S(1)}, bf16[160,128]{1,0:T(8,128)(2,1)S(1)}, u32[]{:S(2)}, u32[]{:S(2)}) collective-permute-start(bf16[160,128]{1,0:T(8,128)(2,1)S(1)} %get-tuple-element.13), channel_id=1, source_target_pairs={{0,12},{1,13},{2,14},{3,15},{4,8},{5,9},{6,10},{7,11},{8,4},{9,5},... | collective-permute-start | bytes 122888 | tf_op jit(solution)/shard_map/ppermute | solution.py:261
  7.2 4.6 %collective-permute-start.3 = (bf16[160,128]{1,0:T(8,128)(2,1)S(1)}, bf16[160,128]{1,0:T(8,128)(2,1)S(1)}, u32[]{:S(2)}, u32[]{:S(2)}) collective-permute-start(bf16[160,128]{1,0:T(8,128)(2,1)S(1)} %get-tuple-element.14), channel_id=1, source_target_pairs={{0,4},{1,5},{2,6},{3,7},{4,0},{5,1},{6,2},{7,3},{8,12},{9,13},{10,... | collective-permute-start | bytes 122888 | tf_op jit(solution)/shard_map/ppermute | solution.py:261
  7.4 5.6 %collective-permute-start.4 = (bf16[64,128]{1,0:T(8,128)(2,1)S(1)}, bf16[64,128]{1,0:T(8,128)(2,1)S(1)}, u32[]{:S(2)}, u32[]{:S(2)}) collective-permute-start(bf16[64,128]{1,0:T(8,128)(2,1)S(1)} %get-tuple-element.15), channel_id=1, source_target_pairs={{0,6},{1,11},{2,4},{3,9},{4,2},{5,15},{6,0},{7,13},{8,14},{9,3},{1... | collective-permute-start | bytes 49160 | tf_op jit(solution)/shard_map/ppermute | solution.py:261
  10.1 3.7 %collective-permute-start.5 = (bf16[64,128]{1,0:T(8,128)(2,1)S(1)}, bf16[64,128]{1,0:T(8,128)(2,1)S(1)}, u32[]{:S(2)}, u32[]{:S(2)}) collective-permute-start(bf16[64,128]{1,0:T(8,128)(2,1)S(1)} %get-tuple-element.16), channel_id=1, source_target_pairs={{0,2},{1,15},{2,0},{3,13},{4,6},{5,11},{6,4},{7,9},{8,10},{9,7},{1... | collective-permute-start | bytes 49160 | tf_op jit(solution)/shard_map/ppermute | solution.py:261
  13.9 2.9 %collective-permute-start.6 = (bf16[496,128]{1,0:T(8,128)(2,1)S(1)}, bf16[496,128]{1,0:T(8,128)(2,1)S(1)}, u32[]{:S(2)}, u32[]{:S(2)}) collective-permute-start(bf16[496,128]{1,0:T(8,128)(2,1)S(1)} %core.1), channel_id=1, source_target_pairs={{0,1},{1,0},{2,3},{3,2},{4,5},{5,4},{6,7},{7,6},{8,9},{9,8},{10,11... | collective-permute-start | bytes 380936 | tf_op jit(solution)/shard_map/ppermute | solution.py:252
  16.2 0.7 %copy-start.1 = (f32[128]{0:T(128)S(1)}, f32[128]{0:T(128)}, u32[]{:S(2)}) copy-start(f32[128]{0:T(128)} %param.17) | copy-start | bytes 1540

commit v6 on v5

--- a/solution.py
+++ b/solution.py
@@ -91,16 +91,15 @@
         out[part:] = other_ref[pl.ds(start, part), :]
 
 
-def core_kernel(n_z, part, own, *refs):
+def core_kernel(n_rights, part, own, *refs):
     ins, out = refs[:-1], refs[-1]
     mine = (1 - lax.axis_index("seq")) * own
     at = 0
-    for k, ref in enumerate(ins):
-        body = ref.shape[0] - part if k < n_z else 0
-        if body:
-            out[at : at + body] = ref[:body]
-            at += body
-        for start in range(body, ref.shape[0], part):
+    for ref in ins:
+        if n_rights:
+            out[at : at + n_rights] = ref[:n_rights]
+            at += n_rights
+        for start in range(n_rights, ref.shape[0], part):
             out[at : at + own] = ref[pl.ds(pl.multiple_of(start + mine, own), own), :]
             at += own
 
@@ -119,62 +118,89 @@
         out_ref[:, tile * LANES : (tile + 1) * LANES] = piece.T.astype(jnp.bfloat16)
 
 
-def pair_kernel(plan, total, offset_ref, w_ref, *refs):
-    out_ref, left_scr, outer_scr = refs[-3], refs[-2], refs[-1]
-    n_col, chans, part, own = plan["n_col"], plan["chans"], plan["part"], plan["own"]
-    n_res, pairs_of = plan["n_res"], plan["pairs"]
-    n_right = part * n_res
-    me = lax.axis_index("seq")
+def fill_left(left_scr, u, slabs, n_s):
+    turns = slabs[0].shape[0] // n_s
+    for turn in range(turns):
+        column = jnp.concatenate([slab[turn * n_s : (turn + 1) * n_s] for slab in slabs], axis=0)
+        depth = column.shape[0]
+        left_scr[u * LANES : (u + 1) * LANES, turn * depth : (turn + 1) * depth] = column.T.astype(jnp.bfloat16)
+
+
+def loop_blocks(n_blocks, body):
+    if n_blocks == 1:
+        body(0)
+    else:
+        pl.loop(0, n_blocks)(body)
+
+
+def update_block(plan, block, u_base, offset, w_ref, weight_of, left_scr, outer_scr, staged):
+    chans, total = plan["chans"], plan["total"]
     half = LANES // 2
     fold = LANES // chans
+    left = left_scr[...]
+    n_u = left.shape[0] // LANES
+    for pair in range(chans // 2):
+        outer = jnp.dot(left, weight_of(pair), preferred_element_type=jnp.float32).astype(jnp.bfloat16)
+        for side in range(2):
+            at = (2 * pair + side) * chans
+            for tile in range(n_u * fold):
+                outer_scr[at : at + chans, tile * LANES : (tile + 1) * LANES] = outer[
+                    tile * chans : (tile + 1) * chans, side * LANES : (side + 1) * LANES
+                ]
+    for u in range(n_u):
+        summed = jnp.dot(
+            w_ref[...], outer_scr[:, u * fold * LANES : (u + 1) * fold * LANES], preferred_element_type=jnp.float32
+        )
+        for residue in range(fold):
+            piece = summed[:, residue * LANES : (residue + 1) * LANES].T
+            piece = (piece / total + offset).astype(jnp.bfloat16)
+            for turn in range(LANES // half):
+                staged[u, turn * fold + residue, pl.ds(block * half, half), :] = piece[
+                    turn * half : (turn + 1) * half
+                ]
+
+
+def write_out(plan, u_base, staged, out_ref, sems):
+    n_col = plan["n_col"]
+    col = lax.axis_index("col")
+    copies = []
+    for u in range(staged.shape[0]):
+        step = u_base + u
+        source = partner(col, step, n_col) if n_col & (n_col - 1) == 0 else (col - step + n_col) % n_col
+        copies.append(pltpu.make_async_copy(staged.at[u], out_ref.at[source], sems.at[u]))
+    for copy in copies:
+        copy.start()
+    for copy in copies:
+        copy.wait()
+
+
+def near_kernel(plan, offset_ref, w_ref, own_ref, other_ref, *refs):
+    z_refs, (other_in, out_ref, weights_out, left_scr, outer_scr, staged, sems) = refs[:-7], refs[-7:]
+    chans, part, own, n_s = plan["chans"], plan["part"], plan["own"], plan["n_s"]
+    n_right = part * plan["n_res"]
+    half = LANES // 2
     pairs = chans // 2
-    rows_dev = out_ref.shape[1]
-    turns = rows_dev // fold
-    n_s = own // turns
-
-    own_ref, other_ref = refs[:2]
-    z_refs = refs[2 : 1 + n_res]
-    x_refs = refs[1 + n_res : 1 + n_res + (n_col - 1) * len(pairs_of)]
-    other_in = refs[-4]
-    mine = pl.multiple_of(me * own, own)
+    mine = pl.multiple_of(lax.axis_index("seq") * own, own)
 
     def rows_of(ref, at):
         return ref[pl.ds(at, own), :].astype(jnp.float32)
 
     start = pl.multiple_of(n_right + lax.axis_index("res") * part + mine, own)
     rights = [(own_ref, 0), (other_ref, 0)]
-    lefts = [[rows_of(own_ref, start), rows_of(other_ref, start)]]
+    lefts = [rows_of(own_ref, start), rows_of(other_ref, start)]
     for k, ref in enumerate(z_refs):
         at = k * (n_right + own)
         rights += [(ref, 0), (other_in, at)]
-        lefts[0] += [rows_of(ref, pl.multiple_of(n_right + mine, own)), rows_of(other_in, at + n_right)]
-    for u in range(n_col - 1):
-        chunks = [None] * n_res
-        for k, (first, second) in enumerate(pairs_of):
-            place = u * len(pairs_of) + k
-            at = (n_res - 1) * (n_right + own) + 2 * place * own
-            heard = [rows_of(x_refs[place], pl.multiple_of(h * part + mine, own)) for h in range(2)]
-            told = [rows_of(other_in, at + (1 - h) * own) for h in range(2)]
-            chunks[first] = [jnp.where(me == 0, a, b) for a, b in zip(heard, told)]
-            chunks[second] = [jnp.where(me == 0, b, a) for a, b in zip(heard, told)]
-        order = [0] + plan["z_steps"]
-        lefts.append([slab for step in order for slab in chunks[step]])
-
-    for u in range(n_col):
-        for turn in range(turns):
-            column = jnp.concatenate([slab[turn * n_s : (turn + 1) * n_s] for slab in lefts[u]], axis=0)
-            depth = column.shape[0]
-            left_scr[u * LANES : (u + 1) * LANES, turn * depth : (turn + 1) * depth] = column.T.astype(jnp.bfloat16)
-
-    n_blocks = n_right // (pairs * n_s)
+        lefts += [rows_of(ref, pl.multiple_of(n_right + mine, own)), rows_of(other_in, at + n_right)]
+    fill_left(left_scr, 0, lefts, n_s)
+    depth = left_scr.shape[1]
     offset = offset_ref[...]
-    col = lax.axis_index("col")
 
     def block_of_columns(block):
         at_block = block * pairs * n_s
         slabs = [ref[pl.ds(at + at_block, pairs * n_s), :].astype(jnp.float32) for ref, at in rights]
-        left = left_scr[...]
-        for pair in range(pairs):
+
+        def weight_of(pair):
             here = jnp.concatenate([slab[pair * n_s : (pair + 1) * n_s] for slab in slabs], axis=0)
             there = pltpu.roll(here, half, 1)
             low = lane_index(here.shape) < half
@@ -185,32 +211,46 @@
                 ],
                 axis=1,
             ).astype(jnp.bfloat16)
-            outer = jnp.dot(left, weights, preferred_element_type=jnp.float32).astype(jnp.bfloat16)
-            for side in range(2):
-                at = (2 * pair + side) * chans
-                for tile in range(n_col * fold):
-                    outer_scr[at : at + chans, tile * LANES : (tile + 1) * LANES] = outer[
-                        tile * chans : (tile + 1) * chans, side * LANES : (side + 1) * LANES
-                    ]
-        for u in range(n_col):
-            summed = jnp.dot(
-                w_ref[...],
-                outer_scr[:, u * fold * LANES : (u + 1) * fold * LANES],
-                preferred_element_type=jnp.float32,
-            )
-            to = partner(col, u, n_col) if n_col & (n_col - 1) == 0 else (col - u + n_col) % n_col
-            for residue in range(fold):
-                piece = summed[:, residue * LANES : (residue + 1) * LANES].T
-                piece = (piece / total + offset).astype(jnp.bfloat16)
-                for turn in range(turns):
-                    out_ref[to, turn * fold + residue, pl.ds(block * half, half), :] = piece[
-                        turn * half : (turn + 1) * half
-                    ]
-
-    if n_blocks == 1:
-        block_of_columns(0)
-    else:
-        pl.loop(0, n_blocks)(block_of_columns)
+            weights_out[pl.ds((block * pairs + pair) * depth, depth), :] = weights
+            return weights
+
+        update_block(plan, block, 0, offset, w_ref, weight_of, left_scr, outer_scr, staged)
+
+    loop_blocks(n_right // (pairs * n_s), block_of_columns)
+    write_out(plan, 0, staged, out_ref, sems)
+
+
+def far_kernel(plan, offset_ref, w_ref, weights_ref, *refs):
+    x_refs, (other_in, _, out_ref, left_scr, outer_scr, staged, sems) = refs[:-7], refs[-7:]
+    chans, part, own, n_s, n_res = plan["chans"], plan["part"], plan["own"], plan["n_s"], plan["n_res"]
+    pairs = chans // 2
+    me = lax.axis_index("seq")
+
+    def rows_of(ref, at):
+        return ref[pl.ds(at, own), :].astype(jnp.float32)
+
+    n_pairs = len(plan["pairs"])
+    for u in range(plan["n_col"] - 1):
+        chunks = [None] * n_res
+        for k, (first, second) in enumerate(plan["pairs"]):
+            place = u * n_pairs + k
+            heard = [rows_of(x_refs[place], pl.multiple_of(h * part + me * own, own)) for h in range(2)]
+            told = [rows_of(other_in, (2 * place + 1 - h) * own) for h in range(2)]
+            chunks[first] = [jnp.where(me == 0, a, b) for a, b in zip(heard, told)]
+            chunks[second] = [jnp.where(me == 0, b, a) for a, b in zip(heard, told)]
+        order = [0] + plan["z_steps"]
+        fill_left(left_scr, u, [slab for step in order for slab in chunks[step]], n_s)
+    depth = left_scr.shape[1]
+    offset = offset_ref[...]
+
+    def block_of_columns(block):
+        def weight_of(pair):
+            return weights_ref[pl.ds((block * pairs + pair) * depth, depth), :]
+
+        update_block(plan, block, 1, offset, w_ref, weight_of, left_scr, outer_scr, staged)
+
+    loop_blocks(weights_ref.shape[0] // (pairs * depth), block_of_columns)
+    write_out(plan, 1, staged, out_ref, sems)
 
 
 def per_device(alignment, scale, shift, w1, b1, w2, b2, w_final, offset):
@@ -283,34 +323,59 @@
         name="weights",
     )(w_final)
 
-    def share(n_z, arrays):
+    def share(arrays, n_rights, n_parts, cost):
         packed = pl.pallas_call(
-            functools.partial(core_kernel, n_z, part, own),
-            out_shape=rows(n_z * (n_right + own) + (len(arrays) - n_z) * 2 * own),
+            functools.partial(core_kernel, n_rights, part, own),
+            out_shape=rows(len(arrays) * (n_rights + n_parts * own)),
             in_specs=[VMEM] * len(arrays),
             out_specs=VMEM,
             compiler_params=params,
+            cost_estimate=cost,
             name="core",
         )(*arrays)
         return to_core(packed)
 
-    other_in = share(len(z_in), z_in + x_in)
+    other_z = share(z_in, n_right, 1, None)
+    other_x = share(x_in, 0, 2, pl.CostEstimate(flops=20_000_000_000, bytes_accessed=0, transcendentals=0))
 
     turns = rows_dev * chans // LANES
     depth = turns * n_s * n_res * n_seq
-    plan = dict(n_res=n_res, n_col=n_col, chans=chans, part=part, own=own, pairs=pairs, z_steps=z_steps)
-    operands = (offset.reshape(1, -1), weights, slab, slab_in, *z_in, *x_in, other_in)
+    total = float(n_s * n_res * n_seq)
+    plan = dict(
+        n_res=n_res, n_col=n_col, chans=chans, part=part, own=own, n_s=n_s, pairs=pairs, z_steps=z_steps, total=total
+    )
+    out_type = jax.ShapeDtypeStruct((n_col, rows_dev, span, pair_width), bf16)
+    n_blocks = n_right // (chans // 2 * n_s)
+
+    def scratch(n_u):
+        return [
+            pltpu.VMEM((n_u * LANES, depth), bf16),
+            pltpu.VMEM((chans * chans, n_u * (LANES // chans) * LANES), bf16),
+            pltpu.VMEM((n_u, rows_dev, span, pair_width), bf16),
+            pltpu.SemaphoreType.DMA((n_u,)),
+        ]
+
+    offset = offset.reshape(1, -1)
+    operands = (offset, weights, slab, slab_in, *z_in, other_z)
+    out, spread = pl.pallas_call(
+        functools.partial(near_kernel, plan),
+        out_shape=[out_type, jax.ShapeDtypeStruct((n_blocks * chans // 2 * depth, 2 * LANES), bf16)],
+        in_specs=[VMEM] * len(operands),
+        out_specs=[HBM, VMEM],
+        scratch_shapes=scratch(1),
+        compiler_params=params,
+        name="near",
+    )(*operands)
+    operands = (offset, weights, spread, *x_in, other_x, out)
     return pl.pallas_call(
-        functools.partial(pair_kernel, plan, float(n_s * n_res * n_seq)),
-        out_shape=jax.ShapeDtypeStruct((n_col, rows_dev, span, pair_width), bf16),
-        in_specs=[VMEM] * len(operands),
-        out_specs=VMEM,
-        scratch_shapes=[
-            pltpu.VMEM((n_col * LANES, depth), bf16),
-            pltpu.VMEM((chans * chans, n_col * (LANES // chans) * LANES), bf16),
-        ],
-        compiler_params=params,
-        name="pair",
+        functools.partial(far_kernel, plan),
+        out_shape=out_type,
+        in_specs=[VMEM] * (len(operands) - 1) + [HBM],
+        out_specs=HBM,
+        scratch_shapes=scratch(n_col - 1),
+        input_output_aliases={len(operands) - 1: 0},
+        compiler_params=params,
+        name="far",
     )(*operands)
 
 

time: 19.2 us -> 20 us (1.042)
  Pallas kernels: 4.17 us -> 5.07 us
  waiting for transfers between devices: 3.77 us -> 3.1 us
  local copies, waits for them, and re-layouts: 0.09 us -> 0.65 us
    pallas_call x2 -> x4, Pallas kernels: 2.15 us -> 3.05 us  [the longest x1 1.52 us: per_device(): pl.pallas_call(functools.partial(near_kernel, plan), out_shape=[out_type,...]
    ppermute x2 -> x3, waiting for transfers between devices: 0.57 us -> 0.01 us  [to_core(): return lax.ppermute(array, 'seq', [(q, 1 - q) for q in range(n_seq)])]
    unnamed x4, local copies, waits for them, and re-layouts: 0.09 us -> 0.65 us
    ppermute x2 -> x3, starting transfers between devices: 2.47 us -> 2.48 us  [to_core(): return lax.ppermute(array, 'seq', [(q, 1 - q) for q in range(n_seq)])]
  transfers between devices with their start and end apart: 7 -> 8, of which waited for: 4 -> 3; matrix products, arithmetic and copies ran while one was open for 0% -> 0% of each run, Pallas kernels for 2% -> 10%
where the time goes in v6:
time: 20 us; the launch traced here: 19.9 us
  starting transfers between devices  11 us (55%)
  Pallas kernels  5.07 us (25%)
  waiting for transfers between devices  3.1 us (16%)
  local copies, waits for them, and re-layouts  0.65 us (3%)
    ppermute x5, starting transfers between devices, to_chip(): return lax.ppermute(array, ('res', 'col', 'seq'), route)  8.5 us
    ppermute x5, waiting for transfers between devices, to_chip(): return lax.ppermute(array, ('res', 'col', 'seq'), route)  3.09 us
    ppermute x3, starting transfers between devices, to_core(): return lax.ppermute(array, 'seq', [(q, 1 - q) for q in range(n_seq)])  2.48 us
    pallas_call x1, Pallas kernels, per_device(): pl.pallas_call(functools.partial(project_kernel, n_res, z_steps), out_sha...  1.62 us
    pallas_call x1, Pallas kernels, per_device(): pl.pallas_call(functools.partial(near_kernel, plan), out_shape=[out_type,...  1.52 us
    pallas_call x1, Pallas kernels, per_device(): pl.pallas_call(functools.partial(far_kernel, plan), out_shape=out_type, i...  1.52 us
    unnamed x4, local copies, waits for them, and re-layouts  0.65 us
  transfers between devices with their start and end apart: 8, of which 3 were waited for; matrix products, arithmetic and copies ran while one was open for 0% of the time, Pallas kernels for 10%

profile of v6, /device:TPU:0, one launch (start us, length us, event | category | flops | bytes accessed | tf_op | source)
XLA Modules:
  0.0 19.9 jit_solution(2770474807540947647)
XLA Ops:
  0.0 1.6 %project.1 = (bf16[256,128]{1,0:T(8,128)(2,1)S(1)}, bf16[160,128]{1,0:T(8,128)(2,1)S(1)}, bf16[160,128]{1,0:T(8,128)(2,1)S(1)}, bf16[160,128]{1,0:T(8,128)(2,1)S(1)}) custom-call(bf16[8,64,256]{2,1,0:T(8,128)(2,1)} %refs_0_.1, f32[1,256]{1,0:T(1,128)} %bitcast.11, f32[1,256]{1,0:T(1,128)} %bitcast.12, bf16[32,256]{1,0:T(8,128)(2,1)} %bitcast.9, ...), custom_call_target="tpu_custom_call" | custom-call | tf_op jit(solution)/shard_map/project/pallas_call | solution.py:275
  1.6 0.5 %collective-permute-start = (bf16[256,128]{1,0:T(8,128)(2,1)S(1)}, bf16[256,128]{1,0:T(8,128)(2,1)S(1)}, u32[]{:S(2)}, u32[]{:S(2)}) collective-permute-start(bf16[256,128]{1,0:T(8,128)(2,1)S(1)} %get-tuple-element.13.own_ref), channel_id=1, source_target_pairs={{0,1},{1,0},{2,3},{3,2},{4,5},{5,4},{6,7},{7,6},{8,9},{9,8},{10,11... | collective-permute-start | bytes 196616 | tf_op jit(solution)/shard_map/ppermute | solution.py:292
  2.1 3.7 %collective-permute-start.1 = (bf16[160,128]{1,0:T(8,128)(2,1)S(1)}, bf16[160,128]{1,0:T(8,128)(2,1)S(1)}, u32[]{:S(2)}, u32[]{:S(2)}) collective-permute-start(bf16[160,128]{1,0:T(8,128)(2,1)S(1)} %get-tuple-element.14), channel_id=1, source_target_pairs={{0,8},{1,9},{2,10},{3,11},{4,12},{5,13},{6,14},{7,15},{8,0},{9,1},... | collective-permute-start | bytes 122888 | tf_op jit(solution)/shard_map/ppermute | solution.py:301
  5.8 1.3 %collective-permute-start.2 = (bf16[160,128]{1,0:T(8,128)(2,1)S(1)}, bf16[160,128]{1,0:T(8,128)(2,1)S(1)}, u32[]{:S(2)}, u32[]{:S(2)}) collective-permute-start(bf16[160,128]{1,0:T(8,128)(2,1)S(1)} %get-tuple-element.15), channel_id=1, source_target_pairs={{0,12},{1,13},{2,14},{3,15},{4,8},{5,9},{6,10},{7,11},{8,4},{9,5},... | collective-permute-start | bytes 122888 | tf_op jit(solution)/shard_map/ppermute | solution.py:301
  7.2 0.2 %collective-permute-start.3 = (bf16[160,128]{1,0:T(8,128)(2,1)S(1)}, bf16[160,128]{1,0:T(8,128)(2,1)S(1)}, u32[]{:S(2)}, u32[]{:S(2)}) collective-permute-start(bf16[160,128]{1,0:T(8,128)(2,1)S(1)} %get-tuple-element.16), channel_id=1, source_target_pairs={{0,4},{1,5},{2,6},{3,7},{4,0},{5,1},{6,2},{7,3},{8,12},{9,13},{10,... | collective-permute-start | bytes 122888 | tf_op jit(solution)/shard_map/ppermute | solution.py:301
  7.4 0.0 collective-permute-done.other_ref
  7.4 2.7 %collective-permute-start.5 = (bf16[64,128]{1,0:T(8,128)(2,1)S(1)}, bf16[64,128]{1,0:T(8,128)(2,1)S(1)}, u32[]{:S(2)}, u32[]{:S(2)}) collective-permute-start(bf16[64,128]{1,0:T(8,128)(2,1)S(1)} %get-tuple-element.18), channel_id=1, source_target_pairs={{0,6},{1,11},{2,4},{3,9},{4,2},{5,15},{6,0},{7,13},{8,14},{9,3},{1... | collective-permute-start | bytes 49160 | tf_op jit(solution)/shard_map/ppermute | solution.py:301
  10.1 0.5 %collective-permute-start.6 = (bf16[64,128]{1,0:T(8,128)(2,1)S(1)}, bf16[64,128]{1,0:T(8,128)(2,1)S(1)}, u32[]{:S(2)}, u32[]{:S(2)}) collective-permute-start(bf16[64,128]{1,0:T(8,128)(2,1)S(1)} %get-tuple-element.19), channel_id=1, source_target_pairs={{0,2},{1,15},{2,0},{3,13},{4,6},{5,11},{6,4},{7,9},{8,10},{9,7},{1... | collective-permute-start | bytes 49160 | tf_op jit(solution)/shard_map/ppermute | solution.py:301
  10.7 0.0 collective-permute-done.1.refs_0_
  10.7 1.1 %collective-permute-done.2.refs_1_ = bf16[160,128]{1,0:T(8,128)(2,1)S(1)} collective-permute-done((bf16[160,128]{1,0:T(8,128)(2,1)S(1)}, bf16[160,128]{1,0:T(8,128)(2,1)S(1)}, u32[]{:S(2)}, u32[]{:S(2)}) %collective-permute-start.2) | collective-permute-done | bytes 40992 | tf_op jit(solution)/shard_map/ppermute | solution.py:301
  11.7 0.0 collective-permute-done.3.refs_2_
  11.7 0.0 copy-start
  11.7 0.1 collective-permute-start.4
  11.8 1.2 %collective-permute-done.5.refs_0_ = bf16[64,128]{1,0:T(8,128)(2,1)S(1)} collective-permute-done((bf16[64,128]{1,0:T(8,128)(2,1)S(1)}, bf16[64,128]{1,0:T(8,128)(2,1)S(1)}, u32[]{:S(2)}, u32[]{:S(2)}) %collective-permute-start.5) | collective-permute-done | bytes 16416 | tf_op jit(solution)/shard_map/ppermute | solution.py:301
  13.0 0.9 %collective-permute-done.6.refs_1_ = bf16[64,128]{1,0:T(8,128)(2,1)S(1)} collective-permute-done((bf16[64,128]{1,0:T(8,128)(2,1)S(1)}, bf16[64,128]{1,0:T(8,128)(2,1)S(1)}, u32[]{:S(2)}, u32[]{:S(2)}) %collective-permute-start.6) | collective-permute-done | bytes 16416 | tf_op jit(solution)/shard_map/ppermute | solution.py:301
  13.9 1.9 %collective-permute-start.7 = (bf16[64,128]{1,0:T(8,128)(2,1)S(1)}, bf16[64,128]{1,0:T(8,128)(2,1)S(1)}, u32[]{:S(2)}, u32[]{:S(2)}) collective-permute-start(bf16[64,128]{1,0:T(8,128)(2,1)S(1)} %core.3), channel_id=1, source_target_pairs={{0,1},{1,0},{2,3},{3,2},{4,5},{5,4},{6,7},{7,6},{8,9},{9,8},{10,11... | collective-permute-start | bytes 49160 | tf_op jit(solution)/shard_map/ppermute | solution.py:292
  15.8 0.0 copy-done
  15.8 0.4 %weights.1.w_ref = bf16[128,1024]{1,0:T(8,128)(2,1)S(1)} custom-call(bf16[1024,128]{1,0:T(8,128)(2,1)S(1)} %copy-done), custom_call_target="tpu_custom_call" | custom-call | tf_op jit(solution)/shard_map/weights/pallas_call | solution.py:316
  16.2 0.0 copy-start.1
  16.2 0.0 collective-permute-done.4.refs_3_
  16.2 0.6 %copy-done.1 = f32[128]{0:T(128)S(1)} copy-done((f32[128]{0:T(128)S(1)}, f32[128]{0:T(128)}, u32[]{:S(2)}) %copy-start.1) | copy-done | bytes 536
  16.8 1.5 %near.1 = (bf16[2,8,64,128]{3,2,1,0:T(8,128)(2,1)}, bf16[2048,256]{1,0:T(8,128)(2,1)S(1)}) custom-call(f32[1,128]{1,0:T(1,128)S(1)} %bitcast.7, bf16[128,1024]{1,0:T(8,128)(2,1)S(1)} %weights.1.w_ref, bf16[256,128]{1,0:T(8,128)(2,1)S(1)} %get-tuple-element.13.own_ref, bf16[256,128]{1,0:T(8,128)(2,1)S(1)} %collective-permute-done.other_ref, ...), custom_call_target="tpu_custom_call" | custom-call | tf_op jit(solution)/shard_map/near/pallas_call | solution.py:360
  18.3 0.0 collective-permute-done.7.refs_2_
  18.4 1.5 %far.1 = bf16[2,8,64,128]{3,2,1,0:T(8,128)(2,1)} custom-call(f32[1,128]{1,0:T(1,128)S(1)} %bitcast.8, bf16[128,1024]{1,0:T(8,128)(2,1)S(1)} %weights.1.w_ref, bf16[2048,256]{1,0:T(8,128)(2,1)S(1)} %get-tuple-element.17.weights_ref, bf16[64,128]{1,0:T(8,128)(2,1)S(1)} %collective-permute-done.5.refs_0_, ...), custom_call_target="tpu_custom_call", output_to_operand_aliasing={{}: (6, {})} | custom-call | tf_op jit(solution)/shard_map/far/pallas_call | solution.py:370
  (3 shorter events, 0.0 us)
Async XLA Ops:
  1.6 5.8 %collective-permute-start = (bf16[256,128]{1,0:T(8,128)(2,1)S(1)}, bf16[256,128]{1,0:T(8,128)(2,1)S(1)}, u32[]{:S(2)}, u32[]{:S(2)}) collective-permute-start(bf16[256,128]{1,0:T(8,128)(2,1)S(1)} %get-tuple-element.13.own_ref), channel_id=1, source_target_pairs={{0,1},{1,0},{2,3},{3,2},{4,5},{5,4},{6,7},{7,6},{8,9},{9,8},{10,11... | collective-permute-start | bytes 196616 | tf_op jit(solution)/shard_map/ppermute | solution.py:292
  2.1 8.5 %collective-permute-start.1 = (bf16[160,128]{1,0:T(8,128)(2,1)S(1)}, bf16[160,128]{1,0:T(8,128)(2,1)S(1)}, u32[]{:S(2)}, u32[]{:S(2)}) collective-permute-start(bf16[160,128]{1,0:T(8,128)(2,1)S(1)} %get-tuple-element.14), channel_id=1, source_target_pairs={{0,8},{1,9},{2,10},{3,11},{4,12},{5,13},{6,14},{7,15},{8,0},{9,1},... | collective-permute-start | bytes 122888 | tf_op jit(solution)/shard_map/ppermute | solution.py:301
  5.8 5.9 %collective-permute-start.2 = (bf16[160,128]{1,0:T(8,128)(2,1)S(1)}, bf16[160,128]{1,0:T(8,128)(2,1)S(1)}, u32[]{:S(2)}, u32[]{:S(2)}) collective-permute-start(bf16[160,128]{1,0:T(8,128)(2,1)S(1)} %get-tuple-element.15), channel_id=1, source_target_pairs={{0,12},{1,13},{2,14},{3,15},{4,8},{5,9},{6,10},{7,11},{8,4},{9,5},... | collective-permute-start | bytes 122888 | tf_op jit(solution)/shard_map/ppermute | solution.py:301
  7.2 4.6 %collective-permute-start.3 = (bf16[160,128]{1,0:T(8,128)(2,1)S(1)}, bf16[160,128]{1,0:T(8,128)(2,1)S(1)}, u32[]{:S(2)}, u32[]{:S(2)}) collective-permute-start(bf16[160,128]{1,0:T(8,128)(2,1)S(1)} %get-tuple-element.16), channel_id=1, source_target_pairs={{0,4},{1,5},{2,6},{3,7},{4,0},{5,1},{6,2},{7,3},{8,12},{9,13},{10,... | collective-permute-start | bytes 122888 | tf_op jit(solution)/shard_map/ppermute | solution.py:301
  7.4 5.6 %collective-permute-start.5 = (bf16[64,128]{1,0:T(8,128)(2,1)S(1)}, bf16[64,128]{1,0:T(8,128)(2,1)S(1)}, u32[]{:S(2)}, u32[]{:S(2)}) collective-permute-start(bf16[64,128]{1,0:T(8,128)(2,1)S(1)} %get-tuple-element.18), channel_id=1, source_target_pairs={{0,6},{1,11},{2,4},{3,9},{4,2},{5,15},{6,0},{7,13},{8,14},{9,3},{1... | collective-permute-start | bytes 49160 | tf_op jit(solution)/shard_map/ppermute | solution.py:301
  10.1 3.7 %collective-permute-start.6 = (bf16[64,128]{1,0:T(8,128)(2,1)S(1)}, bf16[64,128]{1,0:T(8,128)(2,1)S(1)}, u32[]{:S(2)}, u32[]{:S(2)}) collective-permute-start(bf16[64,128]{1,0:T(8,128)(2,1)S(1)} %get-tuple-element.19), channel_id=1, source_target_pairs={{0,2},{1,15},{2,0},{3,13},{4,6},{5,11},{6,4},{7,9},{8,10},{9,7},{1... | collective-permute-start | bytes 49160 | tf_op jit(solution)/shard_map/ppermute | solution.py:301
  11.7 4.0 %copy-start = (bf16[1024,128]{1,0:T(8,128)(2,1)S(1)}, bf16[1024,128]{1,0:T(8,128)(2,1)}, u32[]{:S(2)}) copy-start(bf16[1024,128]{1,0:T(8,128)(2,1)} %w_ref.1) | copy-start | bytes 786436
  11.7 4.4 %collective-permute-start.4 = (bf16[432,128]{1,0:T(8,128)(2,1)S(1)}, bf16[432,128]{1,0:T(8,128)(2,1)S(1)}, u32[]{:S(2)}, u32[]{:S(2)}) collective-permute-start(bf16[432,128]{1,0:T(8,128)(2,1)S(1)} %core.2), channel_id=1, source_target_pairs={{0,1},{1,0},{2,3},{3,2},{4,5},{5,4},{6,7},{7,6},{8,9},{9,8},{10,11... | collective-permute-start | bytes 331784 | tf_op jit(solution)/shard_map/ppermute | solution.py:292
  13.9 4.5 %collective-permute-start.7 = (bf16[64,128]{1,0:T(8,128)(2,1)S(1)}, bf16[64,128]{1,0:T(8,128)(2,1)S(1)}, u32[]{:S(2)}, u32[]{:S(2)}) collective-permute-start(bf16[64,128]{1,0:T(8,128)(2,1)S(1)} %core.3), channel_id=1, source_target_pairs={{0,1},{1,0},{2,3},{3,2},{4,5},{5,4},{6,7},{7,6},{8,9},{9,8},{10,11... | collective-permute-start | bytes 49160 | tf_op jit(solution)/shard_map/ppermute | solution.py:292
  16.2 0.7 %copy-start.1 = (f32[128]{0:T(128)S(1)}, f32[128]{0:T(128)}, u32[]{:S(2)}) copy-start(f32[128]{0:T(128)} %param.17) | copy-start | bytes 1540

commit v7 on v4

--- a/solution.py
+++ b/solution.py
@@ -24,7 +24,7 @@
 
 def project_kernel(n_res, solo, *refs):
     n_in = 7
-    sources, outs, scratch = refs[:n_in], refs[n_in : -n_in - 4], refs[-n_in - 4 :]
+    sources, (slab_out, solo_out), scratch = refs[:n_in], refs[n_in : -n_in - 4], refs[-n_in - 4 :]
     landed, (rows_scr, lane_scr, right_scr, sems) = scratch[:n_in], scratch[n_in:]
     copies = [pltpu.make_async_copy(a, b, sems.at[i]) for i, (a, b) in enumerate(zip(sources, landed))]
     for copy in copies:
@@ -32,7 +32,6 @@
     for copy in copies:
         copy.wait()
     x_ref, scale_ref, shift_ref, w1_ref, b1_ref, w2_ref, b2_ref = landed
-    slab_out, solo_out = outs
     n_s, span, width = x_ref.shape
     chans = w1_ref.shape[0]
     fold = LANES // chans
@@ -95,17 +94,16 @@
         out[at + part :] = other_ref[pl.ds(start, part), :]
 
 
-def core_kernel(parts, part, own, *refs):
+def core_kernel(bodies, part, own, *refs):
     ins, out = refs[:-1], refs[-1]
-    mine = pl.multiple_of((1 - lax.axis_index("seq")) * own, own)
+    mine = (1 - lax.axis_index("seq")) * own
     at = 0
-    for ref, n_parts in zip(ins, parts):
-        body = ref.shape[0] - n_parts * part
+    for body, ref in zip(bodies, ins):
         if body:
             out[at : at + body] = ref[:body]
             at += body
-        for k in range(n_parts):
-            out[at : at + own] = ref[pl.ds(pl.multiple_of(body + k * part + mine, own), own), :]
+        for start in range(body, ref.shape[0], part):
+            out[at : at + own] = ref[pl.ds(pl.multiple_of(start + mine, own), own), :]
             at += own
 
 
@@ -126,7 +124,8 @@
 def pair_kernel(plan, total, offset_ref, w_ref, *refs):
     out_ref, left_scr, outer_scr = refs[-3], refs[-2], refs[-1]
     n_col, chans, part, own = plan["n_col"], plan["chans"], plan["part"], plan["own"]
-    n_right = part * plan["n_res"]
+    n_res = plan["n_res"]
+    n_right = part * n_res
     me = lax.axis_index("seq")
     half = LANES // 2
     fold = LANES // chans
@@ -135,38 +134,40 @@
     turns = rows_dev // fold
     n_s = own // turns
 
+    z_pairs, x_pairs = plan["z_pairs"], plan["x_pairs"]
     own_ref, other_ref, solo_ref = refs[:3]
-    n_pairs = plan["n_pairs"]
-    b_refs = refs[3 : 3 + n_pairs]
-    x_refs = refs[3 + n_pairs : 3 + n_pairs + (n_col - 1) * (n_pairs + 1)]
-    z_other, x_other = refs[3 + n_pairs + (n_col - 1) * (n_pairs + 1) : -3]
+    z_refs = refs[3 : 3 + len(z_pairs)]
+    x_refs, other_in = refs[3 + len(z_pairs) : -4], refs[-4]
     mine = pl.multiple_of(me * own, own)
 
     def rows_of(ref, at):
         return ref[pl.ds(at, own), :].astype(jnp.float32)
 
     start = pl.multiple_of(n_right + lax.axis_index("res") * part + mine, own)
-    rights = [(own_ref, 0), (other_ref, 0), (solo_ref, 0), (z_other, 0)]
+    rights = [(own_ref, 0), (other_ref, 0), (solo_ref, 0), (other_in, 0)]
     lefts = [[rows_of(own_ref, start), rows_of(other_ref, start)]]
-    lefts[0] += [rows_of(solo_ref, pl.multiple_of(n_right + mine, own)), rows_of(z_other, n_right)]
-    for k, ref in enumerate(b_refs):
-        at = n_right + own + k * 2 * (n_right + own)
-        rights += [(ref, 0), (ref, n_right), (z_other, at + n_right), (z_other, at)]
+    lefts[0] += [rows_of(solo_ref, pl.multiple_of(n_right + mine, own)), rows_of(other_in, n_right)]
+    at = n_right + own
+    for ref in z_refs:
+        rights += [(ref, 0), (ref, n_right), (other_in, at + n_right), (other_in, at)]
         lefts[0] += [rows_of(ref, pl.multiple_of(2 * n_right + h * part + mine, own)) for h in range(2)]
-        lefts[0] += [rows_of(z_other, at + 2 * n_right + (1 - h) * own) for h in range(2)]
+        lefts[0] += [rows_of(other_in, at + 2 * n_right + (1 - h) * own) for h in range(2)]
+        at += 2 * (n_right + own)
+
+    def pick(first, second):
+        return [jnp.where(me == 0, a, b) for a, b in zip(first, second)]
+
     for u in range(n_col - 1):
-        chunks = []
-        for k in range(n_pairs + 1):
-            place = u * (n_pairs + 1) + k
+        chunks = [None] * n_res
+        for k, (first, second) in enumerate(x_pairs):
+            place = u * len(x_pairs) + k
             heard = [rows_of(x_refs[place], pl.multiple_of(h * part + mine, own)) for h in range(2)]
-            told = [rows_of(x_other, (2 * place + 1 - h) * own) for h in range(2)]
-            if k < n_pairs:
-                chunks += heard + told
-            else:
-                near = [jnp.where(me == 0, a, b) for a, b in zip(heard, told)]
-                far = [jnp.where(me == 0, b, a) for a, b in zip(heard, told)]
-                chunks = near + far + chunks
-        lefts.append(chunks)
+            told = [rows_of(other_in, at + (2 * place + 1 - h) * own) for h in range(2)]
+            chunks[first], chunks[second] = pick(heard, told), pick(told, heard)
+        order = chunks[0] + chunks[plan["solo"]]
+        for first, second in z_pairs:
+            order += pick(chunks[first], chunks[second]) + pick(chunks[second], chunks[first])
+        lefts.append(order)
 
     for u in range(n_col):
         for turn in range(turns):
@@ -237,7 +238,8 @@
         return jax.ShapeDtypeStruct((n, LANES), bf16)
 
     solo = n_res - 1
-    pairs = [(k, k + 1) for k in range(1, solo, 2)]
+    z_pairs = [(k, k + 1) for k in range(1, solo, 2)]
+    x_pairs = [(k, k + 1) for k in range(n_res - 2, -1, -2)]
 
     taken = (alignment, scale.reshape(1, -1), shift.reshape(1, -1), w1.T, b1.reshape(1, -1), w2.T, b2.reshape(1, -1))
     slab, solo_out = pl.pallas_call(
@@ -270,8 +272,7 @@
 
     slab_in = to_core(slab)
     solo_in = to_chip(solo_out, 0, (solo, solo))
-    sends = [(0, steps) for steps in pairs]
-    sends += [(u, steps) for u in range(1, n_col) for steps in pairs + [(0, solo)]]
+    sends = [(0, steps) for steps in z_pairs] + [(u, steps) for u in range(1, n_col) for steps in x_pairs]
     messages = pl.pallas_call(
         functools.partial(chip_kernel, n_res, [steps for _, steps in sends]),
         out_shape=[rows(2 * part + (0 if u else 2 * n_right)) for u, _ in sends],
@@ -292,25 +293,27 @@
         name="weights",
     )(w_final)
 
-    def share(arrays, parts, n_rows):
-        packed = pl.pallas_call(
-            functools.partial(core_kernel, parts, part, own),
-            out_shape=rows(n_rows),
+    def pack(arrays, bodies, flops):
+        return pl.pallas_call(
+            functools.partial(core_kernel, bodies, part, own),
+            out_shape=rows(sum(b + (a.shape[0] - b) // part * own for a, b in zip(arrays, bodies))),
             in_specs=[VMEM] * len(arrays),
             out_specs=VMEM,
             compiler_params=params,
+            cost_estimate=pl.CostEstimate(flops=flops, bytes_accessed=0, transcendentals=0),
             name="core",
         )(*arrays)
-        return to_core(packed)
-
-    z_in, x_in = heard[: len(pairs)], heard[len(pairs) :]
-    z_other = share([solo_in] + z_in, [1] + [2] * len(z_in), (2 * len(pairs) + 1) * (n_right + own))
-    x_other = share(x_in, [2] * len(x_in), 2 * own * len(x_in))
+
+    arrays = [pack([solo_in], [n_right], 500_000_000)] + heard
+    bodies = [n_right + own] + [array.shape[0] // part // n_res * n_right for array in heard]
+    other_in = to_core(pack(arrays, bodies, 0))
 
     turns = rows_dev * chans // LANES
     depth = turns * n_s * n_res * n_seq
-    plan = dict(n_res=n_res, n_col=n_col, chans=chans, part=part, own=own, n_pairs=len(pairs))
-    operands = (offset.reshape(1, -1), weights, slab, slab_in, solo_in, *heard, z_other, x_other)
+    plan = dict(
+        n_res=n_res, n_col=n_col, chans=chans, part=part, own=own, solo=solo, z_pairs=z_pairs, x_pairs=x_pairs
+    )
+    operands = (offset.reshape(1, -1), weights, slab, slab_in, solo_in, *heard, other_in)
     return pl.pallas_call(
         functools.partial(pair_kernel, plan, float(n_s * n_res * n_seq)),
         out_shape=jax.ShapeDtypeStruct((n_col, rows_dev, span, pair_width), bf16),

time: 24.1 us -> 17.2 us (0.71)
  waiting for transfers between devices: 8.23 us -> 4.23 us
  starting transfers between devices: 11.2 us -> 8.51 us
    ppermute x4, waiting for transfers between devices: 6.9 us -> 3.32 us  [to_chip(): return lax.ppermute(array, ('res', 'col', 'seq'), route)]
    ppermute x3 -> x2, starting transfers between devices: 4.02 us -> 0.59 us  [to_core(): return lax.ppermute(array, 'seq', [(q, 1 - q) for q in range(n_seq)])]
    ppermute x4, starting transfers between devices: 7.21 us -> 7.92 us  [to_chip(): return lax.ppermute(array, ('res', 'col', 'seq'), route)]
    ppermute x3 -> x2, waiting for transfers between devices: 1.33 us -> 0.9 us  [to_core(): return lax.ppermute(array, 'seq', [(q, 1 - q) for q in range(n_seq)])]
  transfers between devices with their start and end apart: 7 -> 6, of which waited for: 5 -> 3; matrix products, arithmetic and copies ran while one was open for 0% -> 0% of each run, Pallas kernels for 2% -> 2%
where the time goes in v7:
time: 17.2 us; the launch traced here: 17 us
  starting transfers between devices  8.51 us (49%)
  waiting for transfers between devices  4.23 us (25%)
  Pallas kernels  4.19 us (24%)
    ppermute x4, starting transfers between devices, to_chip(): return lax.ppermute(array, ('res', 'col', 'seq'), route)  7.92 us
    ppermute x4, waiting for transfers between devices, to_chip(): return lax.ppermute(array, ('res', 'col', 'seq'), route)  3.32 us
    pallas_call x1, Pallas kernels, per_device(): pl.pallas_call(functools.partial(pair_kernel, plan, float(n_s * n_res * n...  2.14 us
    pallas_call x1, Pallas kernels, per_device(): pl.pallas_call(functools.partial(project_kernel, n_res, solo), out_shape=...  1.62 us
    ppermute x2, waiting for transfers between devices, to_core(): return lax.ppermute(array, 'seq', [(q, 1 - q) for q in range(n_seq)])  0.9 us
    ppermute x2, starting transfers between devices, to_core(): return lax.ppermute(array, 'seq', [(q, 1 - q) for q in range(n_seq)])  0.59 us
    pallas_call x1, Pallas kernels, per_device(): pl.pallas_call(weight_kernel, out_shape=jax.ShapeDtypeStruct((pair_width,...  0.4 us
  transfers between devices with their start and end apart: 6, of which 3 were waited for; matrix products, arithmetic and copies ran while one was open for 0% of the time, Pallas kernels for 2%

profile of v7, /device:TPU:0, one launch (start us, length us, event | category | flops | bytes accessed | tf_op | source)
XLA Modules:
  0.0 17.0 jit_solution(16759459145541373911)
XLA Ops:
  0.0 1.6 %project.1 = (bf16[256,128]{1,0:T(8,128)(2,1)S(1)}, bf16[160,128]{1,0:T(8,128)(2,1)S(1)}) custom-call(bf16[8,64,256]{2,1,0:T(8,128)(2,1)} %refs_0_.1, f32[1,256]{1,0:T(1,128)} %bitcast.10, f32[1,256]{1,0:T(1,128)} %bitcast.11, bf16[32,256]{1,0:T(8,128)(2,1)} %bitcast.8, f32[1,32]{1,0:T(1,128)} %bitcast.12, bf16[32,256]{1,0:T(8,128)(2,1)} %bitcast.9, ...), custom_call_target="tpu_custom_call" | custom-call | tf_op jit(solution)/shard_map/project/pallas_call | solution.py:245
  1.6 0.5 %collective-permute-start = (bf16[256,128]{1,0:T(8,128)(2,1)S(1)}, bf16[256,128]{1,0:T(8,128)(2,1)S(1)}, u32[]{:S(2)}, u32[]{:S(2)}) collective-permute-start(bf16[256,128]{1,0:T(8,128)(2,1)S(1)} %get-tuple-element.10.own_ref.refs_0_), channel_id=1, source_target_pairs={{0,1},{1,0},{2,3},{3,2},{4,5},{5,4},{6,7},{7,6},{8,9},{9,8},{10,11... | collective-permute-start | bytes 196616 | tf_op jit(solution)/shard_map/ppermute | solution.py:262
  2.1 4.7 %collective-permute-start.1 = (bf16[160,128]{1,0:T(8,128)(2,1)S(1)}, bf16[160,128]{1,0:T(8,128)(2,1)S(1)}, u32[]{:S(2)}, u32[]{:S(2)}) collective-permute-start(bf16[160,128]{1,0:T(8,128)(2,1)S(1)} %get-tuple-element.11), channel_id=1, source_target_pairs={{0,12},{1,13},{2,14},{3,15},{4,8},{5,9},{6,10},{7,11},{8,4},{9,5},... | collective-permute-start | bytes 122888 | tf_op jit(solution)/shard_map/ppermute | solution.py:271
  6.8 0.0 collective-permute-done.other_ref.refs_1_
  6.8 0.1 collective-permute-start.2
  6.9 2.6 %collective-permute-start.3 = (bf16[64,128]{1,0:T(8,128)(2,1)S(1)}, bf16[64,128]{1,0:T(8,128)(2,1)S(1)}, u32[]{:S(2)}, u32[]{:S(2)}) collective-permute-start(bf16[64,128]{1,0:T(8,128)(2,1)S(1)} %get-tuple-element.13), channel_id=1, source_target_pairs={{0,10},{1,15},{2,8},{3,13},{4,14},{5,11},{6,12},{7,9},{8,2},{9,7},... | collective-permute-start | bytes 49160 | tf_op jit(solution)/shard_map/ppermute | solution.py:271
  9.6 0.5 %collective-permute-start.4 = (bf16[64,128]{1,0:T(8,128)(2,1)S(1)}, bf16[64,128]{1,0:T(8,128)(2,1)S(1)}, u32[]{:S(2)}, u32[]{:S(2)}) collective-permute-start(bf16[64,128]{1,0:T(8,128)(2,1)S(1)} %get-tuple-element.14), channel_id=1, source_target_pairs={{0,2},{1,7},{2,0},{3,5},{4,6},{5,3},{6,4},{7,1},{8,10},{9,15},{10,... | collective-permute-start | bytes 49160 | tf_op jit(solution)/shard_map/ppermute | solution.py:271
  10.1 0.0 collective-permute-done.1.refs_0_.refs_2_
  10.1 0.0 copy-start
  10.1 2.8 %collective-permute-done.3.refs_2_.refs_4_ = bf16[64,128]{1,0:T(8,128)(2,1)S(1)} collective-permute-done((bf16[64,128]{1,0:T(8,128)(2,1)S(1)}, bf16[64,128]{1,0:T(8,128)(2,1)S(1)}, u32[]{:S(2)}, u32[]{:S(2)}) %collective-permute-start.3) | collective-permute-done | bytes 16416 | tf_op jit(solution)/shard_map/ppermute | solution.py:271
  13.0 0.5 %collective-permute-done.4.refs_3_.refs_5_ = bf16[64,128]{1,0:T(8,128)(2,1)S(1)} collective-permute-done((bf16[64,128]{1,0:T(8,128)(2,1)S(1)}, bf16[64,128]{1,0:T(8,128)(2,1)S(1)}, u32[]{:S(2)}, u32[]{:S(2)}) %collective-permute-start.4) | collective-permute-done | bytes 16416 | tf_op jit(solution)/shard_map/ppermute | solution.py:271
  13.4 0.0 collective-permute-done.2.refs_1_.refs_3_
  13.5 0.1 collective-permute-start.5
  13.5 0.0 copy-done
  13.6 0.4 %weights.1.w_ref = bf16[128,1024]{1,0:T(8,128)(2,1)S(1)} custom-call(bf16[1024,128]{1,0:T(8,128)(2,1)S(1)} %copy-done), custom_call_target="tpu_custom_call" | custom-call | tf_op jit(solution)/shard_map/weights/pallas_call | solution.py:286
  14.0 0.0 copy-start.1
  14.0 0.9 %collective-permute-done.5.refs_6_ = bf16[496,128]{1,0:T(8,128)(2,1)S(1)} collective-permute-done((bf16[496,128]{1,0:T(8,128)(2,1)S(1)}, bf16[496,128]{1,0:T(8,128)(2,1)S(1)}, u32[]{:S(2)}, u32[]{:S(2)}) %collective-permute-start.5) | collective-permute-done | bytes 127008 | tf_op jit(solution)/shard_map/ppermute | solution.py:262
  14.9 0.0 copy-done.1
  14.9 2.1 %pair.1 = bf16[2,8,64,128]{3,2,1,0:T(8,128)(2,1)} custom-call(f32[1,128]{1,0:T(1,128)S(1)} %bitcast.7, bf16[128,1024]{1,0:T(8,128)(2,1)S(1)} %weights.1.w_ref, bf16[256,128]{1,0:T(8,128)(2,1)S(1)} %get-tuple-element.10.own_ref.refs_0_, bf16[256,128]{1,0:T(8,128)(2,1)S(1)} %collective-permute-done.other_ref.refs_1_, ...), custom_call_target="tpu_custom_call" | custom-call | tf_op jit(solution)/shard_map/pair/pallas_call | solution.py:317
  (3 shorter events, 0.0 us)
Async XLA Ops:
  1.6 5.2 %collective-permute-start = (bf16[256,128]{1,0:T(8,128)(2,1)S(1)}, bf16[256,128]{1,0:T(8,128)(2,1)S(1)}, u32[]{:S(2)}, u32[]{:S(2)}) collective-permute-start(bf16[256,128]{1,0:T(8,128)(2,1)S(1)} %get-tuple-element.10.own_ref.refs_0_), channel_id=1, source_target_pairs={{0,1},{1,0},{2,3},{3,2},{4,5},{5,4},{6,7},{7,6},{8,9},{9,8},{10,11... | collective-permute-start | bytes 196616 | tf_op jit(solution)/shard_map/ppermute | solution.py:262
  2.1 8.0 %collective-permute-start.1 = (bf16[160,128]{1,0:T(8,128)(2,1)S(1)}, bf16[160,128]{1,0:T(8,128)(2,1)S(1)}, u32[]{:S(2)}, u32[]{:S(2)}) collective-permute-start(bf16[160,128]{1,0:T(8,128)(2,1)S(1)} %get-tuple-element.11), channel_id=1, source_target_pairs={{0,12},{1,13},{2,14},{3,15},{4,8},{5,9},{6,10},{7,11},{8,4},{9,5},... | collective-permute-start | bytes 122888 | tf_op jit(solution)/shard_map/ppermute | solution.py:271
  6.8 6.6 %collective-permute-start.2 = (bf16[320,128]{1,0:T(8,128)(2,1)S(1)}, bf16[320,128]{1,0:T(8,128)(2,1)S(1)}, u32[]{:S(2)}, u32[]{:S(2)}) collective-permute-start(bf16[320,128]{1,0:T(8,128)(2,1)S(1)} %get-tuple-element.12), channel_id=1, source_target_pairs={{0,4},{1,9},{2,6},{3,11},{4,0},{5,13},{6,2},{7,15},{8,12},{9,1},{1... | collective-permute-start | bytes 245768 | tf_op jit(solution)/shard_map/ppermute | solution.py:271
  6.9 6.0 %collective-permute-start.3 = (bf16[64,128]{1,0:T(8,128)(2,1)S(1)}, bf16[64,128]{1,0:T(8,128)(2,1)S(1)}, u32[]{:S(2)}, u32[]{:S(2)}) collective-permute-start(bf16[64,128]{1,0:T(8,128)(2,1)S(1)} %get-tuple-element.13), channel_id=1, source_target_pairs={{0,10},{1,15},{2,8},{3,13},{4,14},{5,11},{6,12},{7,9},{8,2},{9,7},... | collective-permute-start | bytes 49160 | tf_op jit(solution)/shard_map/ppermute | solution.py:271
  9.6 3.9 %collective-permute-start.4 = (bf16[64,128]{1,0:T(8,128)(2,1)S(1)}, bf16[64,128]{1,0:T(8,128)(2,1)S(1)}, u32[]{:S(2)}, u32[]{:S(2)}) collective-permute-start(bf16[64,128]{1,0:T(8,128)(2,1)S(1)} %get-tuple-element.14), channel_id=1, source_target_pairs={{0,2},{1,7},{2,0},{3,5},{4,6},{5,3},{6,4},{7,1},{8,10},{9,15},{10,... | collective-permute-start | bytes 49160 | tf_op jit(solution)/shard_map/ppermute | solution.py:271
  10.1 3.4 %copy-start = (bf16[1024,128]{1,0:T(8,128)(2,1)S(1)}, bf16[1024,128]{1,0:T(8,128)(2,1)}, u32[]{:S(2)}) copy-start(bf16[1024,128]{1,0:T(8,128)(2,1)} %w_ref.1) | copy-start | bytes 786436
  13.5 1.4 %collective-permute-start.5 = (bf16[496,128]{1,0:T(8,128)(2,1)S(1)}, bf16[496,128]{1,0:T(8,128)(2,1)S(1)}, u32[]{:S(2)}, u32[]{:S(2)}) collective-permute-start(bf16[496,128]{1,0:T(8,128)(2,1)S(1)} %core.3), channel_id=1, source_target_pairs={{0,1},{1,0},{2,3},{3,2},{4,5},{5,4},{6,7},{7,6},{8,9},{9,8},{10,11... | collective-permute-start | bytes 380936 | tf_op jit(solution)/shard_map/ppermute | solution.py:262
  14.0 0.9 %copy-start.1 = (f32[128]{0:T(128)S(1)}, f32[128]{0:T(128)}, u32[]{:S(2)}) copy-start(f32[128]{0:T(128)} %param.17) | copy-start | bytes 1540

commit v8 on v6

--- a/solution.py
+++ b/solution.py
@@ -22,9 +22,9 @@
     return lax.broadcasted_iota(jnp.int32, shape, len(shape) - 1)
 
 
-def project_kernel(n_res, steps, *refs):
+def project_kernel(n_res, solo, *refs):
     n_in = 7
-    sources, (slab_out, *z_outs), scratch = refs[:n_in], refs[n_in : -n_in - 4], refs[-n_in - 4 :]
+    sources, (slab_out, solo_out), scratch = refs[:n_in], refs[n_in : -n_in - 4], refs[-n_in - 4 :]
     landed, (rows_scr, lane_scr, right_scr, sems) = scratch[:n_in], scratch[n_in:]
     copies = [pltpu.make_async_copy(a, b, sems.at[i]) for i, (a, b) in enumerate(zip(sources, landed))]
     for copy in copies:
@@ -74,10 +74,9 @@
     part = n_left // n_res
     slab_out[:n_right] = right_slab
     slab_out[n_right:] = lane_scr[...].astype(jnp.bfloat16)
-    for step, out in zip(steps, z_outs):
-        to = partner(lax.axis_index("res"), step, n_res)
-        out[:n_right] = right_slab
-        out[n_right:] = lane_scr[pl.ds(pl.multiple_of(to * part, part), part), :].astype(jnp.bfloat16)
+    to = partner(lax.axis_index("res"), solo, n_res)
+    solo_out[:n_right] = right_slab
+    solo_out[n_right:] = lane_scr[pl.ds(pl.multiple_of(to * part, part), part), :].astype(jnp.bfloat16)
 
 
 def chip_kernel(n_res, steps, own_ref, other_ref, *outs):
@@ -87,24 +86,28 @@
     for (first, second), out in zip(steps, outs):
         to = partner(here, jnp.where(me == 0, first, second), n_res)
         start = pl.multiple_of(n_right + to * part, part)
-        out[:part] = own_ref[pl.ds(start, part), :]
-        out[part:] = other_ref[pl.ds(start, part), :]
-
-
-def core_kernel(n_rights, part, own, *refs):
-    ins, out = refs[:-1], refs[-1]
+        at = out.shape[0] - 2 * part
+        if at:
+            out[:n_right] = own_ref[:n_right]
+            out[n_right:at] = other_ref[:n_right]
+        out[at : at + part] = own_ref[pl.ds(start, part), :]
+        out[at + part :] = other_ref[pl.ds(start, part), :]
+
+
+def core_kernel(bodies, part, own, *refs):
+    ins, out = refs[: len(bodies)], refs[-1]
     mine = (1 - lax.axis_index("seq")) * own
     at = 0
-    for ref in ins:
-        if n_rights:
-            out[at : at + n_rights] = ref[:n_rights]
-            at += n_rights
-        for start in range(n_rights, ref.shape[0], part):
+    for body, ref in zip(bodies, ins):
+        if body:
+            out[at : at + body] = ref[:body]
+            at += body
+        for start in range(body, ref.shape[0], part):
             out[at : at + own] = ref[pl.ds(pl.multiple_of(start + mine, own), own), :]
             at += own
 
 
-def weight_kernel(w_ref, out_ref, scr):
+def weight_kernel(w_ref, _, out_ref, scr):
     chans_sq, width = w_ref.shape
     chans = int(round(chans_sq**0.5))
     scr[...] = w_ref[...].astype(jnp.float32)
@@ -133,7 +136,7 @@
         pl.loop(0, n_blocks)(body)
 
 
-def update_block(plan, block, u_base, offset, w_ref, weight_of, left_scr, outer_scr, staged):
+def update_block(plan, block, offset, w_ref, weight_of, left_scr, outer_scr, staged):
     chans, total = plan["chans"], plan["total"]
     half = LANES // 2
     fold = LANES // chans
@@ -153,48 +156,50 @@
         )
         for residue in range(fold):
             piece = summed[:, residue * LANES : (residue + 1) * LANES].T
-            piece = (piece / total + offset).astype(jnp.bfloat16)
+            piece = (piece / total + offset[...]).astype(jnp.bfloat16)
             for turn in range(LANES // half):
                 staged[u, turn * fold + residue, pl.ds(block * half, half), :] = piece[
                     turn * half : (turn + 1) * half
                 ]
 
 
-def write_out(plan, u_base, staged, out_ref, sems):
+def start_out(plan, u_base, staged, out_ref, sems):
     n_col = plan["n_col"]
     col = lax.axis_index("col")
     copies = []
     for u in range(staged.shape[0]):
         step = u_base + u
         source = partner(col, step, n_col) if n_col & (n_col - 1) == 0 else (col - step + n_col) % n_col
-        copies.append(pltpu.make_async_copy(staged.at[u], out_ref.at[source], sems.at[u]))
-    for copy in copies:
-        copy.start()
-    for copy in copies:
-        copy.wait()
-
-
-def near_kernel(plan, offset_ref, w_ref, own_ref, other_ref, *refs):
-    z_refs, (other_in, out_ref, weights_out, left_scr, outer_scr, staged, sems) = refs[:-7], refs[-7:]
+        copies.append(pltpu.make_async_copy(staged.at[u], out_ref.at[source], sems.at[step]))
+        copies[-1].start()
+    return copies
+
+
+def near_kernel(plan, offset_ref, w_ref, own_ref, other_ref, solo_ref, *refs):
+    z_refs, (other_in, staged, weights_out, offset, left_scr, outer_scr, sem) = refs[:-7], refs[-7:]
     chans, part, own, n_s = plan["chans"], plan["part"], plan["own"], plan["n_s"]
     n_right = part * plan["n_res"]
     half = LANES // 2
     pairs = chans // 2
     mine = pl.multiple_of(lax.axis_index("seq") * own, own)
+    fetch = pltpu.make_async_copy(offset_ref, offset, sem)
+    fetch.start()
 
     def rows_of(ref, at):
         return ref[pl.ds(at, own), :].astype(jnp.float32)
 
     start = pl.multiple_of(n_right + lax.axis_index("res") * part + mine, own)
-    rights = [(own_ref, 0), (other_ref, 0)]
+    rights = [(own_ref, 0), (other_ref, 0), (solo_ref, 0), (other_in, 0)]
     lefts = [rows_of(own_ref, start), rows_of(other_ref, start)]
-    for k, ref in enumerate(z_refs):
-        at = k * (n_right + own)
-        rights += [(ref, 0), (other_in, at)]
-        lefts += [rows_of(ref, pl.multiple_of(n_right + mine, own)), rows_of(other_in, at + n_right)]
+    lefts += [rows_of(solo_ref, pl.multiple_of(n_right + mine, own)), rows_of(other_in, n_right)]
+    at = n_right + own
+    for ref in z_refs:
+        rights += [(ref, 0), (ref, n_right), (other_in, at + n_right), (other_in, at)]
+        lefts += [rows_of(ref, pl.multiple_of(2 * n_right + h * part + mine, own)) for h in range(2)]
+        lefts += [rows_of(other_in, at + 2 * n_right + (1 - h) * own) for h in range(2)]
+        at += 2 * (n_right + own)
     fill_left(left_scr, 0, lefts, n_s)
     depth = left_scr.shape[1]
-    offset = offset_ref[...]
 
     def block_of_columns(block):
         at_block = block * pairs * n_s
@@ -214,43 +219,49 @@
             weights_out[pl.ds((block * pairs + pair) * depth, depth), :] = weights
             return weights
 
-        update_block(plan, block, 0, offset, w_ref, weight_of, left_scr, outer_scr, staged)
-
+        update_block(plan, block, offset, w_ref, weight_of, left_scr, outer_scr, staged)
+
+    fetch.wait()
     loop_blocks(n_right // (pairs * n_s), block_of_columns)
-    write_out(plan, 0, staged, out_ref, sems)
-
-
-def far_kernel(plan, offset_ref, w_ref, weights_ref, *refs):
-    x_refs, (other_in, _, out_ref, left_scr, outer_scr, staged, sems) = refs[:-7], refs[-7:]
+
+
+def far_kernel(plan, offset_ref, w_ref, weights_ref, near_ref, *refs):
+    x_refs, (other_in, out_ref, left_scr, outer_scr, staged, sems) = refs[:-6], refs[-6:]
     chans, part, own, n_s, n_res = plan["chans"], plan["part"], plan["own"], plan["n_s"], plan["n_res"]
     pairs = chans // 2
     me = lax.axis_index("seq")
+    copies = start_out(plan, 0, near_ref, out_ref, sems)
 
     def rows_of(ref, at):
         return ref[pl.ds(at, own), :].astype(jnp.float32)
 
-    n_pairs = len(plan["pairs"])
+    def pick(first, second):
+        return [jnp.where(me == 0, a, b) for a, b in zip(first, second)]
+
+    x_pairs = plan["x_pairs"]
     for u in range(plan["n_col"] - 1):
         chunks = [None] * n_res
-        for k, (first, second) in enumerate(plan["pairs"]):
-            place = u * n_pairs + k
+        for k, (first, second) in enumerate(x_pairs):
+            place = u * len(x_pairs) + k
             heard = [rows_of(x_refs[place], pl.multiple_of(h * part + me * own, own)) for h in range(2)]
             told = [rows_of(other_in, (2 * place + 1 - h) * own) for h in range(2)]
-            chunks[first] = [jnp.where(me == 0, a, b) for a, b in zip(heard, told)]
-            chunks[second] = [jnp.where(me == 0, b, a) for a, b in zip(heard, told)]
-        order = [0] + plan["z_steps"]
-        fill_left(left_scr, u, [slab for step in order for slab in chunks[step]], n_s)
+            chunks[first], chunks[second] = pick(heard, told), pick(told, heard)
+        order = chunks[0] + chunks[plan["solo"]]
+        for first, second in plan["z_pairs"]:
+            order += pick(chunks[first], chunks[second]) + pick(chunks[second], chunks[first])
+        fill_left(left_scr, u, order, n_s)
     depth = left_scr.shape[1]
-    offset = offset_ref[...]
 
     def block_of_columns(block):
         def weight_of(pair):
             return weights_ref[pl.ds((block * pairs + pair) * depth, depth), :]
 
-        update_block(plan, block, 1, offset, w_ref, weight_of, left_scr, outer_scr, staged)
+        update_block(plan, block, offset_ref, w_ref, weight_of, left_scr, outer_scr, staged)
 
     loop_blocks(weights_ref.shape[0] // (pairs * depth), block_of_columns)
-    write_out(plan, 1, staged, out_ref, sems)
+    copies += start_out(plan, 1, staged, out_ref, sems)
+    for copy in copies:
+        copy.wait()
 
 
 def per_device(alignment, scale, shift, w1, b1, w2, b2, w_final, offset):
@@ -268,15 +279,16 @@
     def rows(n):
         return jax.ShapeDtypeStruct((n, LANES), bf16)
 
-    z_steps = [k for k in range(1, n_res) if k > 1] + [1] * (n_res > 1)
-    pairs = [(k, k + 1) for k in range(1, n_res - 1, 2)] + [(0, n_res - 1)]
+    solo = n_res - 1
+    z_pairs = [(k, k + 1) for k in range(1, solo, 2)]
+    x_pairs = [(k, k + 1) for k in range(n_res - 2, -1, -2)]
 
     taken = (alignment, scale.reshape(1, -1), shift.reshape(1, -1), w1.T, b1.reshape(1, -1), w2.T, b2.reshape(1, -1))
-    slab, *z_out = pl.pallas_call(
-        functools.partial(project_kernel, n_res, z_steps),
-        out_shape=[rows(n_right + n_left)] + [rows(n_right + part)] * len(z_steps),
+    slab, solo_out = pl.pallas_call(
+        functools.partial(project_kernel, n_res, solo),
+        out_shape=[rows(n_right + n_left), rows(n_right + part)],
         in_specs=[HBM] * len(taken),
-        out_specs=[VMEM] * n_res,
+        out_specs=[VMEM] * 2,
         scratch_shapes=[pltpu.VMEM(a.shape, a.dtype) for a in taken]
         + [
             pltpu.VMEM((n_s * span, LANES), jnp.float32),
@@ -301,79 +313,82 @@
         return lax.ppermute(array, ("res", "col", "seq"), route)
 
     slab_in = to_core(slab)
-    z_in = [to_chip(array, 0, (step, step)) for array, step in zip(z_out, z_steps)]
-    sends = [(u, steps) for u in range(1, n_col) for steps in pairs]
+    solo_in = to_chip(solo_out, 0, (solo, solo))
+    sends = [(0, steps) for steps in z_pairs] + [(u, steps) for u in range(1, n_col) for steps in x_pairs]
     messages = pl.pallas_call(
         functools.partial(chip_kernel, n_res, [steps for _, steps in sends]),
-        out_shape=[rows(2 * part)] * len(sends),
+        out_shape=[rows(2 * part + (0 if u else 2 * n_right)) for u, _ in sends],
         in_specs=[VMEM] * 2,
         out_specs=[VMEM] * len(sends),
         compiler_params=params,
         name="chip",
     )(slab, slab_in)
-    x_in = [to_chip(message, u, steps) for message, (u, steps) in zip(messages, sends)]
-
+    heard = [to_chip(message, u, steps) for message, (u, steps) in zip(messages, sends)]
+
+    def pack(arrays, bodies, flops, after=()):
+        return pl.pallas_call(
+            functools.partial(core_kernel, bodies, part, own),
+            out_shape=rows(sum(b + (a.shape[0] - b) // part * own for a, b in zip(arrays, bodies))),
+            in_specs=[VMEM] * (len(arrays) + len(after)),
+            out_specs=VMEM,
+            compiler_params=params,
+            cost_estimate=pl.CostEstimate(flops=flops, bytes_accessed=0, transcendentals=0),
+            name="core",
+        )(*arrays, *after)
+
+    z_in, x_in = heard[: len(z_pairs)], heard[len(z_pairs) :]
+    arrays = [pack([solo_in], [n_right], 500_000_000)] + z_in
     weights = pl.pallas_call(
         weight_kernel,
         out_shape=jax.ShapeDtypeStruct((pair_width, chans * chans), bf16),
-        in_specs=[VMEM],
+        in_specs=[VMEM] * 2,
         out_specs=VMEM,
         scratch_shapes=[pltpu.VMEM((chans * chans, pair_width), jnp.float32)],
         compiler_params=params,
         name="weights",
-    )(w_final)
-
-    def share(arrays, n_rights, n_parts, cost):
-        packed = pl.pallas_call(
-            functools.partial(core_kernel, n_rights, part, own),
-            out_shape=rows(len(arrays) * (n_rights + n_parts * own)),
-            in_specs=[VMEM] * len(arrays),
-            out_specs=VMEM,
-            compiler_params=params,
-            cost_estimate=cost,
-            name="core",
-        )(*arrays)
-        return to_core(packed)
-
-    other_z = share(z_in, n_right, 1, None)
-    other_x = share(x_in, 0, 2, pl.CostEstimate(flops=20_000_000_000, bytes_accessed=0, transcendentals=0))
+    )(w_final, arrays[0])
+
+    other_z = to_core(pack(arrays, [n_right + own] + [2 * n_right] * len(z_in), 0))
+    other_x = to_core(pack(x_in, [0] * len(x_in), 20_000_000_000, (weights,)))
 
     turns = rows_dev * chans // LANES
     depth = turns * n_s * n_res * n_seq
-    total = float(n_s * n_res * n_seq)
-    plan = dict(
-        n_res=n_res, n_col=n_col, chans=chans, part=part, own=own, n_s=n_s, pairs=pairs, z_steps=z_steps, total=total
-    )
-    out_type = jax.ShapeDtypeStruct((n_col, rows_dev, span, pair_width), bf16)
+    plan = dict(n_res=n_res, n_col=n_col, chans=chans, part=part, own=own, n_s=n_s, total=float(n_s * n_res * n_seq))
+    plan.update(solo=solo, z_pairs=z_pairs, x_pairs=x_pairs)
     n_blocks = n_right // (chans // 2 * n_s)
 
     def scratch(n_u):
         return [
             pltpu.VMEM((n_u * LANES, depth), bf16),
             pltpu.VMEM((chans * chans, n_u * (LANES // chans) * LANES), bf16),
-            pltpu.VMEM((n_u, rows_dev, span, pair_width), bf16),
-            pltpu.SemaphoreType.DMA((n_u,)),
         ]
 
-    offset = offset.reshape(1, -1)
-    operands = (offset, weights, slab, slab_in, *z_in, other_z)
-    out, spread = pl.pallas_call(
+    def rows_type(n_u):
+        return jax.ShapeDtypeStruct((n_u, rows_dev, span, pair_width), bf16)
+
+    offset = pltpu.with_memory_space_constraint(offset.reshape(1, -1), pltpu.HBM)
+    operands = (offset, weights, slab, slab_in, solo_in, *z_in, other_z)
+    near, spread, offset = pl.pallas_call(
         functools.partial(near_kernel, plan),
-        out_shape=[out_type, jax.ShapeDtypeStruct((n_blocks * chans // 2 * depth, 2 * LANES), bf16)],
-        in_specs=[VMEM] * len(operands),
-        out_specs=[HBM, VMEM],
-        scratch_shapes=scratch(1),
+        out_shape=[
+            rows_type(1),
+            jax.ShapeDtypeStruct((n_blocks * chans // 2 * depth, 2 * LANES), bf16),
+            jax.ShapeDtypeStruct(offset.shape, offset.dtype),
+        ],
+        in_specs=[HBM] + [VMEM] * (len(operands) - 1),
+        out_specs=[VMEM] * 3,
+        scratch_shapes=scratch(1) + [pltpu.SemaphoreType.DMA(())],
         compiler_params=params,
         name="near",
     )(*operands)
-    operands = (offset, weights, spread, *x_in, other_x, out)
+    operands = (offset, weights, spread, near, *x_in, other_x)
     return pl.pallas_call(
         functools.partial(far_kernel, plan),
-        out_shape=out_type,
-        in_specs=[VMEM] * (len(operands) - 1) + [HBM],
+        out_shape=rows_type(n_col),
+        in_specs=[VMEM] * len(operands),
         out_specs=HBM,
-        scratch_shapes=scratch(n_col - 1),
-        input_output_aliases={len(operands) - 1: 0},
+        scratch_shapes=scratch(n_col - 1)
+        + [pltpu.VMEM((n_col - 1, rows_dev, span, pair_width), bf16), pltpu.SemaphoreType.DMA((n_col,))],
         compiler_params=params,
         name="far",
     )(*operands)

time: 20 us -> 17 us (0.85)
  starting transfers between devices: 11 us -> 8.52 us
  waiting for transfers between devices: 3.1 us -> 2.8 us
  local copies, waits for them, and re-layouts: 0.65 us -> 0.41 us
    ppermute x3, starting transfers between devices: 2.48 us -> 0.59 us  [to_core(): return lax.ppermute(array, 'seq', [(q, 1 - q) for q in range(n_seq)])]
    ppermute x5 -> x4, waiting for transfers between devices: 3.09 us -> 2.42 us  [to_chip(): return lax.ppermute(array, ('res', 'col', 'seq'), route)]
    ppermute x5 -> x4, starting transfers between devices: 8.5 us -> 7.92 us  [to_chip(): return lax.ppermute(array, ('res', 'col', 'seq'), route)]
    ppermute x3, waiting for transfers between devices: 0.01 us -> 0.38 us  [to_core(): return lax.ppermute(array, 'seq', [(q, 1 - q) for q in range(n_seq)])]
    unnamed x4 -> x2, local copies, waits for them, and re-layouts: 0.65 us -> 0.41 us
    pallas_call x5 -> x6, Pallas kernels: 4.68 us -> 4.63 us  [the longest x1 1.62 us: per_device(): pl.pallas_call(functools.partial(project_kernel, n_res, solo), out_shape=...]
  transfers between devices with their start and end apart: 8 -> 7, of which waited for: 3 -> 4; matrix products, arithmetic and copies ran while one was open for 0% -> 0% of each run, Pallas kernels for 10% -> 11%
where the time goes in v8:
time: 17 us; the launch traced here: 16.8 us
  starting transfers between devices  8.52 us (50%)
  Pallas kernels  5.04 us (30%)
  waiting for transfers between devices  2.8 us (16%)
  local copies, waits for them, and re-layouts  0.41 us (2%)
    ppermute x4, starting transfers between devices, to_chip(): return lax.ppermute(array, ('res', 'col', 'seq'), route)  7.92 us
    ppermute x4, waiting for transfers between devices, to_chip(): return lax.ppermute(array, ('res', 'col', 'seq'), route)  2.42 us
    pallas_call x1, Pallas kernels, per_device(): pl.pallas_call(functools.partial(project_kernel, n_res, solo), out_shape=...  1.62 us
    pallas_call x1, Pallas kernels, per_device(): pl.pallas_call(functools.partial(far_kernel, plan), out_shape=rows_type(n...  1.54 us
    pallas_call x1, Pallas kernels, per_device(): pl.pallas_call(functools.partial(near_kernel, plan), out_shape=[rows_type...  1.45 us
    ppermute x3, starting transfers between devices, to_core(): return lax.ppermute(array, 'seq', [(q, 1 - q) for q in range(n_seq)])  0.59 us
    unnamed x2, local copies, waits for them, and re-layouts  0.41 us
    pallas_call x1, Pallas kernels, per_device(): pl.pallas_call(weight_kernel, out_shape=jax.ShapeDtypeStruct((pair_width,...  0.4 us
  transfers between devices with their start and end apart: 7, of which 4 were waited for; matrix products, arithmetic and copies ran while one was open for 0% of the time, Pallas kernels for 11%

profile of v8, /device:TPU:0, one launch (start us, length us, event | category | flops | bytes accessed | tf_op | source)
XLA Modules:
  0.0 16.8 jit_solution(12178696449112151357)
XLA Ops:
  0.0 1.6 %project.1 = (bf16[256,128]{1,0:T(8,128)(2,1)S(1)}, bf16[160,128]{1,0:T(8,128)(2,1)S(1)}) custom-call(bf16[8,64,256]{2,1,0:T(8,128)(2,1)} %refs_0_.1, f32[1,256]{1,0:T(1,128)} %bitcast.9, f32[1,256]{1,0:T(1,128)} %bitcast.10, bf16[32,256]{1,0:T(8,128)(2,1)} %bitcast.7, f32[1,32]{1,0:T(1,128)} %bitcast.11, bf16[32,256]{1,0:T(8,128)(2,1)} %bitcast.8, ...), custom_call_target="tpu_custom_call" | custom-call | tf_op jit(solution)/shard_map/project/pallas_call | solution.py:287
  1.6 0.5 %collective-permute-start.1 = (bf16[256,128]{1,0:T(8,128)(2,1)S(1)}, bf16[256,128]{1,0:T(8,128)(2,1)S(1)}, u32[]{:S(2)}, u32[]{:S(2)}) collective-permute-start(bf16[256,128]{1,0:T(8,128)(2,1)S(1)} %get-tuple-element.14.own_ref), channel_id=1, source_target_pairs={{0,1},{1,0},{2,3},{3,2},{4,5},{5,4},{6,7},{7,6},{8,9},{9,8},{10,11... | collective-permute-start | bytes 196616 | tf_op jit(solution)/shard_map/ppermute | solution.py:304
  2.1 4.7 %collective-permute-start = (bf16[160,128]{1,0:T(8,128)(2,1)S(1)}, bf16[160,128]{1,0:T(8,128)(2,1)S(1)}, u32[]{:S(2)}, u32[]{:S(2)}) collective-permute-start(bf16[160,128]{1,0:T(8,128)(2,1)S(1)} %get-tuple-element.13), channel_id=1, source_target_pairs={{0,12},{1,13},{2,14},{3,15},{4,8},{5,9},{6,10},{7,11},{8,4},{9,5},... | collective-permute-start | bytes 122888 | tf_op jit(solution)/shard_map/ppermute | solution.py:313
  6.8 0.0 collective-permute-done.1.other_ref
  6.8 0.1 collective-permute-start.2
  6.9 2.6 %collective-permute-start.4 = (bf16[64,128]{1,0:T(8,128)(2,1)S(1)}, bf16[64,128]{1,0:T(8,128)(2,1)S(1)}, u32[]{:S(2)}, u32[]{:S(2)}) collective-permute-start(bf16[64,128]{1,0:T(8,128)(2,1)S(1)} %get-tuple-element.19), channel_id=1, source_target_pairs={{0,10},{1,15},{2,8},{3,13},{4,14},{5,11},{6,12},{7,9},{8,2},{9,7},... | collective-permute-start | bytes 49160 | tf_op jit(solution)/shard_map/ppermute | solution.py:313
  9.6 0.0 copy-start
  9.6 0.5 %collective-permute-start.5 = (bf16[64,128]{1,0:T(8,128)(2,1)S(1)}, bf16[64,128]{1,0:T(8,128)(2,1)S(1)}, u32[]{:S(2)}, u32[]{:S(2)}) collective-permute-start(bf16[64,128]{1,0:T(8,128)(2,1)S(1)} %get-tuple-element.20), channel_id=1, source_target_pairs={{0,2},{1,7},{2,0},{3,5},{4,6},{5,3},{6,4},{7,1},{8,10},{9,15},{10,... | collective-permute-start | bytes 49160 | tf_op jit(solution)/shard_map/ppermute | solution.py:313
  10.1 0.0 collective-permute-done.refs_0_.solo_ref
  10.1 0.4 %copy-done = bf16[1024,128]{1,0:T(8,128)(2,1)S(1)} copy-done((bf16[1024,128]{1,0:T(8,128)(2,1)S(1)}, bf16[1024,128]{1,0:T(8,128)(2,1)}, u32[]{:S(2)}) %copy-start) | copy-done | bytes 262168
  10.5 0.4 %weights.1.w_ref.refs_2_ = bf16[128,1024]{1,0:T(8,128)(2,1)S(1)} custom-call(bf16[1024,128]{1,0:T(8,128)(2,1)S(1)} %copy-done, bf16[144,128]{1,0:T(8,128)(2,1)S(1)} %core.3._.refs_0_), custom_call_target="tpu_custom_call" | custom-call | tf_op jit(solution)/shard_map/weights/pallas_call | solution.py:341
  10.9 1.5 %collective-permute-done.2.refs_1_.refs_0_ = bf16[320,128]{1,0:T(8,128)(2,1)S(1)} collective-permute-done((bf16[320,128]{1,0:T(8,128)(2,1)S(1)}, bf16[320,128]{1,0:T(8,128)(2,1)S(1)}, u32[]{:S(2)}, u32[]{:S(2)}) %collective-permute-start.2) | collective-permute-done | bytes 81952 | tf_op jit(solution)/shard_map/ppermute | solution.py:313
  12.4 0.1 collective-permute-start.3
  12.5 0.4 %collective-permute-done.4.refs_0_ = bf16[64,128]{1,0:T(8,128)(2,1)S(1)} collective-permute-done((bf16[64,128]{1,0:T(8,128)(2,1)S(1)}, bf16[64,128]{1,0:T(8,128)(2,1)S(1)}, u32[]{:S(2)}, u32[]{:S(2)}) %collective-permute-start.4) | collective-permute-done | bytes 16416 | tf_op jit(solution)/shard_map/ppermute | solution.py:313
  13.0 0.5 %collective-permute-done.5.refs_1_ = bf16[64,128]{1,0:T(8,128)(2,1)S(1)} collective-permute-done((bf16[64,128]{1,0:T(8,128)(2,1)S(1)}, bf16[64,128]{1,0:T(8,128)(2,1)S(1)}, u32[]{:S(2)}, u32[]{:S(2)}) %collective-permute-start.5) | collective-permute-done | bytes 16416 | tf_op jit(solution)/shard_map/ppermute | solution.py:313
  13.4 0.0 collective-permute-start.6
  13.4 0.4 %collective-permute-done.3.refs_1_ = bf16[432,128]{1,0:T(8,128)(2,1)S(1)} collective-permute-done((bf16[432,128]{1,0:T(8,128)(2,1)S(1)}, bf16[432,128]{1,0:T(8,128)(2,1)S(1)}, u32[]{:S(2)}, u32[]{:S(2)}) %collective-permute-start.3) | collective-permute-done | bytes 110624 | tf_op jit(solution)/shard_map/ppermute | solution.py:304
  13.8 1.5 %near.1 = (bf16[1,8,64,128]{3,2,1,0:T(8,128)(2,1)S(1)}, bf16[2048,256]{1,0:T(8,128)(2,1)S(1)}, f32[1,128]{1,0:T(1,128)S(1)}) custom-call(f32[1,128]{1,0:T(1,128)} %bitcast.13, bf16[128,1024]{1,0:T(8,128)(2,1)S(1)} %weights.1.w_ref.refs_2_, bf16[256,128]{1,0:T(8,128)(2,1)S(1)} %get-tuple-element.14.own_ref, ...), custom_call_target="tpu_custom_call" | custom-call | tf_op jit(solution)/shard_map/near/pallas_call | solution.py:371
  15.3 0.0 collective-permute-done.6.refs_2_
  15.3 1.5 %far.1 = bf16[2,8,64,128]{3,2,1,0:T(8,128)(2,1)} custom-call(f32[1,128]{1,0:T(1,128)S(1)} %get-tuple-element.16.offset_ref, bf16[128,1024]{1,0:T(8,128)(2,1)S(1)} %weights.1.w_ref.refs_2_, bf16[2048,256]{1,0:T(8,128)(2,1)S(1)} %get-tuple-element.17.weights_ref, bf16[1,8,64,128]{3,2,1,0:T(8,128)(2,1)S(1)} %get-tuple-element.18.near_ref, ...), custom_call_target="tpu_custom_call" | custom-call | tf_op jit(solution)/shard_map/far/pallas_call | solution.py:385
  (4 shorter events, 0.0 us)
Async XLA Ops:
  1.6 5.2 %collective-permute-start.1 = (bf16[256,128]{1,0:T(8,128)(2,1)S(1)}, bf16[256,128]{1,0:T(8,128)(2,1)S(1)}, u32[]{:S(2)}, u32[]{:S(2)}) collective-permute-start(bf16[256,128]{1,0:T(8,128)(2,1)S(1)} %get-tuple-element.14.own_ref), channel_id=1, source_target_pairs={{0,1},{1,0},{2,3},{3,2},{4,5},{5,4},{6,7},{7,6},{8,9},{9,8},{10,11... | collective-permute-start | bytes 196616 | tf_op jit(solution)/shard_map/ppermute | solution.py:304
  2.1 8.0 %collective-permute-start = (bf16[160,128]{1,0:T(8,128)(2,1)S(1)}, bf16[160,128]{1,0:T(8,128)(2,1)S(1)}, u32[]{:S(2)}, u32[]{:S(2)}) collective-permute-start(bf16[160,128]{1,0:T(8,128)(2,1)S(1)} %get-tuple-element.13), channel_id=1, source_target_pairs={{0,12},{1,13},{2,14},{3,15},{4,8},{5,9},{6,10},{7,11},{8,4},{9,5},... | collective-permute-start | bytes 122888 | tf_op jit(solution)/shard_map/ppermute | solution.py:313
  6.8 5.6 %collective-permute-start.2 = (bf16[320,128]{1,0:T(8,128)(2,1)S(1)}, bf16[320,128]{1,0:T(8,128)(2,1)S(1)}, u32[]{:S(2)}, u32[]{:S(2)}) collective-permute-start(bf16[320,128]{1,0:T(8,128)(2,1)S(1)} %get-tuple-element.15), channel_id=1, source_target_pairs={{0,4},{1,9},{2,6},{3,11},{4,0},{5,13},{6,2},{7,15},{8,12},{9,1},{1... | collective-permute-start | bytes 245768 | tf_op jit(solution)/shard_map/ppermute | solution.py:313
  6.9 6.0 %collective-permute-start.4 = (bf16[64,128]{1,0:T(8,128)(2,1)S(1)}, bf16[64,128]{1,0:T(8,128)(2,1)S(1)}, u32[]{:S(2)}, u32[]{:S(2)}) collective-permute-start(bf16[64,128]{1,0:T(8,128)(2,1)S(1)} %get-tuple-element.19), channel_id=1, source_target_pairs={{0,10},{1,15},{2,8},{3,13},{4,14},{5,11},{6,12},{7,9},{8,2},{9,7},... | collective-permute-start | bytes 49160 | tf_op jit(solution)/shard_map/ppermute | solution.py:313
  9.6 0.9 %copy-start = (bf16[1024,128]{1,0:T(8,128)(2,1)S(1)}, bf16[1024,128]{1,0:T(8,128)(2,1)}, u32[]{:S(2)}) copy-start(bf16[1024,128]{1,0:T(8,128)(2,1)} %w_ref.1) | copy-start | bytes 786436
  9.6 3.9 %collective-permute-start.5 = (bf16[64,128]{1,0:T(8,128)(2,1)S(1)}, bf16[64,128]{1,0:T(8,128)(2,1)S(1)}, u32[]{:S(2)}, u32[]{:S(2)}) collective-permute-start(bf16[64,128]{1,0:T(8,128)(2,1)S(1)} %get-tuple-element.20), channel_id=1, source_target_pairs={{0,2},{1,7},{2,0},{3,5},{4,6},{5,3},{6,4},{7,1},{8,10},{9,15},{10,... | collective-permute-start | bytes 49160 | tf_op jit(solution)/shard_map/ppermute | solution.py:313
  12.4 1.4 %collective-permute-start.3 = (bf16[432,128]{1,0:T(8,128)(2,1)S(1)}, bf16[432,128]{1,0:T(8,128)(2,1)S(1)}, u32[]{:S(2)}, u32[]{:S(2)}) collective-permute-start(bf16[432,128]{1,0:T(8,128)(2,1)S(1)} %core.4), channel_id=1, source_target_pairs={{0,1},{1,0},{2,3},{3,2},{4,5},{5,4},{6,7},{7,6},{8,9},{9,8},{10,11... | collective-permute-start | bytes 331784 | tf_op jit(solution)/shard_map/ppermute | solution.py:304
  13.4 1.8 %collective-permute-start.6 = (bf16[64,128]{1,0:T(8,128)(2,1)S(1)}, bf16[64,128]{1,0:T(8,128)(2,1)S(1)}, u32[]{:S(2)}, u32[]{:S(2)}) collective-permute-start(bf16[64,128]{1,0:T(8,128)(2,1)S(1)} %core.5), channel_id=1, source_target_pairs={{0,1},{1,0},{2,3},{3,2},{4,5},{5,4},{6,7},{7,6},{8,9},{9,8},{10,11... | collective-permute-start | bytes 49160 | tf_op jit(solution)/shard_map/ppermute | solution.py:304

commit v9 on v8

--- a/solution.py
+++ b/solution.py
@@ -107,9 +107,10 @@
             at += own
 
 
-def weight_kernel(w_ref, _, out_ref, scr):
+def weight_kernel(w_ref, offset_ref, _, out_ref, offset_out, scr):
     chans_sq, width = w_ref.shape
     chans = int(round(chans_sq**0.5))
+    offset_out[...] = offset_ref[...]
     scr[...] = w_ref[...].astype(jnp.float32)
     pairs = chans // 2
     fold = LANES // chans
@@ -175,15 +176,13 @@
     return copies
 
 
-def near_kernel(plan, offset_ref, w_ref, own_ref, other_ref, solo_ref, *refs):
-    z_refs, (other_in, staged, weights_out, offset, left_scr, outer_scr, sem) = refs[:-7], refs[-7:]
+def near_kernel(plan, offset, w_ref, own_ref, other_ref, solo_ref, *refs):
+    z_refs, (other_in, staged, weights_out, left_scr, outer_scr) = refs[:-5], refs[-5:]
     chans, part, own, n_s = plan["chans"], plan["part"], plan["own"], plan["n_s"]
     n_right = part * plan["n_res"]
     half = LANES // 2
     pairs = chans // 2
     mine = pl.multiple_of(lax.axis_index("seq") * own, own)
-    fetch = pltpu.make_async_copy(offset_ref, offset, sem)
-    fetch.start()
 
     def rows_of(ref, at):
         return ref[pl.ds(at, own), :].astype(jnp.float32)
@@ -221,7 +220,6 @@
 
         update_block(plan, block, offset, w_ref, weight_of, left_scr, outer_scr, staged)
 
-    fetch.wait()
     loop_blocks(n_right // (pairs * n_s), block_of_columns)
 
 
@@ -338,16 +336,19 @@
 
     z_in, x_in = heard[: len(z_pairs)], heard[len(z_pairs) :]
     arrays = [pack([solo_in], [n_right], 500_000_000)] + z_in
-    weights = pl.pallas_call(
+    offset = offset.reshape(1, -1)
+    weights, offset = pl.pallas_call(
         weight_kernel,
-        out_shape=jax.ShapeDtypeStruct((pair_width, chans * chans), bf16),
-        in_specs=[VMEM] * 2,
-        out_specs=VMEM,
+        out_shape=[
+            jax.ShapeDtypeStruct((pair_width, chans * chans), bf16),
+            jax.ShapeDtypeStruct(offset.shape, offset.dtype),
+        ],
+        in_specs=[VMEM] * 3,
+        out_specs=[VMEM] * 2,
         scratch_shapes=[pltpu.VMEM((chans * chans, pair_width), jnp.float32)],
         compiler_params=params,
         name="weights",
-    )(w_final, arrays[0])
-
+    )(w_final, offset, arrays[0])
     other_z = to_core(pack(arrays, [n_right + own] + [2 * n_right] * len(z_in), 0))
     other_x = to_core(pack(x_in, [0] * len(x_in), 20_000_000_000, (weights,)))
 
@@ -366,18 +367,16 @@
     def rows_type(n_u):
         return jax.ShapeDtypeStruct((n_u, rows_dev, span, pair_width), bf16)
 
-    offset = pltpu.with_memory_space_constraint(offset.reshape(1, -1), pltpu.HBM)
     operands = (offset, weights, slab, slab_in, solo_in, *z_in, other_z)
-    near, spread, offset = pl.pallas_call(
+    near, spread = pl.pallas_call(
         functools.partial(near_kernel, plan),
         out_shape=[
             rows_type(1),
             jax.ShapeDtypeStruct((n_blocks * chans // 2 * depth, 2 * LANES), bf16),
-            jax.ShapeDtypeStruct(offset.shape, offset.dtype),
         ],
-        in_specs=[HBM] + [VMEM] * (len(operands) - 1),
-        out_specs=[VMEM] * 3,
-        scratch_shapes=scratch(1) + [pltpu.SemaphoreType.DMA(())],
+        in_specs=[VMEM] * len(operands),
+        out_specs=[VMEM] * 2,
+        scratch_shapes=scratch(1),
         compiler_params=params,
         name="near",
     )(*operands)

time: 17 us -> 16.4 us (0.965)
  Pallas kernels: 5.04 us -> 4.42 us
  waiting for transfers between devices: 2.8 us -> 2.53 us
  local copies, waits for them, and re-layouts: 0.41 us -> 0.67 us
    pallas_call x1, Pallas kernels: 1.45 us -> 0.86 us  [per_device(): pl.pallas_call(functools.partial(near_kernel, plan), out_shape=[rows_type...]
    ppermute x4, waiting for transfers between devices: 2.42 us -> 2.15 us  [to_chip(): return lax.ppermute(array, ('res', 'col', 'seq'), route)]
    unnamed x2 -> x4, local copies, waits for them, and re-layouts: 0.41 us -> 0.67 us
  transfers between devices with their start and end apart: 7 -> 7, of which waited for: 4 -> 4; matrix products, arithmetic and copies ran while one was open for 0% -> 0% of each run, Pallas kernels for 11% -> 8%
where the time goes in v9:
time: 16.4 us; the launch traced here: 16.2 us
  starting transfers between devices  8.52 us (52%)
  Pallas kernels  4.42 us (27%)
  waiting for transfers between devices  2.53 us (15%)
  local copies, waits for them, and re-layouts  0.67 us (4%)
    ppermute x4, starting transfers between devices, to_chip(): return lax.ppermute(array, ('res', 'col', 'seq'), route)  7.92 us
    ppermute x4, waiting for transfers between devices, to_chip(): return lax.ppermute(array, ('res', 'col', 'seq'), route)  2.15 us
    pallas_call x1, Pallas kernels, per_device(): pl.pallas_call(functools.partial(project_kernel, n_res, solo), out_shape=...  1.62 us
    pallas_call x1, Pallas kernels, per_device(): pl.pallas_call(functools.partial(far_kernel, plan), out_shape=rows_type(n...  1.52 us
    pallas_call x1, Pallas kernels, per_device(): pl.pallas_call(functools.partial(near_kernel, plan), out_shape=[rows_type...  0.86 us
    unnamed x4, local copies, waits for them, and re-layouts  0.67 us
    ppermute x3, starting transfers between devices, to_core(): return lax.ppermute(array, 'seq', [(q, 1 - q) for q in range(n_seq)])  0.59 us
    pallas_call x1, Pallas kernels, per_device(): pl.pallas_call(weight_kernel, out_shape=[jax.ShapeDtypeStruct((pair_width...  0.4 us
  transfers between devices with their start and end apart: 7, of which 4 were waited for; matrix products, arithmetic and copies ran while one was open for 0% of the time, Pallas kernels for 8%

profile of v9, /device:TPU:0, one launch (start us, length us, event | category | flops | bytes accessed | tf_op | source)
XLA Modules:
  0.0 16.2 jit_solution(7128179589836499265)
XLA Ops:
  0.0 1.6 %project.1 = (bf16[256,128]{1,0:T(8,128)(2,1)S(1)}, bf16[160,128]{1,0:T(8,128)(2,1)S(1)}) custom-call(bf16[8,64,256]{2,1,0:T(8,128)(2,1)} %refs_0_.1, f32[1,256]{1,0:T(1,128)} %bitcast.10, f32[1,256]{1,0:T(1,128)} %bitcast.11, bf16[32,256]{1,0:T(8,128)(2,1)} %bitcast.8, f32[1,32]{1,0:T(1,128)} %bitcast.12, bf16[32,256]{1,0:T(8,128)(2,1)} %bitcast.9, ...), custom_call_target="tpu_custom_call" | custom-call | tf_op jit(solution)/shard_map/project/pallas_call | solution.py:285
  1.6 0.5 %collective-permute-start.1 = (bf16[256,128]{1,0:T(8,128)(2,1)S(1)}, bf16[256,128]{1,0:T(8,128)(2,1)S(1)}, u32[]{:S(2)}, u32[]{:S(2)}) collective-permute-start(bf16[256,128]{1,0:T(8,128)(2,1)S(1)} %get-tuple-element.17.own_ref), channel_id=1, source_target_pairs={{0,1},{1,0},{2,3},{3,2},{4,5},{5,4},{6,7},{7,6},{8,9},{9,8},{10,11... | collective-permute-start | bytes 196616 | tf_op jit(solution)/shard_map/ppermute | solution.py:302
  2.1 4.7 %collective-permute-start = (bf16[160,128]{1,0:T(8,128)(2,1)S(1)}, bf16[160,128]{1,0:T(8,128)(2,1)S(1)}, u32[]{:S(2)}, u32[]{:S(2)}) collective-permute-start(bf16[160,128]{1,0:T(8,128)(2,1)S(1)} %get-tuple-element.14), channel_id=1, source_target_pairs={{0,12},{1,13},{2,14},{3,15},{4,8},{5,9},{6,10},{7,11},{8,4},{9,5},... | collective-permute-start | bytes 122888 | tf_op jit(solution)/shard_map/ppermute | solution.py:311
  6.8 0.0 collective-permute-done.1.other_ref
  6.8 0.1 collective-permute-start.2
  6.9 2.6 %collective-permute-start.4 = (bf16[64,128]{1,0:T(8,128)(2,1)S(1)}, bf16[64,128]{1,0:T(8,128)(2,1)S(1)}, u32[]{:S(2)}, u32[]{:S(2)}) collective-permute-start(bf16[64,128]{1,0:T(8,128)(2,1)S(1)} %get-tuple-element.21), channel_id=1, source_target_pairs={{0,10},{1,15},{2,8},{3,13},{4,14},{5,11},{6,12},{7,9},{8,2},{9,7},... | collective-permute-start | bytes 49160 | tf_op jit(solution)/shard_map/ppermute | solution.py:311
  9.6 0.0 copy-start
  9.6 0.5 %collective-permute-start.5 = (bf16[64,128]{1,0:T(8,128)(2,1)S(1)}, bf16[64,128]{1,0:T(8,128)(2,1)S(1)}, u32[]{:S(2)}, u32[]{:S(2)}) collective-permute-start(bf16[64,128]{1,0:T(8,128)(2,1)S(1)} %get-tuple-element.22), channel_id=1, source_target_pairs={{0,2},{1,7},{2,0},{3,5},{4,6},{5,3},{6,4},{7,1},{8,10},{9,15},{10,... | collective-permute-start | bytes 49160 | tf_op jit(solution)/shard_map/ppermute | solution.py:311
  10.1 0.0 collective-permute-done.refs_0_.solo_ref
  10.1 0.0 copy-start.1
  10.1 0.4 %copy-done = bf16[1024,128]{1,0:T(8,128)(2,1)S(1)} copy-done((bf16[1024,128]{1,0:T(8,128)(2,1)S(1)}, bf16[1024,128]{1,0:T(8,128)(2,1)}, u32[]{:S(2)}) %copy-start) | copy-done | bytes 262168
  10.5 0.3 %copy-done.1 = f32[128]{0:T(128)S(1)} copy-done((f32[128]{0:T(128)S(1)}, f32[128]{0:T(128)}, u32[]{:S(2)}) %copy-start.1) | copy-done | bytes 536
  10.8 0.4 %weights.1 = (bf16[128,1024]{1,0:T(8,128)(2,1)S(1)}, f32[1,128]{1,0:T(1,128)S(1)}) custom-call(bf16[1024,128]{1,0:T(8,128)(2,1)S(1)} %copy-done, f32[1,128]{1,0:T(1,128)S(1)} %bitcast.7, bf16[144,128]{1,0:T(8,128)(2,1)S(1)} %core.3._.refs_0_), custom_call_target="tpu_custom_call" | custom-call | tf_op jit(solution)/shard_map/weights/pallas_call | solution.py:340
  11.2 1.2 %collective-permute-done.2.refs_1_.refs_0_ = bf16[320,128]{1,0:T(8,128)(2,1)S(1)} collective-permute-done((bf16[320,128]{1,0:T(8,128)(2,1)S(1)}, bf16[320,128]{1,0:T(8,128)(2,1)S(1)}, u32[]{:S(2)}, u32[]{:S(2)}) %collective-permute-start.2) | collective-permute-done | bytes 81952 | tf_op jit(solution)/shard_map/ppermute | solution.py:311
  12.4 0.1 collective-permute-start.3
  12.5 0.4 %collective-permute-done.4.refs_0_ = bf16[64,128]{1,0:T(8,128)(2,1)S(1)} collective-permute-done((bf16[64,128]{1,0:T(8,128)(2,1)S(1)}, bf16[64,128]{1,0:T(8,128)(2,1)S(1)}, u32[]{:S(2)}, u32[]{:S(2)}) %collective-permute-start.4) | collective-permute-done | bytes 16416 | tf_op jit(solution)/shard_map/ppermute | solution.py:311
  13.0 0.5 %collective-permute-done.5.refs_1_ = bf16[64,128]{1,0:T(8,128)(2,1)S(1)} collective-permute-done((bf16[64,128]{1,0:T(8,128)(2,1)S(1)}, bf16[64,128]{1,0:T(8,128)(2,1)S(1)}, u32[]{:S(2)}, u32[]{:S(2)}) %collective-permute-start.5) | collective-permute-done | bytes 16416 | tf_op jit(solution)/shard_map/ppermute | solution.py:311
  13.4 0.0 collective-permute-start.6
  13.4 0.4 %collective-permute-done.3.refs_1_ = bf16[432,128]{1,0:T(8,128)(2,1)S(1)} collective-permute-done((bf16[432,128]{1,0:T(8,128)(2,1)S(1)}, bf16[432,128]{1,0:T(8,128)(2,1)S(1)}, u32[]{:S(2)}, u32[]{:S(2)}) %collective-permute-start.3) | collective-permute-done | bytes 110624 | tf_op jit(solution)/shard_map/ppermute | solution.py:302
  13.8 0.9 %near.1 = (bf16[1,8,64,128]{3,2,1,0:T(8,128)(2,1)S(1)}, bf16[2048,256]{1,0:T(8,128)(2,1)S(1)}) custom-call(f32[1,128]{1,0:T(1,128)S(1)} %get-tuple-element.15.offset.offset_ref, bf16[128,1024]{1,0:T(8,128)(2,1)S(1)} %get-tuple-element.16.w_ref.refs_2_, bf16[256,128]{1,0:T(8,128)(2,1)S(1)} %get-tuple-element.17.own_ref, ...), custom_call_target="tpu_custom_call" | custom-call | tf_op jit(solution)/shard_map/near/pallas_call | solution.py:371
  14.7 0.0 collective-permute-done.6.refs_2_
  14.7 1.5 %far.1 = bf16[2,8,64,128]{3,2,1,0:T(8,128)(2,1)} custom-call(f32[1,128]{1,0:T(1,128)S(1)} %get-tuple-element.15.offset.offset_ref, bf16[128,1024]{1,0:T(8,128)(2,1)S(1)} %get-tuple-element.16.w_ref.refs_2_, bf16[2048,256]{1,0:T(8,128)(2,1)S(1)} %get-tuple-element.19.weights_ref, bf16[1,8,64,128]{3,2,1,0:T(8,128)(2,1)S(1)} %get-tuple-element.20.near_ref, ...), custom_call_target="tpu_custom_call" | custom-call | tf_op jit(solution)/shard_map/far/pallas_call | solution.py:384
  (4 shorter events, 0.0 us)
Async XLA Ops:
  1.6 5.2 %collective-permute-start.1 = (bf16[256,128]{1,0:T(8,128)(2,1)S(1)}, bf16[256,128]{1,0:T(8,128)(2,1)S(1)}, u32[]{:S(2)}, u32[]{:S(2)}) collective-permute-start(bf16[256,128]{1,0:T(8,128)(2,1)S(1)} %get-tuple-element.17.own_ref), channel_id=1, source_target_pairs={{0,1},{1,0},{2,3},{3,2},{4,5},{5,4},{6,7},{7,6},{8,9},{9,8},{10,11... | collective-permute-start | bytes 196616 | tf_op jit(solution)/shard_map/ppermute | solution.py:302
  2.1 8.0 %collective-permute-start = (bf16[160,128]{1,0:T(8,128)(2,1)S(1)}, bf16[160,128]{1,0:T(8,128)(2,1)S(1)}, u32[]{:S(2)}, u32[]{:S(2)}) collective-permute-start(bf16[160,128]{1,0:T(8,128)(2,1)S(1)} %get-tuple-element.14), channel_id=1, source_target_pairs={{0,12},{1,13},{2,14},{3,15},{4,8},{5,9},{6,10},{7,11},{8,4},{9,5},... | collective-permute-start | bytes 122888 | tf_op jit(solution)/shard_map/ppermute | solution.py:311
  6.8 5.6 %collective-permute-start.2 = (bf16[320,128]{1,0:T(8,128)(2,1)S(1)}, bf16[320,128]{1,0:T(8,128)(2,1)S(1)}, u32[]{:S(2)}, u32[]{:S(2)}) collective-permute-start(bf16[320,128]{1,0:T(8,128)(2,1)S(1)} %get-tuple-element.18), channel_id=1, source_target_pairs={{0,4},{1,9},{2,6},{3,11},{4,0},{5,13},{6,2},{7,15},{8,12},{9,1},{1... | collective-permute-start | bytes 245768 | tf_op jit(solution)/shard_map/ppermute | solution.py:311
  6.9 6.0 %collective-permute-start.4 = (bf16[64,128]{1,0:T(8,128)(2,1)S(1)}, bf16[64,128]{1,0:T(8,128)(2,1)S(1)}, u32[]{:S(2)}, u32[]{:S(2)}) collective-permute-start(bf16[64,128]{1,0:T(8,128)(2,1)S(1)} %get-tuple-element.21), channel_id=1, source_target_pairs={{0,10},{1,15},{2,8},{3,13},{4,14},{5,11},{6,12},{7,9},{8,2},{9,7},... | collective-permute-start | bytes 49160 | tf_op jit(solution)/shard_map/ppermute | solution.py:311
  9.6 0.9 %copy-start = (bf16[1024,128]{1,0:T(8,128)(2,1)S(1)}, bf16[1024,128]{1,0:T(8,128)(2,1)}, u32[]{:S(2)}) copy-start(bf16[1024,128]{1,0:T(8,128)(2,1)} %w_ref.1) | copy-start | bytes 786436
  9.6 3.9 %collective-permute-start.5 = (bf16[64,128]{1,0:T(8,128)(2,1)S(1)}, bf16[64,128]{1,0:T(8,128)(2,1)S(1)}, u32[]{:S(2)}, u32[]{:S(2)}) collective-permute-start(bf16[64,128]{1,0:T(8,128)(2,1)S(1)} %get-tuple-element.22), channel_id=1, source_target_pairs={{0,2},{1,7},{2,0},{3,5},{4,6},{5,3},{6,4},{7,1},{8,10},{9,15},{10,... | collective-permute-start | bytes 49160 | tf_op jit(solution)/shard_map/ppermute | solution.py:311
  10.1 0.7 %copy-start.1 = (f32[128]{0:T(128)S(1)}, f32[128]{0:T(128)}, u32[]{:S(2)}) copy-start(f32[128]{0:T(128)} %param.17) | copy-start | bytes 1540
  12.4 1.4 %collective-permute-start.3 = (bf16[432,128]{1,0:T(8,128)(2,1)S(1)}, bf16[432,128]{1,0:T(8,128)(2,1)S(1)}, u32[]{:S(2)}, u32[]{:S(2)}) collective-permute-start(bf16[432,128]{1,0:T(8,128)(2,1)S(1)} %core.4), channel_id=1, source_target_pairs={{0,1},{1,0},{2,3},{3,2},{4,5},{5,4},{6,7},{7,6},{8,9},{9,8},{10,11... | collective-permute-start | bytes 331784 | tf_op jit(solution)/shard_map/ppermute | solution.py:302
  13.4 1.2 %collective-permute-start.6 = (bf16[64,128]{1,0:T(8,128)(2,1)S(1)}, bf16[64,128]{1,0:T(8,128)(2,1)S(1)}, u32[]{:S(2)}, u32[]{:S(2)}) collective-permute-start(bf16[64,128]{1,0:T(8,128)(2,1)S(1)} %core.5), channel_id=1, source_target_pairs={{0,1},{1,0},{2,3},{3,2},{4,5},{5,4},{6,7},{7,6},{8,9},{9,8},{10,11... | collective-permute-start | bytes 49160 | tf_op jit(solution)/shard_map/ppermute | solution.py:302

commit v10 on v9

--- a/solution.py
+++ b/solution.py
@@ -277,8 +277,9 @@
     def rows(n):
         return jax.ShapeDtypeStruct((n, LANES), bf16)
 
-    solo = n_res - 1
-    z_pairs = [(k, k + 1) for k in range(1, solo, 2)]
+    solo = n_res // 2
+    others = [k for k in range(n_res - 1, 0, -1) if k != solo]
+    z_pairs = list(zip(others[::2], others[1::2]))
     x_pairs = [(k, k + 1) for k in range(n_res - 2, -1, -2)]
 
     taken = (alignment, scale.reshape(1, -1), shift.reshape(1, -1), w1.T, b1.reshape(1, -1), w2.T, b2.reshape(1, -1))

time: 16.4 us -> 16.7 us (1.018)
  starting transfers between devices: 8.52 us -> 8.82 us
    ppermute x4, starting transfers between devices: 7.92 us -> 8.23 us  [to_chip(): return lax.ppermute(array, ('res', 'col', 'seq'), route)]
  transfers between devices with their start and end apart: 7 -> 7, of which waited for: 4 -> 3; matrix products, arithmetic and copies ran while one was open for 0% -> 0% of each run, Pallas kernels for 8% -> 8%
where the time goes in v10:
time: 16.7 us; the launch traced here: 16.6 us
  starting transfers between devices  8.82 us (53%)
  Pallas kernels  4.43 us (27%)
  waiting for transfers between devices  2.59 us (16%)
  local copies, waits for them, and re-layouts  0.67 us (4%)
    ppermute x4, starting transfers between devices, to_chip(): return lax.ppermute(array, ('res', 'col', 'seq'), route)  8.23 us
    ppermute x4, waiting for transfers between devices, to_chip(): return lax.ppermute(array, ('res', 'col', 'seq'), route)  2.28 us
    pallas_call x1, Pallas kernels, per_device(): pl.pallas_call(functools.partial(project_kernel, n_res, solo), out_shape=...  1.62 us
    pallas_call x1, Pallas kernels, per_device(): pl.pallas_call(functools.partial(far_kernel, plan), out_shape=rows_type(n...  1.52 us
    pallas_call x1, Pallas kernels, per_device(): pl.pallas_call(functools.partial(near_kernel, plan), out_shape=[rows_type...  0.86 us
    unnamed x4, local copies, waits for them, and re-layouts  0.67 us
    ppermute x3, starting transfers between devices, to_core(): return lax.ppermute(array, 'seq', [(q, 1 - q) for q in range(n_seq)])  0.59 us
    pallas_call x1, Pallas kernels, per_device(): pl.pallas_call(weight_kernel, out_shape=[jax.ShapeDtypeStruct((pair_width...  0.4 us
  transfers between devices with their start and end apart: 7, of which 3 were waited for; matrix products, arithmetic and copies ran while one was open for 0% of the time, Pallas kernels for 8%

profile of v10, /device:TPU:0, one launch (start us, length us, event | category | flops | bytes accessed | tf_op | source)
XLA Modules:
  0.0 16.6 jit_solution(2684318366668504936)
XLA Ops:
  0.0 1.6 %project.1 = (bf16[256,128]{1,0:T(8,128)(2,1)S(1)}, bf16[160,128]{1,0:T(8,128)(2,1)S(1)}) custom-call(bf16[8,64,256]{2,1,0:T(8,128)(2,1)} %refs_0_.1, f32[1,256]{1,0:T(1,128)} %bitcast.10, f32[1,256]{1,0:T(1,128)} %bitcast.11, bf16[32,256]{1,0:T(8,128)(2,1)} %bitcast.8, f32[1,32]{1,0:T(1,128)} %bitcast.12, bf16[32,256]{1,0:T(8,128)(2,1)} %bitcast.9, ...), custom_call_target="tpu_custom_call" | custom-call | tf_op jit(solution)/shard_map/project/pallas_call | solution.py:286
  1.6 0.5 %collective-permute-start.1 = (bf16[256,128]{1,0:T(8,128)(2,1)S(1)}, bf16[256,128]{1,0:T(8,128)(2,1)S(1)}, u32[]{:S(2)}, u32[]{:S(2)}) collective-permute-start(bf16[256,128]{1,0:T(8,128)(2,1)S(1)} %get-tuple-element.17.own_ref), channel_id=1, source_target_pairs={{0,1},{1,0},{2,3},{3,2},{4,5},{5,4},{6,7},{7,6},{8,9},{9,8},{10,11... | collective-permute-start | bytes 196616 | tf_op jit(solution)/shard_map/ppermute | solution.py:303
  2.1 3.7 %collective-permute-start = (bf16[160,128]{1,0:T(8,128)(2,1)S(1)}, bf16[160,128]{1,0:T(8,128)(2,1)S(1)}, u32[]{:S(2)}, u32[]{:S(2)}) collective-permute-start(bf16[160,128]{1,0:T(8,128)(2,1)S(1)} %get-tuple-element.14), channel_id=1, source_target_pairs={{0,8},{1,9},{2,10},{3,11},{4,12},{5,13},{6,14},{7,15},{8,0},{9,1},... | collective-permute-start | bytes 122888 | tf_op jit(solution)/shard_map/ppermute | solution.py:312
  5.8 0.0 collective-permute-done.1.other_ref
  5.8 2.2 %collective-permute-start.2 = (bf16[320,128]{1,0:T(8,128)(2,1)S(1)}, bf16[320,128]{1,0:T(8,128)(2,1)S(1)}, u32[]{:S(2)}, u32[]{:S(2)}) collective-permute-start(bf16[320,128]{1,0:T(8,128)(2,1)S(1)} %get-tuple-element.18), channel_id=1, source_target_pairs={{0,12},{1,5},{2,14},{3,7},{4,8},{5,1},{6,10},{7,3},{8,4},{9,13},{1... | collective-permute-start | bytes 245768 | tf_op jit(solution)/shard_map/ppermute | solution.py:312
  8.1 1.8 %collective-permute-start.4 = (bf16[64,128]{1,0:T(8,128)(2,1)S(1)}, bf16[64,128]{1,0:T(8,128)(2,1)S(1)}, u32[]{:S(2)}, u32[]{:S(2)}) collective-permute-start(bf16[64,128]{1,0:T(8,128)(2,1)S(1)} %get-tuple-element.21), channel_id=1, source_target_pairs={{0,10},{1,15},{2,8},{3,13},{4,14},{5,11},{6,12},{7,9},{8,2},{9,7},... | collective-permute-start | bytes 49160 | tf_op jit(solution)/shard_map/ppermute | solution.py:312
  9.9 0.0 copy-start
  9.9 0.5 %collective-permute-start.5 = (bf16[64,128]{1,0:T(8,128)(2,1)S(1)}, bf16[64,128]{1,0:T(8,128)(2,1)S(1)}, u32[]{:S(2)}, u32[]{:S(2)}) collective-permute-start(bf16[64,128]{1,0:T(8,128)(2,1)S(1)} %get-tuple-element.22), channel_id=1, source_target_pairs={{0,2},{1,7},{2,0},{3,5},{4,6},{5,3},{6,4},{7,1},{8,10},{9,15},{10,... | collective-permute-start | bytes 49160 | tf_op jit(solution)/shard_map/ppermute | solution.py:312
  10.4 0.0 collective-permute-done.refs_0_.solo_ref
  10.4 0.0 copy-start.1
  10.4 0.4 %copy-done = bf16[1024,128]{1,0:T(8,128)(2,1)S(1)} copy-done((bf16[1024,128]{1,0:T(8,128)(2,1)S(1)}, bf16[1024,128]{1,0:T(8,128)(2,1)}, u32[]{:S(2)}) %copy-start) | copy-done | bytes 262168
  10.8 0.3 %copy-done.1 = f32[128]{0:T(128)S(1)} copy-done((f32[128]{0:T(128)S(1)}, f32[128]{0:T(128)}, u32[]{:S(2)}) %copy-start.1) | copy-done | bytes 536
  11.1 0.4 %weights.1 = (bf16[128,1024]{1,0:T(8,128)(2,1)S(1)}, f32[1,128]{1,0:T(1,128)S(1)}) custom-call(bf16[1024,128]{1,0:T(8,128)(2,1)S(1)} %copy-done, f32[1,128]{1,0:T(1,128)S(1)} %bitcast.7, bf16[144,128]{1,0:T(8,128)(2,1)S(1)} %core.3._.refs_0_), custom_call_target="tpu_custom_call" | custom-call | tf_op jit(solution)/shard_map/weights/pallas_call | solution.py:341
  11.5 0.8 %collective-permute-done.2.refs_1_.refs_0_ = bf16[320,128]{1,0:T(8,128)(2,1)S(1)} collective-permute-done((bf16[320,128]{1,0:T(8,128)(2,1)S(1)}, bf16[320,128]{1,0:T(8,128)(2,1)S(1)}, u32[]{:S(2)}, u32[]{:S(2)}) %collective-permute-start.2) | collective-permute-done | bytes 81952 | tf_op jit(solution)/shard_map/ppermute | solution.py:312
  12.3 0.1 collective-permute-start.3
  12.4 1.4 %collective-permute-done.4.refs_0_ = bf16[64,128]{1,0:T(8,128)(2,1)S(1)} collective-permute-done((bf16[64,128]{1,0:T(8,128)(2,1)S(1)}, bf16[64,128]{1,0:T(8,128)(2,1)S(1)}, u32[]{:S(2)}, u32[]{:S(2)}) %collective-permute-start.4) | collective-permute-done | bytes 16416 | tf_op jit(solution)/shard_map/ppermute | solution.py:312
  13.8 0.0 collective-permute-done.5.refs_1_
  13.9 0.0 collective-permute-start.6
  13.9 0.0 collective-permute-done.3.refs_1_
  13.9 0.9 %near.1 = (bf16[1,8,64,128]{3,2,1,0:T(8,128)(2,1)S(1)}, bf16[2048,256]{1,0:T(8,128)(2,1)S(1)}) custom-call(f32[1,128]{1,0:T(1,128)S(1)} %get-tuple-element.15.offset.offset_ref, bf16[128,1024]{1,0:T(8,128)(2,1)S(1)} %get-tuple-element.16.w_ref.refs_2_, bf16[256,128]{1,0:T(8,128)(2,1)S(1)} %get-tuple-element.17.own_ref, ...), custom_call_target="tpu_custom_call" | custom-call | tf_op jit(solution)/shard_map/near/pallas_call | solution.py:372
  14.7 0.3 %collective-permute-done.6.refs_2_ = bf16[64,128]{1,0:T(8,128)(2,1)S(1)} collective-permute-done((bf16[64,128]{1,0:T(8,128)(2,1)S(1)}, bf16[64,128]{1,0:T(8,128)(2,1)S(1)}, u32[]{:S(2)}, u32[]{:S(2)}) %collective-permute-start.6) | collective-permute-done | bytes 16416 | tf_op jit(solution)/shard_map/ppermute | solution.py:303
  15.0 1.5 %far.1 = bf16[2,8,64,128]{3,2,1,0:T(8,128)(2,1)} custom-call(f32[1,128]{1,0:T(1,128)S(1)} %get-tuple-element.15.offset.offset_ref, bf16[128,1024]{1,0:T(8,128)(2,1)S(1)} %get-tuple-element.16.w_ref.refs_2_, bf16[2048,256]{1,0:T(8,128)(2,1)S(1)} %get-tuple-element.19.weights_ref, bf16[1,8,64,128]{3,2,1,0:T(8,128)(2,1)S(1)} %get-tuple-element.20.near_ref, ...), custom_call_target="tpu_custom_call" | custom-call | tf_op jit(solution)/shard_map/far/pallas_call | solution.py:385
  (4 shorter events, 0.0 us)
Async XLA Ops:
  1.6 4.2 %collective-permute-start.1 = (bf16[256,128]{1,0:T(8,128)(2,1)S(1)}, bf16[256,128]{1,0:T(8,128)(2,1)S(1)}, u32[]{:S(2)}, u32[]{:S(2)}) collective-permute-start(bf16[256,128]{1,0:T(8,128)(2,1)S(1)} %get-tuple-element.17.own_ref), channel_id=1, source_target_pairs={{0,1},{1,0},{2,3},{3,2},{4,5},{5,4},{6,7},{7,6},{8,9},{9,8},{10,11... | collective-permute-start | bytes 196616 | tf_op jit(solution)/shard_map/ppermute | solution.py:303
  2.1 8.3 %collective-permute-start = (bf16[160,128]{1,0:T(8,128)(2,1)S(1)}, bf16[160,128]{1,0:T(8,128)(2,1)S(1)}, u32[]{:S(2)}, u32[]{:S(2)}) collective-permute-start(bf16[160,128]{1,0:T(8,128)(2,1)S(1)} %get-tuple-element.14), channel_id=1, source_target_pairs={{0,8},{1,9},{2,10},{3,11},{4,12},{5,13},{6,14},{7,15},{8,0},{9,1},... | collective-permute-start | bytes 122888 | tf_op jit(solution)/shard_map/ppermute | solution.py:312
  5.8 6.5 %collective-permute-start.2 = (bf16[320,128]{1,0:T(8,128)(2,1)S(1)}, bf16[320,128]{1,0:T(8,128)(2,1)S(1)}, u32[]{:S(2)}, u32[]{:S(2)}) collective-permute-start(bf16[320,128]{1,0:T(8,128)(2,1)S(1)} %get-tuple-element.18), channel_id=1, source_target_pairs={{0,12},{1,5},{2,14},{3,7},{4,8},{5,1},{6,10},{7,3},{8,4},{9,13},{1... | collective-permute-start | bytes 245768 | tf_op jit(solution)/shard_map/ppermute | solution.py:312
  8.1 5.7 %collective-permute-start.4 = (bf16[64,128]{1,0:T(8,128)(2,1)S(1)}, bf16[64,128]{1,0:T(8,128)(2,1)S(1)}, u32[]{:S(2)}, u32[]{:S(2)}) collective-permute-start(bf16[64,128]{1,0:T(8,128)(2,1)S(1)} %get-tuple-element.21), channel_id=1, source_target_pairs={{0,10},{1,15},{2,8},{3,13},{4,14},{5,11},{6,12},{7,9},{8,2},{9,7},... | collective-permute-start | bytes 49160 | tf_op jit(solution)/shard_map/ppermute | solution.py:312
  9.9 0.9 %copy-start = (bf16[1024,128]{1,0:T(8,128)(2,1)S(1)}, bf16[1024,128]{1,0:T(8,128)(2,1)}, u32[]{:S(2)}) copy-start(bf16[1024,128]{1,0:T(8,128)(2,1)} %w_ref.1) | copy-start | bytes 786436
  9.9 4.0 %collective-permute-start.5 = (bf16[64,128]{1,0:T(8,128)(2,1)S(1)}, bf16[64,128]{1,0:T(8,128)(2,1)S(1)}, u32[]{:S(2)}, u32[]{:S(2)}) collective-permute-start(bf16[64,128]{1,0:T(8,128)(2,1)S(1)} %get-tuple-element.22), channel_id=1, source_target_pairs={{0,2},{1,7},{2,0},{3,5},{4,6},{5,3},{6,4},{7,1},{8,10},{9,15},{10,... | collective-permute-start | bytes 49160 | tf_op jit(solution)/shard_map/ppermute | solution.py:312
  10.4 0.7 %copy-start.1 = (f32[128]{0:T(128)S(1)}, f32[128]{0:T(128)}, u32[]{:S(2)}) copy-start(f32[128]{0:T(128)} %param.17) | copy-start | bytes 1540
  12.3 1.5 %collective-permute-start.3 = (bf16[432,128]{1,0:T(8,128)(2,1)S(1)}, bf16[432,128]{1,0:T(8,128)(2,1)S(1)}, u32[]{:S(2)}, u32[]{:S(2)}) collective-permute-start(bf16[432,128]{1,0:T(8,128)(2,1)S(1)} %core.4), channel_id=1, source_target_pairs={{0,1},{1,0},{2,3},{3,2},{4,5},{5,4},{6,7},{7,6},{8,9},{9,8},{10,11... | collective-permute-start | bytes 331784 | tf_op jit(solution)/shard_map/ppermute | solution.py:303
  13.9 1.2 %collective-permute-start.6 = (bf16[64,128]{1,0:T(8,128)(2,1)S(1)}, bf16[64,128]{1,0:T(8,128)(2,1)S(1)}, u32[]{:S(2)}, u32[]{:S(2)}) collective-permute-start(bf16[64,128]{1,0:T(8,128)(2,1)S(1)} %core.5), channel_id=1, source_target_pairs={{0,1},{1,0},{2,3},{3,2},{4,5},{5,4},{6,7},{7,6},{8,9},{9,8},{10,11... | collective-permute-start | bytes 49160 | tf_op jit(solution)/shard_map/ppermute | solution.py:303

commit v11 on v9

--- a/solution.py
+++ b/solution.py
@@ -1,4 +1,5 @@
 import functools
+import math
 
 import jax
 import jax.numpy as jnp
@@ -23,13 +24,16 @@
 
 
 def project_kernel(n_res, solo, *refs):
-    n_in = 7
-    sources, (slab_out, solo_out), scratch = refs[:n_in], refs[n_in : -n_in - 4], refs[-n_in - 4 :]
-    landed, (rows_scr, lane_scr, right_scr, sems) = scratch[:n_in], scratch[n_in:]
-    copies = [pltpu.make_async_copy(a, b, sems.at[i]) for i, (a, b) in enumerate(zip(sources, landed))]
+    n_in, n_later = 7, 2
+    sources, refs = refs[: n_in + n_later], refs[n_in + n_later :]
+    (slab_out, solo_out), later = refs[:2], refs[2 : 2 + n_later]
+    landed, (rows_scr, lane_scr, right_scr, sems) = refs[2 + n_later : -4], refs[-4:]
+    copies = [
+        pltpu.make_async_copy(a, b, sems.at[i]) for i, (a, b) in enumerate(zip(sources, (*landed, *later)))
+    ]
     for copy in copies:
         copy.start()
-    for copy in copies:
+    for copy in copies[:n_in]:
         copy.wait()
     x_ref, scale_ref, shift_ref, w1_ref, b1_ref, w2_ref, b2_ref = landed
     n_s, span, width = x_ref.shape
@@ -77,6 +81,8 @@
     to = partner(lax.axis_index("res"), solo, n_res)
     solo_out[:n_right] = right_slab
     solo_out[n_right:] = lane_scr[pl.ds(pl.multiple_of(to * part, part), part), :].astype(jnp.bfloat16)
+    for copy in copies[n_in:]:
+        copy.wait()
 
 
 def chip_kernel(n_res, steps, own_ref, other_ref, *outs):
@@ -107,10 +113,9 @@
             at += own
 
 
-def weight_kernel(w_ref, offset_ref, _, out_ref, offset_out, scr):
+def weight_kernel(w_ref, _, out_ref, scr):
     chans_sq, width = w_ref.shape
     chans = int(round(chans_sq**0.5))
-    offset_out[...] = offset_ref[...]
     scr[...] = w_ref[...].astype(jnp.float32)
     pairs = chans // 2
     fold = LANES // chans
@@ -137,7 +142,7 @@
         pl.loop(0, n_blocks)(body)
 
 
-def update_block(plan, block, offset, w_ref, weight_of, left_scr, outer_scr, staged):
+def update_block(plan, block, offset, w_ref, weight_of, left_scr, outer_scr, staged, finish=None):
     chans, total = plan["chans"], plan["total"]
     half = LANES // 2
     fold = LANES // chans
@@ -151,29 +156,33 @@
                 outer_scr[at : at + chans, tile * LANES : (tile + 1) * LANES] = outer[
                     tile * chans : (tile + 1) * chans, side * LANES : (side + 1) * LANES
                 ]
+    inverse = 1.0 / total if math.frexp(total)[0] == 0.5 else None
+    step = min(fold, 2)
     for u in range(n_u):
-        summed = jnp.dot(
-            w_ref[...], outer_scr[:, u * fold * LANES : (u + 1) * fold * LANES], preferred_element_type=jnp.float32
-        )
-        for residue in range(fold):
-            piece = summed[:, residue * LANES : (residue + 1) * LANES].T
-            piece = (piece / total + offset[...]).astype(jnp.bfloat16)
-            for turn in range(LANES // half):
-                staged[u, turn * fold + residue, pl.ds(block * half, half), :] = piece[
-                    turn * half : (turn + 1) * half
-                ]
-
-
-def start_out(plan, u_base, staged, out_ref, sems):
+        for first in range(0, fold, step):
+            at = (u * fold + first) * LANES
+            summed = jnp.dot(
+                w_ref[...], outer_scr[:, at : at + step * LANES], preferred_element_type=jnp.float32
+            )
+            for k in range(step):
+                piece = summed[:, k * LANES : (k + 1) * LANES].T
+                piece = piece / total if inverse is None else piece * inverse
+                piece = (piece + offset[...]).astype(jnp.bfloat16)
+                for turn in range(LANES // half):
+                    staged[u, turn * fold + first + k, pl.ds(block * half, half), :] = piece[
+                        turn * half : (turn + 1) * half
+                    ]
+            if finish is not None:
+                for turn in range(LANES // half):
+                    finish(u, turn * fold + first, step)
+
+
+def row_copy(plan, step, staged, out_ref, sem):
     n_col = plan["n_col"]
     col = lax.axis_index("col")
-    copies = []
-    for u in range(staged.shape[0]):
-        step = u_base + u
-        source = partner(col, step, n_col) if n_col & (n_col - 1) == 0 else (col - step + n_col) % n_col
-        copies.append(pltpu.make_async_copy(staged.at[u], out_ref.at[source], sems.at[step]))
-        copies[-1].start()
-    return copies
+    source = partner(col, step, n_col) if n_col & (n_col - 1) == 0 else (col - step + n_col) % n_col
+    row, rows = staged[1]
+    return pltpu.make_async_copy(staged[0].at[pl.ds(row, rows)], out_ref.at[source, pl.ds(row, rows)], sem)
 
 
 def near_kernel(plan, offset, w_ref, own_ref, other_ref, solo_ref, *refs):
@@ -228,7 +237,9 @@
     chans, part, own, n_s, n_res = plan["chans"], plan["part"], plan["own"], plan["n_s"], plan["n_res"]
     pairs = chans // 2
     me = lax.axis_index("seq")
-    copies = start_out(plan, 0, near_ref, out_ref, sems)
+    rows_dev = near_ref.shape[1]
+    copies = [row_copy(plan, 0, (near_ref.at[0], (0, rows_dev)), out_ref, sems.at[0, 0])]
+    copies[0].start()
 
     def rows_of(ref, at):
         return ref[pl.ds(at, own), :].astype(jnp.float32)
@@ -254,10 +265,19 @@
         def weight_of(pair):
             return weights_ref[pl.ds((block * pairs + pair) * depth, depth), :]
 
-        update_block(plan, block, offset_ref, w_ref, weight_of, left_scr, outer_scr, staged)
-
-    loop_blocks(weights_ref.shape[0] // (pairs * depth), block_of_columns)
-    copies += start_out(plan, 1, staged, out_ref, sems)
+        update_block(
+            plan, block, offset_ref, w_ref, weight_of, left_scr, outer_scr, staged, finish if n_blocks == 1 else None
+        )
+
+    def finish(u, row, rows):
+        copies.append(row_copy(plan, 1 + u, (staged.at[u], (row, rows)), out_ref, sems.at[1 + u, row]))
+        copies[-1].start()
+
+    n_blocks = weights_ref.shape[0] // (pairs * depth)
+    loop_blocks(n_blocks, block_of_columns)
+    if n_blocks > 1:
+        for u in range(staged.shape[0]):
+            finish(u, 0, rows_dev)
     for copy in copies:
         copy.wait()
 
@@ -277,26 +297,28 @@
     def rows(n):
         return jax.ShapeDtypeStruct((n, LANES), bf16)
 
-    solo = n_res - 1
-    z_pairs = [(k, k + 1) for k in range(1, solo, 2)]
+    solo = 1
+    z_pairs = [(k, k + 1) for k in range(2, n_res, 2)]
     x_pairs = [(k, k + 1) for k in range(n_res - 2, -1, -2)]
 
     taken = (alignment, scale.reshape(1, -1), shift.reshape(1, -1), w1.T, b1.reshape(1, -1), w2.T, b2.reshape(1, -1))
-    slab, solo_out = pl.pallas_call(
+    later = (w_final, offset.reshape(1, -1))
+    slab, solo_out, w_final, offset = pl.pallas_call(
         functools.partial(project_kernel, n_res, solo),
-        out_shape=[rows(n_right + n_left), rows(n_right + part)],
-        in_specs=[HBM] * len(taken),
-        out_specs=[VMEM] * 2,
+        out_shape=[rows(n_right + n_left), rows(n_right + part)]
+        + [jax.ShapeDtypeStruct(a.shape, a.dtype) for a in later],
+        in_specs=[HBM] * len(taken + later),
+        out_specs=[VMEM] * 4,
         scratch_shapes=[pltpu.VMEM(a.shape, a.dtype) for a in taken]
         + [
             pltpu.VMEM((n_s * span, LANES), jnp.float32),
             pltpu.VMEM((n_left, LANES), jnp.float32),
             pltpu.VMEM((n_right, LANES), jnp.float32),
-            pltpu.SemaphoreType.DMA((len(taken),)),
+            pltpu.SemaphoreType.DMA((len(taken + later),)),
         ],
         compiler_params=params,
         name="project",
-    )(*[pltpu.with_memory_space_constraint(a, pltpu.HBM) for a in taken])
+    )(*[pltpu.with_memory_space_constraint(a, pltpu.HBM) for a in taken + later])
 
     def to_core(array):
         return lax.ppermute(array, "seq", [(q, 1 - q) for q in range(n_seq)])
@@ -336,19 +358,15 @@
 
     z_in, x_in = heard[: len(z_pairs)], heard[len(z_pairs) :]
     arrays = [pack([solo_in], [n_right], 500_000_000)] + z_in
-    offset = offset.reshape(1, -1)
-    weights, offset = pl.pallas_call(
+    weights = pl.pallas_call(
         weight_kernel,
-        out_shape=[
-            jax.ShapeDtypeStruct((pair_width, chans * chans), bf16),
-            jax.ShapeDtypeStruct(offset.shape, offset.dtype),
-        ],
-        in_specs=[VMEM] * 3,
-        out_specs=[VMEM] * 2,
+        out_shape=jax.ShapeDtypeStruct((pair_width, chans * chans), bf16),
+        in_specs=[VMEM] * 2,
+        out_specs=VMEM,
         scratch_shapes=[pltpu.VMEM((chans * chans, pair_width), jnp.float32)],
         compiler_params=params,
         name="weights",
-    )(w_final, offset, arrays[0])
+    )(w_final, arrays[0])
     other_z = to_core(pack(arrays, [n_right + own] + [2 * n_right] * len(z_in), 0))
     other_x = to_core(pack(x_in, [0] * len(x_in), 20_000_000_000, (weights,)))
 
@@ -387,7 +405,7 @@
         in_specs=[VMEM] * len(operands),
         out_specs=HBM,
         scratch_shapes=scratch(n_col - 1)
-        + [pltpu.VMEM((n_col - 1, rows_dev, span, pair_width), bf16), pltpu.SemaphoreType.DMA((n_col,))],
+        + [pltpu.VMEM((n_col - 1, rows_dev, span, pair_width), bf16), pltpu.SemaphoreType.DMA((n_col, rows_dev))],
         compiler_params=params,
         name="far",
     )(*operands)

time: 16.4 us -> 16.3 us (level)
  waiting for transfers between devices: 2.53 us -> 3.81 us
  starting transfers between devices: 8.52 us -> 7.79 us
  local copies, waits for them, and re-layouts: 0.67 us -> 0 us
    ppermute x4, waiting for transfers between devices: 2.15 us -> 3.58 us  [to_chip(): return lax.ppermute(array, ('res', 'col', 'seq'), route)]
    ppermute x4, starting transfers between devices: 7.92 us -> 7.1 us  [to_chip(): return lax.ppermute(array, ('res', 'col', 'seq'), route)]
    unnamed x4 -> x0, local copies, waits for them, and re-layouts: 0.67 us -> none
where the time goes in v11:
time: 16.3 us; the launch traced here: 16.2 us
  starting transfers between devices  7.79 us (48%)
  Pallas kernels  4.54 us (28%)
  waiting for transfers between devices  3.81 us (23%)
    ppermute x4, starting transfers between devices, to_chip(): return lax.ppermute(array, ('res', 'col', 'seq'), route)  7.1 us
    ppermute x4, waiting for transfers between devices, to_chip(): return lax.ppermute(array, ('res', 'col', 'seq'), route)  3.58 us
    pallas_call x1, Pallas kernels, per_device(): pl.pallas_call(functools.partial(project_kernel, n_res, solo), out_shape=...  1.64 us
    pallas_call x1, Pallas kernels, per_device(): pl.pallas_call(functools.partial(far_kernel, plan), out_shape=rows_type(n...  1.62 us
    pallas_call x1, Pallas kernels, per_device(): pl.pallas_call(functools.partial(near_kernel, plan), out_shape=[rows_type...  0.85 us
    ppermute x3, starting transfers between devices, to_core(): return lax.ppermute(array, 'seq', [(q, 1 - q) for q in range(n_seq)])  0.69 us
    pallas_call x1, Pallas kernels, per_device(): pl.pallas_call(weight_kernel, out_shape=jax.ShapeDtypeStruct((pair_width,...  0.4 us
  transfers between devices with their start and end apart: 7, of which 4 were waited for; matrix products, arithmetic and copies ran while one was open for 0% of the time, Pallas kernels for 8%

profile of v11, /device:TPU:0, one launch (start us, length us, event | category | flops | bytes accessed | tf_op | source)
XLA Modules:
  0.0 16.2 jit_solution(804266067187459551)
XLA Ops:
  0.0 1.6 %project.1 = (bf16[256,128]{1,0:T(8,128)(2,1)S(1)}, bf16[160,128]{1,0:T(8,128)(2,1)S(1)}, bf16[1024,128]{1,0:T(8,128)(2,1)S(1)}, f32[1,128]{1,0:T(1,128)S(1)}) custom-call(bf16[8,64,256]{2,1,0:T(8,128)(2,1)} %refs_0_.1, f32[1,256]{1,0:T(1,128)} %bitcast.9, f32[1,256]{1,0:T(1,128)} %bitcast.10, bf16[32,256]{1,0:T(8,128)(2,1)} %bitcast.7, f32[1,32]{1,0:T(1,128)} %bitcast.11, ...), custom_call_target="tpu_custom_call" | custom-call | tf_op jit(solution)/shard_map/project/pallas_call | solution.py:306
  1.6 0.5 %collective-permute-start.1 = (bf16[256,128]{1,0:T(8,128)(2,1)S(1)}, bf16[256,128]{1,0:T(8,128)(2,1)S(1)}, u32[]{:S(2)}, u32[]{:S(2)}) collective-permute-start(bf16[256,128]{1,0:T(8,128)(2,1)S(1)} %get-tuple-element.17.own_ref), channel_id=1, source_target_pairs={{0,1},{1,0},{2,3},{3,2},{4,5},{5,4},{6,7},{7,6},{8,9},{9,8},{10,11... | collective-permute-start | bytes 196616 | tf_op jit(solution)/shard_map/ppermute | solution.py:324
  2.2 2.6 %collective-permute-start = (bf16[160,128]{1,0:T(8,128)(2,1)S(1)}, bf16[160,128]{1,0:T(8,128)(2,1)S(1)}, u32[]{:S(2)}, u32[]{:S(2)}) collective-permute-start(bf16[160,128]{1,0:T(8,128)(2,1)S(1)} %get-tuple-element.16), channel_id=1, source_target_pairs={{0,4},{1,5},{2,6},{3,7},{4,0},{5,1},{6,2},{7,3},{8,12},{9,13},{10,... | collective-permute-start | bytes 122888 | tf_op jit(solution)/shard_map/ppermute | solution.py:333
  4.8 0.0 collective-permute-done.1.other_ref
  4.8 2.7 %collective-permute-start.2 = (bf16[320,128]{1,0:T(8,128)(2,1)S(1)}, bf16[320,128]{1,0:T(8,128)(2,1)S(1)}, u32[]{:S(2)}, u32[]{:S(2)}) collective-permute-start(bf16[320,128]{1,0:T(8,128)(2,1)S(1)} %get-tuple-element.18), channel_id=1, source_target_pairs={{0,8},{1,13},{2,10},{3,15},{4,12},{5,9},{6,14},{7,11},{8,0},{9,5},... | collective-permute-start | bytes 245768 | tf_op jit(solution)/shard_map/ppermute | solution.py:333
  7.5 1.3 %collective-permute-start.4 = (bf16[64,128]{1,0:T(8,128)(2,1)S(1)}, bf16[64,128]{1,0:T(8,128)(2,1)S(1)}, u32[]{:S(2)}, u32[]{:S(2)}) collective-permute-start(bf16[64,128]{1,0:T(8,128)(2,1)S(1)} %get-tuple-element.21), channel_id=1, source_target_pairs={{0,10},{1,15},{2,8},{3,13},{4,14},{5,11},{6,12},{7,9},{8,2},{9,7},... | collective-permute-start | bytes 49160 | tf_op jit(solution)/shard_map/ppermute | solution.py:333
  8.8 0.5 %collective-permute-start.5 = (bf16[64,128]{1,0:T(8,128)(2,1)S(1)}, bf16[64,128]{1,0:T(8,128)(2,1)S(1)}, u32[]{:S(2)}, u32[]{:S(2)}) collective-permute-start(bf16[64,128]{1,0:T(8,128)(2,1)S(1)} %get-tuple-element.22), channel_id=1, source_target_pairs={{0,2},{1,7},{2,0},{3,5},{4,6},{5,3},{6,4},{7,1},{8,10},{9,15},{10,... | collective-permute-start | bytes 49160 | tf_op jit(solution)/shard_map/ppermute | solution.py:333
  9.3 0.0 collective-permute-done.refs_0_.solo_ref
  9.3 0.4 %weights.1.w_ref.refs_2_ = bf16[128,1024]{1,0:T(8,128)(2,1)S(1)} custom-call(bf16[1024,128]{1,0:T(8,128)(2,1)S(1)} %get-tuple-element.15.w_ref, bf16[144,128]{1,0:T(8,128)(2,1)S(1)} %core.3._.refs_0_), custom_call_target="tpu_custom_call" | custom-call | tf_op jit(solution)/shard_map/weights/pallas_call | solution.py:361
  9.7 2.5 %collective-permute-done.2.refs_1_.refs_0_ = bf16[320,128]{1,0:T(8,128)(2,1)S(1)} collective-permute-done((bf16[320,128]{1,0:T(8,128)(2,1)S(1)}, bf16[320,128]{1,0:T(8,128)(2,1)S(1)}, u32[]{:S(2)}, u32[]{:S(2)}) %collective-permute-start.2) | collective-permute-done | bytes 81952 | tf_op jit(solution)/shard_map/ppermute | solution.py:333
  12.3 0.1 collective-permute-start.3
  12.3 1.0 %collective-permute-done.4.refs_0_ = bf16[64,128]{1,0:T(8,128)(2,1)S(1)} collective-permute-done((bf16[64,128]{1,0:T(8,128)(2,1)S(1)}, bf16[64,128]{1,0:T(8,128)(2,1)S(1)}, u32[]{:S(2)}, u32[]{:S(2)}) %collective-permute-start.4) | collective-permute-done | bytes 16416 | tf_op jit(solution)/shard_map/ppermute | solution.py:333
  13.4 0.0 collective-permute-done.5.refs_1_
  13.4 0.1 collective-permute-start.6
  13.5 0.2 collective-permute-done.3.refs_1_
  13.6 0.9 %near.1 = (bf16[1,8,64,128]{3,2,1,0:T(8,128)(2,1)S(1)}, bf16[2048,256]{1,0:T(8,128)(2,1)S(1)}) custom-call(f32[1,128]{1,0:T(1,128)S(1)} %get-tuple-element.14.offset.offset_ref, bf16[128,1024]{1,0:T(8,128)(2,1)S(1)} %weights.1.w_ref.refs_2_, bf16[256,128]{1,0:T(8,128)(2,1)S(1)} %get-tuple-element.17.own_ref, ...), custom_call_target="tpu_custom_call" | custom-call | tf_op jit(solution)/shard_map/near/pallas_call | solution.py:389
  14.5 0.1 collective-permute-done.6.refs_2_
  14.6 1.6 %far.1 = bf16[2,8,64,128]{3,2,1,0:T(8,128)(2,1)} custom-call(f32[1,128]{1,0:T(1,128)S(1)} %get-tuple-element.14.offset.offset_ref, bf16[128,1024]{1,0:T(8,128)(2,1)S(1)} %weights.1.w_ref.refs_2_, bf16[2048,256]{1,0:T(8,128)(2,1)S(1)} %get-tuple-element.19.weights_ref, bf16[1,8,64,128]{3,2,1,0:T(8,128)(2,1)S(1)} %get-tuple-element.20.near_ref, ...), custom_call_target="tpu_custom_call" | custom-call | tf_op jit(solution)/shard_map/far/pallas_call | solution.py:402
  (4 shorter events, 0.0 us)
Async XLA Ops:
  1.6 3.2 %collective-permute-start.1 = (bf16[256,128]{1,0:T(8,128)(2,1)S(1)}, bf16[256,128]{1,0:T(8,128)(2,1)S(1)}, u32[]{:S(2)}, u32[]{:S(2)}) collective-permute-start(bf16[256,128]{1,0:T(8,128)(2,1)S(1)} %get-tuple-element.17.own_ref), channel_id=1, source_target_pairs={{0,1},{1,0},{2,3},{3,2},{4,5},{5,4},{6,7},{7,6},{8,9},{9,8},{10,11... | collective-permute-start | bytes 196616 | tf_op jit(solution)/shard_map/ppermute | solution.py:324
  2.2 7.1 %collective-permute-start = (bf16[160,128]{1,0:T(8,128)(2,1)S(1)}, bf16[160,128]{1,0:T(8,128)(2,1)S(1)}, u32[]{:S(2)}, u32[]{:S(2)}) collective-permute-start(bf16[160,128]{1,0:T(8,128)(2,1)S(1)} %get-tuple-element.16), channel_id=1, source_target_pairs={{0,4},{1,5},{2,6},{3,7},{4,0},{5,1},{6,2},{7,3},{8,12},{9,13},{10,... | collective-permute-start | bytes 122888 | tf_op jit(solution)/shard_map/ppermute | solution.py:333
  4.8 7.4 %collective-permute-start.2 = (bf16[320,128]{1,0:T(8,128)(2,1)S(1)}, bf16[320,128]{1,0:T(8,128)(2,1)S(1)}, u32[]{:S(2)}, u32[]{:S(2)}) collective-permute-start(bf16[320,128]{1,0:T(8,128)(2,1)S(1)} %get-tuple-element.18), channel_id=1, source_target_pairs={{0,8},{1,13},{2,10},{3,15},{4,12},{5,9},{6,14},{7,11},{8,0},{9,5},... | collective-permute-start | bytes 245768 | tf_op jit(solution)/shard_map/ppermute | solution.py:333
  7.5 5.9 %collective-permute-start.4 = (bf16[64,128]{1,0:T(8,128)(2,1)S(1)}, bf16[64,128]{1,0:T(8,128)(2,1)S(1)}, u32[]{:S(2)}, u32[]{:S(2)}) collective-permute-start(bf16[64,128]{1,0:T(8,128)(2,1)S(1)} %get-tuple-element.21), channel_id=1, source_target_pairs={{0,10},{1,15},{2,8},{3,13},{4,14},{5,11},{6,12},{7,9},{8,2},{9,7},... | collective-permute-start | bytes 49160 | tf_op jit(solution)/shard_map/ppermute | solution.py:333
  8.8 4.6 %collective-permute-start.5 = (bf16[64,128]{1,0:T(8,128)(2,1)S(1)}, bf16[64,128]{1,0:T(8,128)(2,1)S(1)}, u32[]{:S(2)}, u32[]{:S(2)}) collective-permute-start(bf16[64,128]{1,0:T(8,128)(2,1)S(1)} %get-tuple-element.22), channel_id=1, source_target_pairs={{0,2},{1,7},{2,0},{3,5},{4,6},{5,3},{6,4},{7,1},{8,10},{9,15},{10,... | collective-permute-start | bytes 49160 | tf_op jit(solution)/shard_map/ppermute | solution.py:333
  12.3 1.4 %collective-permute-start.3 = (bf16[432,128]{1,0:T(8,128)(2,1)S(1)}, bf16[432,128]{1,0:T(8,128)(2,1)S(1)}, u32[]{:S(2)}, u32[]{:S(2)}) collective-permute-start(bf16[432,128]{1,0:T(8,128)(2,1)S(1)} %core.4), channel_id=1, source_target_pairs={{0,1},{1,0},{2,3},{3,2},{4,5},{5,4},{6,7},{7,6},{8,9},{9,8},{10,11... | collective-permute-start | bytes 331784 | tf_op jit(solution)/shard_map/ppermute | solution.py:324
  13.4 1.2 %collective-permute-start.6 = (bf16[64,128]{1,0:T(8,128)(2,1)S(1)}, bf16[64,128]{1,0:T(8,128)(2,1)S(1)}, u32[]{:S(2)}, u32[]{:S(2)}) collective-permute-start(bf16[64,128]{1,0:T(8,128)(2,1)S(1)} %core.5), channel_id=1, source_target_pairs={{0,1},{1,0},{2,3},{3,2},{4,5},{5,4},{6,7},{7,6},{8,9},{9,8},{10,11... | collective-permute-start | bytes 49160 | tf_op jit(solution)/shard_map/ppermute | solution.py:324

commit v12 on v11

--- a/solution.py
+++ b/solution.py
@@ -19,11 +19,35 @@
     return index ^ step if size & (size - 1) == 0 else (index + step) % size
 
 
+def routes(n_res):
+    def turn(k):
+        return [(z + k) % n_res for z in range(n_res)]
+
+    def swap(k):
+        return [partner(z, k, n_res) for z in range(n_res)]
+
+    solo_route = [turn(1)] * 2
+    z_routes = [[turn(k), turn(k + 1)] for k in range(2, n_res, 2)]
+    x_routes = [[swap(k), swap(k + 1)] for k in range(n_res - 2, -1, -2)]
+    return solo_route, z_routes, x_routes
+
+
+def sources(route):
+    return [[to.index(z) for z in range(len(to))] for to in route]
+
+
+def look_up(route, core, chip):
+    found = 0
+    for k, (first, second) in enumerate(zip(*route)):
+        found = jnp.where(chip == k, jnp.where(core == 0, first, second), found)
+    return found
+
+
 def lane_index(shape):
     return lax.broadcasted_iota(jnp.int32, shape, len(shape) - 1)
 
 
-def project_kernel(n_res, solo, *refs):
+def project_kernel(n_res, solo_route, *refs):
     n_in, n_later = 7, 2
     sources, refs = refs[: n_in + n_later], refs[n_in + n_later :]
     (slab_out, solo_out), later = refs[:2], refs[2 : 2 + n_later]
@@ -78,19 +102,19 @@
     part = n_left // n_res
     slab_out[:n_right] = right_slab
     slab_out[n_right:] = lane_scr[...].astype(jnp.bfloat16)
-    to = partner(lax.axis_index("res"), solo, n_res)
+    to = look_up(solo_route, 0, lax.axis_index("res"))
     solo_out[:n_right] = right_slab
     solo_out[n_right:] = lane_scr[pl.ds(pl.multiple_of(to * part, part), part), :].astype(jnp.bfloat16)
     for copy in copies[n_in:]:
         copy.wait()
 
 
-def chip_kernel(n_res, steps, own_ref, other_ref, *outs):
+def chip_kernel(n_res, ways, own_ref, other_ref, *outs):
     n_right = own_ref.shape[0] // 2
     part = n_right // n_res
     me, here = lax.axis_index("seq"), lax.axis_index("res")
-    for (first, second), out in zip(steps, outs):
-        to = partner(here, jnp.where(me == 0, first, second), n_res)
+    for route, out in zip(ways, outs):
+        to = look_up(route, me, here)
         start = pl.multiple_of(n_right + to * part, part)
         at = out.shape[0] - 2 * part
         if at:
@@ -142,7 +166,7 @@
         pl.loop(0, n_blocks)(body)
 
 
-def update_block(plan, block, offset, w_ref, weight_of, left_scr, outer_scr, staged, finish=None):
+def update_block(plan, block, offset, w_ref, weight_of, left_scr, outer_scr, staged):
     chans, total = plan["chans"], plan["total"]
     half = LANES // 2
     fold = LANES // chans
@@ -172,17 +196,13 @@
                     staged[u, turn * fold + first + k, pl.ds(block * half, half), :] = piece[
                         turn * half : (turn + 1) * half
                     ]
-            if finish is not None:
-                for turn in range(LANES // half):
-                    finish(u, turn * fold + first, step)
 
 
 def row_copy(plan, step, staged, out_ref, sem):
     n_col = plan["n_col"]
     col = lax.axis_index("col")
     source = partner(col, step, n_col) if n_col & (n_col - 1) == 0 else (col - step + n_col) % n_col
-    row, rows = staged[1]
-    return pltpu.make_async_copy(staged[0].at[pl.ds(row, rows)], out_ref.at[source, pl.ds(row, rows)], sem)
+    return pltpu.make_async_copy(staged, out_ref.at[source], sem)
 
 
 def near_kernel(plan, offset, w_ref, own_ref, other_ref, solo_ref, *refs):
@@ -237,47 +257,44 @@
     chans, part, own, n_s, n_res = plan["chans"], plan["part"], plan["own"], plan["n_s"], plan["n_res"]
     pairs = chans // 2
     me = lax.axis_index("seq")
-    rows_dev = near_ref.shape[1]
-    copies = [row_copy(plan, 0, (near_ref.at[0], (0, rows_dev)), out_ref, sems.at[0, 0])]
+    copies = [row_copy(plan, 0, near_ref.at[0], out_ref, sems.at[0])]
     copies[0].start()
 
     def rows_of(ref, at):
         return ref[pl.ds(at, own), :].astype(jnp.float32)
 
-    def pick(first, second):
-        return [jnp.where(me == 0, a, b) for a, b in zip(first, second)]
-
-    x_pairs = plan["x_pairs"]
+    here = lax.axis_index("res")
+    order = [here, look_up(sources(plan["solo"]), me, here)]
+    for route in plan["z_routes"]:
+        order += [look_up(sources(route), core, here) for core in (me, 1 - me)]
+    x_routes = plan["x_routes"]
     for u in range(plan["n_col"] - 1):
-        chunks = [None] * n_res
-        for k, (first, second) in enumerate(x_pairs):
-            place = u * len(x_pairs) + k
+        held = []
+        for k, route in enumerate(x_routes):
+            place = u * len(x_routes) + k
             heard = [rows_of(x_refs[place], pl.multiple_of(h * part + me * own, own)) for h in range(2)]
             told = [rows_of(other_in, (2 * place + 1 - h) * own) for h in range(2)]
-            chunks[first], chunks[second] = pick(heard, told), pick(told, heard)
-        order = chunks[0] + chunks[plan["solo"]]
-        for first, second in plan["z_pairs"]:
-            order += pick(chunks[first], chunks[second]) + pick(chunks[second], chunks[first])
-        fill_left(left_scr, u, order, n_s)
+            held += [(look_up(sources(route), me, here), heard), (look_up(sources(route), 1 - me, here), told)]
+        slabs = []
+        for chip in order:
+            for side in range(2):
+                found = held[0][1][side]
+                for source, slab in held[1:]:
+                    found = jnp.where(source == chip, slab[side], found)
+                slabs.append(found)
+        fill_left(left_scr, u, slabs, n_s)
     depth = left_scr.shape[1]
 
     def block_of_columns(block):
         def weight_of(pair):
             return weights_ref[pl.ds((block * pairs + pair) * depth, depth), :]
 
-        update_block(
-            plan, block, offset_ref, w_ref, weight_of, left_scr, outer_scr, staged, finish if n_blocks == 1 else None
-        )
-
-    def finish(u, row, rows):
-        copies.append(row_copy(plan, 1 + u, (staged.at[u], (row, rows)), out_ref, sems.at[1 + u, row]))
+        update_block(plan, block, offset_ref, w_ref, weight_of, left_scr, outer_scr, staged)
+
+    loop_blocks(weights_ref.shape[0] // (pairs * depth), block_of_columns)
+    for u in range(staged.shape[0]):
+        copies.append(row_copy(plan, 1 + u, staged.at[u], out_ref, sems.at[1 + u]))
         copies[-1].start()
-
-    n_blocks = weights_ref.shape[0] // (pairs * depth)
-    loop_blocks(n_blocks, block_of_columns)
-    if n_blocks > 1:
-        for u in range(staged.shape[0]):
-            finish(u, 0, rows_dev)
     for copy in copies:
         copy.wait()
 
@@ -297,9 +314,7 @@
     def rows(n):
         return jax.ShapeDtypeStruct((n, LANES), bf16)
 
-    solo = 1
-    z_pairs = [(k, k + 1) for k in range(2, n_res, 2)]
-    x_pairs = [(k, k + 1) for k in range(n_res - 2, -1, -2)]
+    solo, z_routes, x_routes = routes(n_res)
 
     taken = (alignment, scale.reshape(1, -1), shift.reshape(1, -1), w1.T, b1.reshape(1, -1), w2.T, b2.reshape(1, -1))
     later = (w_final, offset.reshape(1, -1))
@@ -323,27 +338,27 @@
     def to_core(array):
         return lax.ppermute(array, "seq", [(q, 1 - q) for q in range(n_seq)])
 
-    def to_chip(array, step_col, steps):
-        route = []
+    def to_chip(array, step_col, route):
+        pairs = []
         for r in range(n_res):
             for c in range(n_col):
                 for q in range(n_seq):
-                    to = partner(r, steps[q], n_res) * n_col + partner(c, step_col, n_col)
-                    route.append(((r * n_col + c) * n_seq + q, to * n_seq + q))
-        return lax.ppermute(array, ("res", "col", "seq"), route)
+                    to = route[q][r] * n_col + partner(c, step_col, n_col)
+                    pairs.append(((r * n_col + c) * n_seq + q, to * n_seq + q))
+        return lax.ppermute(array, ("res", "col", "seq"), pairs)
 
     slab_in = to_core(slab)
-    solo_in = to_chip(solo_out, 0, (solo, solo))
-    sends = [(0, steps) for steps in z_pairs] + [(u, steps) for u in range(1, n_col) for steps in x_pairs]
+    solo_in = to_chip(solo_out, 0, solo)
+    sends = [(0, route) for route in z_routes] + [(u, route) for u in range(1, n_col) for route in x_routes]
     messages = pl.pallas_call(
-        functools.partial(chip_kernel, n_res, [steps for _, steps in sends]),
+        functools.partial(chip_kernel, n_res, [route for _, route in sends]),
         out_shape=[rows(2 * part + (0 if u else 2 * n_right)) for u, _ in sends],
         in_specs=[VMEM] * 2,
         out_specs=[VMEM] * len(sends),
         compiler_params=params,
         name="chip",
     )(slab, slab_in)
-    heard = [to_chip(message, u, steps) for message, (u, steps) in zip(messages, sends)]
+    heard = [to_chip(message, u, route) for message, (u, route) in zip(messages, sends)]
 
     def pack(arrays, bodies, flops, after=()):
         return pl.pallas_call(
@@ -356,7 +371,7 @@
             name="core",
         )(*arrays, *after)
 
-    z_in, x_in = heard[: len(z_pairs)], heard[len(z_pairs) :]
+    z_in, x_in = heard[: len(z_routes)], heard[len(z_routes) :]
     arrays = [pack([solo_in], [n_right], 500_000_000)] + z_in
     weights = pl.pallas_call(
         weight_kernel,
@@ -373,7 +388,7 @@
     turns = rows_dev * chans // LANES
     depth = turns * n_s * n_res * n_seq
     plan = dict(n_res=n_res, n_col=n_col, chans=chans, part=part, own=own, n_s=n_s, total=float(n_s * n_res * n_seq))
-    plan.update(solo=solo, z_pairs=z_pairs, x_pairs=x_pairs)
+    plan.update(solo=solo, z_routes=z_routes, x_routes=x_routes)
     n_blocks = n_right // (chans // 2 * n_s)
 
     def scratch(n_u):
@@ -405,7 +420,7 @@
         in_specs=[VMEM] * len(operands),
         out_specs=HBM,
         scratch_shapes=scratch(n_col - 1)
-        + [pltpu.VMEM((n_col - 1, rows_dev, span, pair_width), bf16), pltpu.SemaphoreType.DMA((n_col, rows_dev))],
+        + [pltpu.VMEM((n_col - 1, rows_dev, span, pair_width), bf16), pltpu.SemaphoreType.DMA((n_col,))],
         compiler_params=params,
         name="far",
     )(*operands)

time: 16.3 us -> 15.9 us (0.975)
  waiting for transfers between devices: 3.81 us -> 3.33 us
    ppermute x4, waiting for transfers between devices: 3.58 us -> 3.24 us  [to_chip(): return lax.ppermute(array, ('res', 'col', 'seq'), pairs)]
  transfers between devices with their start and end apart: 7 -> 7, of which waited for: 4 -> 3; matrix products, arithmetic and copies ran while one was open for 0% -> 0% of each run, Pallas kernels for 8% -> 8%
where the time goes in v12:
time: 15.9 us; the launch traced here: 15.7 us
  starting transfers between devices  7.9 us (50%)
  Pallas kernels  4.45 us (28%)
  waiting for transfers between devices  3.33 us (21%)
    ppermute x4, starting transfers between devices, to_chip(): return lax.ppermute(array, ('res', 'col', 'seq'), pairs)  7.07 us
    ppermute x4, waiting for transfers between devices, to_chip(): return lax.ppermute(array, ('res', 'col', 'seq'), pairs)  3.24 us
    pallas_call x1, Pallas kernels, per_device(): pl.pallas_call(functools.partial(project_kernel, n_res, solo), out_shape=...  1.64 us
    pallas_call x1, Pallas kernels, per_device(): pl.pallas_call(functools.partial(far_kernel, plan), out_shape=rows_type(n...  1.52 us
    pallas_call x1, Pallas kernels, per_device(): pl.pallas_call(functools.partial(near_kernel, plan), out_shape=[rows_type...  0.85 us
    ppermute x3, starting transfers between devices, to_core(): return lax.ppermute(array, 'seq', [(q, 1 - q) for q in range(n_seq)])  0.82 us
    pallas_call x1, Pallas kernels, per_device(): pl.pallas_call(weight_kernel, out_shape=jax.ShapeDtypeStruct((pair_width,...  0.4 us
  transfers between devices with their start and end apart: 7, of which 3 were waited for; matrix products, arithmetic and copies ran while one was open for 0% of the time, Pallas kernels for 8%

profile of v12, /device:TPU:0, one launch (start us, length us, event | category | flops | bytes accessed | tf_op | source)
XLA Modules:
  0.0 15.7 jit_solution(3374457580899410128)
XLA Ops:
  0.0 1.6 %project.1 = (bf16[256,128]{1,0:T(8,128)(2,1)S(1)}, bf16[160,128]{1,0:T(8,128)(2,1)S(1)}, bf16[1024,128]{1,0:T(8,128)(2,1)S(1)}, f32[1,128]{1,0:T(1,128)S(1)}) custom-call(bf16[8,64,256]{2,1,0:T(8,128)(2,1)} %refs_0_.1, f32[1,256]{1,0:T(1,128)} %bitcast.9, f32[1,256]{1,0:T(1,128)} %bitcast.10, bf16[32,256]{1,0:T(8,128)(2,1)} %bitcast.7, f32[1,32]{1,0:T(1,128)} %bitcast.11, ...), custom_call_target="tpu_custom_call" | custom-call | tf_op jit(solution)/shard_map/project/pallas_call | solution.py:321
  1.6 0.5 %collective-permute-start.1 = (bf16[256,128]{1,0:T(8,128)(2,1)S(1)}, bf16[256,128]{1,0:T(8,128)(2,1)S(1)}, u32[]{:S(2)}, u32[]{:S(2)}) collective-permute-start(bf16[256,128]{1,0:T(8,128)(2,1)S(1)} %get-tuple-element.17.own_ref), channel_id=1, source_target_pairs={{0,1},{1,0},{2,3},{3,2},{4,5},{5,4},{6,7},{7,6},{8,9},{9,8},{10,11... | collective-permute-start | bytes 196616 | tf_op jit(solution)/shard_map/ppermute | solution.py:339
  2.2 2.6 %collective-permute-start = (bf16[160,128]{1,0:T(8,128)(2,1)S(1)}, bf16[160,128]{1,0:T(8,128)(2,1)S(1)}, u32[]{:S(2)}, u32[]{:S(2)}) collective-permute-start(bf16[160,128]{1,0:T(8,128)(2,1)S(1)} %get-tuple-element.16), channel_id=1, source_target_pairs={{0,4},{1,5},{2,6},{3,7},{4,8},{5,9},{6,10},{7,11},{8,12},{9,13},{1... | collective-permute-start | bytes 122888 | tf_op jit(solution)/shard_map/ppermute | solution.py:348
  4.8 0.0 collective-permute-done.1.other_ref
  4.8 2.6 %collective-permute-start.2 = (bf16[320,128]{1,0:T(8,128)(2,1)S(1)}, bf16[320,128]{1,0:T(8,128)(2,1)S(1)}, u32[]{:S(2)}, u32[]{:S(2)}) collective-permute-start(bf16[320,128]{1,0:T(8,128)(2,1)S(1)} %get-tuple-element.18), channel_id=1, source_target_pairs={{0,8},{1,13},{2,10},{3,15},{4,12},{5,1},{6,14},{7,3},{8,0},{9,5},{... | collective-permute-start | bytes 245768 | tf_op jit(solution)/shard_map/ppermute | solution.py:348
  7.5 1.3 %collective-permute-start.4 = (bf16[64,128]{1,0:T(8,128)(2,1)S(1)}, bf16[64,128]{1,0:T(8,128)(2,1)S(1)}, u32[]{:S(2)}, u32[]{:S(2)}) collective-permute-start(bf16[64,128]{1,0:T(8,128)(2,1)S(1)} %get-tuple-element.21), channel_id=1, source_target_pairs={{0,10},{1,15},{2,8},{3,13},{4,14},{5,11},{6,12},{7,9},{8,2},{9,7},... | collective-permute-start | bytes 49160 | tf_op jit(solution)/shard_map/ppermute | solution.py:348
  8.7 0.5 %collective-permute-start.5 = (bf16[64,128]{1,0:T(8,128)(2,1)S(1)}, bf16[64,128]{1,0:T(8,128)(2,1)S(1)}, u32[]{:S(2)}, u32[]{:S(2)}) collective-permute-start(bf16[64,128]{1,0:T(8,128)(2,1)S(1)} %get-tuple-element.22), channel_id=1, source_target_pairs={{0,2},{1,7},{2,0},{3,5},{4,6},{5,3},{6,4},{7,1},{8,10},{9,15},{10,... | collective-permute-start | bytes 49160 | tf_op jit(solution)/shard_map/ppermute | solution.py:348
  9.3 0.0 collective-permute-done.refs_0_.solo_ref
  9.3 0.4 %weights.1.w_ref.refs_2_ = bf16[128,1024]{1,0:T(8,128)(2,1)S(1)} custom-call(bf16[1024,128]{1,0:T(8,128)(2,1)S(1)} %get-tuple-element.15.w_ref, bf16[144,128]{1,0:T(8,128)(2,1)S(1)} %core.3._.refs_0_), custom_call_target="tpu_custom_call" | custom-call | tf_op jit(solution)/shard_map/weights/pallas_call | solution.py:376
  9.7 2.1 %collective-permute-done.2.refs_1_.refs_0_ = bf16[320,128]{1,0:T(8,128)(2,1)S(1)} collective-permute-done((bf16[320,128]{1,0:T(8,128)(2,1)S(1)}, bf16[320,128]{1,0:T(8,128)(2,1)S(1)}, u32[]{:S(2)}, u32[]{:S(2)}) %collective-permute-start.2) | collective-permute-done | bytes 81952 | tf_op jit(solution)/shard_map/ppermute | solution.py:348
  11.8 0.1 collective-permute-start.3
  11.9 1.1 %collective-permute-done.4.refs_0_ = bf16[64,128]{1,0:T(8,128)(2,1)S(1)} collective-permute-done((bf16[64,128]{1,0:T(8,128)(2,1)S(1)}, bf16[64,128]{1,0:T(8,128)(2,1)S(1)}, u32[]{:S(2)}, u32[]{:S(2)}) %collective-permute-start.4) | collective-permute-done | bytes 16416 | tf_op jit(solution)/shard_map/ppermute | solution.py:348
  13.0 0.0 collective-permute-done.5.refs_1_
  13.0 0.2 %collective-permute-start.6 = (bf16[64,128]{1,0:T(8,128)(2,1)S(1)}, bf16[64,128]{1,0:T(8,128)(2,1)S(1)}, u32[]{:S(2)}, u32[]{:S(2)}) collective-permute-start(bf16[64,128]{1,0:T(8,128)(2,1)S(1)} %core.5), channel_id=1, source_target_pairs={{0,1},{1,0},{2,3},{3,2},{4,5},{5,4},{6,7},{7,6},{8,9},{9,8},{10,11... | collective-permute-start | bytes 49160 | tf_op jit(solution)/shard_map/ppermute | solution.py:339
  13.3 0.0 collective-permute-done.3.refs_1_
  13.3 0.9 %near.1 = (bf16[1,8,64,128]{3,2,1,0:T(8,128)(2,1)S(1)}, bf16[2048,256]{1,0:T(8,128)(2,1)S(1)}) custom-call(f32[1,128]{1,0:T(1,128)S(1)} %get-tuple-element.14.offset.offset_ref, bf16[128,1024]{1,0:T(8,128)(2,1)S(1)} %weights.1.w_ref.refs_2_, bf16[256,128]{1,0:T(8,128)(2,1)S(1)} %get-tuple-element.17.own_ref, ...), custom_call_target="tpu_custom_call" | custom-call | tf_op jit(solution)/shard_map/near/pallas_call | solution.py:404
  14.1 0.1 collective-permute-done.6.refs_2_
  14.2 1.5 %far.1 = bf16[2,8,64,128]{3,2,1,0:T(8,128)(2,1)} custom-call(f32[1,128]{1,0:T(1,128)S(1)} %get-tuple-element.14.offset.offset_ref, bf16[128,1024]{1,0:T(8,128)(2,1)S(1)} %weights.1.w_ref.refs_2_, bf16[2048,256]{1,0:T(8,128)(2,1)S(1)} %get-tuple-element.19.weights_ref, bf16[1,8,64,128]{3,2,1,0:T(8,128)(2,1)S(1)} %get-tuple-element.20.near_ref, ...), custom_call_target="tpu_custom_call" | custom-call | tf_op jit(solution)/shard_map/far/pallas_call | solution.py:417
  (4 shorter events, 0.0 us)
Async XLA Ops:
  1.6 3.2 %collective-permute-start.1 = (bf16[256,128]{1,0:T(8,128)(2,1)S(1)}, bf16[256,128]{1,0:T(8,128)(2,1)S(1)}, u32[]{:S(2)}, u32[]{:S(2)}) collective-permute-start(bf16[256,128]{1,0:T(8,128)(2,1)S(1)} %get-tuple-element.17.own_ref), channel_id=1, source_target_pairs={{0,1},{1,0},{2,3},{3,2},{4,5},{5,4},{6,7},{7,6},{8,9},{9,8},{10,11... | collective-permute-start | bytes 196616 | tf_op jit(solution)/shard_map/ppermute | solution.py:339
  2.2 7.1 %collective-permute-start = (bf16[160,128]{1,0:T(8,128)(2,1)S(1)}, bf16[160,128]{1,0:T(8,128)(2,1)S(1)}, u32[]{:S(2)}, u32[]{:S(2)}) collective-permute-start(bf16[160,128]{1,0:T(8,128)(2,1)S(1)} %get-tuple-element.16), channel_id=1, source_target_pairs={{0,4},{1,5},{2,6},{3,7},{4,8},{5,9},{6,10},{7,11},{8,12},{9,13},{1... | collective-permute-start | bytes 122888 | tf_op jit(solution)/shard_map/ppermute | solution.py:348
  4.8 7.0 %collective-permute-start.2 = (bf16[320,128]{1,0:T(8,128)(2,1)S(1)}, bf16[320,128]{1,0:T(8,128)(2,1)S(1)}, u32[]{:S(2)}, u32[]{:S(2)}) collective-permute-start(bf16[320,128]{1,0:T(8,128)(2,1)S(1)} %get-tuple-element.18), channel_id=1, source_target_pairs={{0,8},{1,13},{2,10},{3,15},{4,12},{5,1},{6,14},{7,3},{8,0},{9,5},{... | collective-permute-start | bytes 245768 | tf_op jit(solution)/shard_map/ppermute | solution.py:348
  7.5 5.5 %collective-permute-start.4 = (bf16[64,128]{1,0:T(8,128)(2,1)S(1)}, bf16[64,128]{1,0:T(8,128)(2,1)S(1)}, u32[]{:S(2)}, u32[]{:S(2)}) collective-permute-start(bf16[64,128]{1,0:T(8,128)(2,1)S(1)} %get-tuple-element.21), channel_id=1, source_target_pairs={{0,10},{1,15},{2,8},{3,13},{4,14},{5,11},{6,12},{7,9},{8,2},{9,7},... | collective-permute-start | bytes 49160 | tf_op jit(solution)/shard_map/ppermute | solution.py:348
  8.7 4.3 %collective-permute-start.5 = (bf16[64,128]{1,0:T(8,128)(2,1)S(1)}, bf16[64,128]{1,0:T(8,128)(2,1)S(1)}, u32[]{:S(2)}, u32[]{:S(2)}) collective-permute-start(bf16[64,128]{1,0:T(8,128)(2,1)S(1)} %get-tuple-element.22), channel_id=1, source_target_pairs={{0,2},{1,7},{2,0},{3,5},{4,6},{5,3},{6,4},{7,1},{8,10},{9,15},{10,... | collective-permute-start | bytes 49160 | tf_op jit(solution)/shard_map/ppermute | solution.py:348
  11.8 1.4 %collective-permute-start.3 = (bf16[432,128]{1,0:T(8,128)(2,1)S(1)}, bf16[432,128]{1,0:T(8,128)(2,1)S(1)}, u32[]{:S(2)}, u32[]{:S(2)}) collective-permute-start(bf16[432,128]{1,0:T(8,128)(2,1)S(1)} %core.4), channel_id=1, source_target_pairs={{0,1},{1,0},{2,3},{3,2},{4,5},{5,4},{6,7},{7,6},{8,9},{9,8},{10,11... | collective-permute-start | bytes 331784 | tf_op jit(solution)/shard_map/ppermute | solution.py:339
  13.0 1.2 %collective-permute-start.6 = (bf16[64,128]{1,0:T(8,128)(2,1)S(1)}, bf16[64,128]{1,0:T(8,128)(2,1)S(1)}, u32[]{:S(2)}, u32[]{:S(2)}) collective-permute-start(bf16[64,128]{1,0:T(8,128)(2,1)S(1)} %core.5), channel_id=1, source_target_pairs={{0,1},{1,0},{2,3},{3,2},{4,5},{5,4},{6,7},{7,6},{8,9},{9,8},{10,11... | collective-permute-start | bytes 49160 | tf_op jit(solution)/shard_map/ppermute | solution.py:339

commit v13 on v12

--- a/solution.py
+++ b/solution.py
@@ -233,17 +233,21 @@
         at_block = block * pairs * n_s
         slabs = [ref[pl.ds(at + at_block, pairs * n_s), :].astype(jnp.float32) for ref, at in rights]
 
+        below = lane_index((depth // (LANES // half), LANES)) < half
+        low = below.astype(jnp.float32).astype(jnp.bfloat16)
+        high = 1 - low
+
         def weight_of(pair):
             here = jnp.concatenate([slab[pair * n_s : (pair + 1) * n_s] for slab in slabs], axis=0)
-            there = pltpu.roll(here, half, 1)
-            low = lane_index(here.shape) < half
+            there = pltpu.roll(here, half, 1).astype(jnp.bfloat16)
+            here = here.astype(jnp.bfloat16)
             weights = jnp.concatenate(
                 [
-                    jnp.concatenate([jnp.where(low, here, 0.0), jnp.where(low, 0.0, there)], axis=0),
-                    jnp.concatenate([jnp.where(low, there, 0.0), jnp.where(low, 0.0, here)], axis=0),
+                    jnp.concatenate([here * low, there * high], axis=0),
+                    jnp.concatenate([there * low, here * high], axis=0),
                 ],
                 axis=1,
-            ).astype(jnp.bfloat16)
+            )
             weights_out[pl.ds((block * pairs + pair) * depth, depth), :] = weights
             return weights
 

time: 15.9 us -> 15.9 us (level)
  no operation moved by 1% of the time
where the time goes in v13:
time: 15.9 us; the launch traced here: 15.7 us
  starting transfers between devices  7.9 us (50%)
  Pallas kernels  4.45 us (28%)
  waiting for transfers between devices  3.33 us (21%)
    ppermute x4, starting transfers between devices, to_chip(): return lax.ppermute(array, ('res', 'col', 'seq'), pairs)  7.07 us
    ppermute x4, waiting for transfers between devices, to_chip(): return lax.ppermute(array, ('res', 'col', 'seq'), pairs)  3.24 us
    pallas_call x1, Pallas kernels, per_device(): pl.pallas_call(functools.partial(project_kernel, n_res, solo), out_shape=...  1.64 us
    pallas_call x1, Pallas kernels, per_device(): pl.pallas_call(functools.partial(far_kernel, plan), out_shape=rows_type(n...  1.52 us
    pallas_call x1, Pallas kernels, per_device(): pl.pallas_call(functools.partial(near_kernel, plan), out_shape=[rows_type...  0.86 us
    ppermute x3, starting transfers between devices, to_core(): return lax.ppermute(array, 'seq', [(q, 1 - q) for q in range(n_seq)])  0.82 us
    pallas_call x1, Pallas kernels, per_device(): pl.pallas_call(weight_kernel, out_shape=jax.ShapeDtypeStruct((pair_width,...  0.4 us
  transfers between devices with their start and end apart: 7, of which 3 were waited for; matrix products, arithmetic and copies ran while one was open for 0% of the time, Pallas kernels for 8%

profile of v13, /device:TPU:0, one launch (start us, length us, event | category | flops | bytes accessed | tf_op | source)
XLA Modules:
  0.0 15.7 jit_solution(12034436870739701386)
XLA Ops:
  0.0 1.6 %project.1 = (bf16[256,128]{1,0:T(8,128)(2,1)S(1)}, bf16[160,128]{1,0:T(8,128)(2,1)S(1)}, bf16[1024,128]{1,0:T(8,128)(2,1)S(1)}, f32[1,128]{1,0:T(1,128)S(1)}) custom-call(bf16[8,64,256]{2,1,0:T(8,128)(2,1)} %refs_0_.1, f32[1,256]{1,0:T(1,128)} %bitcast.9, f32[1,256]{1,0:T(1,128)} %bitcast.10, bf16[32,256]{1,0:T(8,128)(2,1)} %bitcast.7, f32[1,32]{1,0:T(1,128)} %bitcast.11, ...), custom_call_target="tpu_custom_call" | custom-call | tf_op jit(solution)/shard_map/project/pallas_call | solution.py:325
  1.6 0.5 %collective-permute-start.1 = (bf16[256,128]{1,0:T(8,128)(2,1)S(1)}, bf16[256,128]{1,0:T(8,128)(2,1)S(1)}, u32[]{:S(2)}, u32[]{:S(2)}) collective-permute-start(bf16[256,128]{1,0:T(8,128)(2,1)S(1)} %get-tuple-element.17.own_ref), channel_id=1, source_target_pairs={{0,1},{1,0},{2,3},{3,2},{4,5},{5,4},{6,7},{7,6},{8,9},{9,8},{10,11... | collective-permute-start | bytes 196616 | tf_op jit(solution)/shard_map/ppermute | solution.py:343
  2.2 2.6 %collective-permute-start = (bf16[160,128]{1,0:T(8,128)(2,1)S(1)}, bf16[160,128]{1,0:T(8,128)(2,1)S(1)}, u32[]{:S(2)}, u32[]{:S(2)}) collective-permute-start(bf16[160,128]{1,0:T(8,128)(2,1)S(1)} %get-tuple-element.16), channel_id=1, source_target_pairs={{0,4},{1,5},{2,6},{3,7},{4,8},{5,9},{6,10},{7,11},{8,12},{9,13},{1... | collective-permute-start | bytes 122888 | tf_op jit(solution)/shard_map/ppermute | solution.py:352
  4.8 0.0 collective-permute-done.1.other_ref
  4.8 2.6 %collective-permute-start.2 = (bf16[320,128]{1,0:T(8,128)(2,1)S(1)}, bf16[320,128]{1,0:T(8,128)(2,1)S(1)}, u32[]{:S(2)}, u32[]{:S(2)}) collective-permute-start(bf16[320,128]{1,0:T(8,128)(2,1)S(1)} %get-tuple-element.18), channel_id=1, source_target_pairs={{0,8},{1,13},{2,10},{3,15},{4,12},{5,1},{6,14},{7,3},{8,0},{9,5},{... | collective-permute-start | bytes 245768 | tf_op jit(solution)/shard_map/ppermute | solution.py:352
  7.5 1.3 %collective-permute-start.4 = (bf16[64,128]{1,0:T(8,128)(2,1)S(1)}, bf16[64,128]{1,0:T(8,128)(2,1)S(1)}, u32[]{:S(2)}, u32[]{:S(2)}) collective-permute-start(bf16[64,128]{1,0:T(8,128)(2,1)S(1)} %get-tuple-element.21), channel_id=1, source_target_pairs={{0,10},{1,15},{2,8},{3,13},{4,14},{5,11},{6,12},{7,9},{8,2},{9,7},... | collective-permute-start | bytes 49160 | tf_op jit(solution)/shard_map/ppermute | solution.py:352
  8.7 0.5 %collective-permute-start.5 = (bf16[64,128]{1,0:T(8,128)(2,1)S(1)}, bf16[64,128]{1,0:T(8,128)(2,1)S(1)}, u32[]{:S(2)}, u32[]{:S(2)}) collective-permute-start(bf16[64,128]{1,0:T(8,128)(2,1)S(1)} %get-tuple-element.22), channel_id=1, source_target_pairs={{0,2},{1,7},{2,0},{3,5},{4,6},{5,3},{6,4},{7,1},{8,10},{9,15},{10,... | collective-permute-start | bytes 49160 | tf_op jit(solution)/shard_map/ppermute | solution.py:352
  9.3 0.0 collective-permute-done.refs_0_.solo_ref
  9.3 0.4 %weights.1.w_ref.refs_2_ = bf16[128,1024]{1,0:T(8,128)(2,1)S(1)} custom-call(bf16[1024,128]{1,0:T(8,128)(2,1)S(1)} %get-tuple-element.15.w_ref, bf16[144,128]{1,0:T(8,128)(2,1)S(1)} %core.3._.refs_0_), custom_call_target="tpu_custom_call" | custom-call | tf_op jit(solution)/shard_map/weights/pallas_call | solution.py:380
  9.7 2.1 %collective-permute-done.2.refs_1_.refs_0_ = bf16[320,128]{1,0:T(8,128)(2,1)S(1)} collective-permute-done((bf16[320,128]{1,0:T(8,128)(2,1)S(1)}, bf16[320,128]{1,0:T(8,128)(2,1)S(1)}, u32[]{:S(2)}, u32[]{:S(2)}) %collective-permute-start.2) | collective-permute-done | bytes 81952 | tf_op jit(solution)/shard_map/ppermute | solution.py:352
  11.8 0.1 collective-permute-start.3
  11.9 1.1 %collective-permute-done.4.refs_0_ = bf16[64,128]{1,0:T(8,128)(2,1)S(1)} collective-permute-done((bf16[64,128]{1,0:T(8,128)(2,1)S(1)}, bf16[64,128]{1,0:T(8,128)(2,1)S(1)}, u32[]{:S(2)}, u32[]{:S(2)}) %collective-permute-start.4) | collective-permute-done | bytes 16416 | tf_op jit(solution)/shard_map/ppermute | solution.py:352
  13.0 0.0 collective-permute-done.5.refs_1_
  13.0 0.2 %collective-permute-start.6 = (bf16[64,128]{1,0:T(8,128)(2,1)S(1)}, bf16[64,128]{1,0:T(8,128)(2,1)S(1)}, u32[]{:S(2)}, u32[]{:S(2)}) collective-permute-start(bf16[64,128]{1,0:T(8,128)(2,1)S(1)} %core.5), channel_id=1, source_target_pairs={{0,1},{1,0},{2,3},{3,2},{4,5},{5,4},{6,7},{7,6},{8,9},{9,8},{10,11... | collective-permute-start | bytes 49160 | tf_op jit(solution)/shard_map/ppermute | solution.py:343
  13.3 0.0 collective-permute-done.3.refs_1_
  13.3 0.9 %near.1 = (bf16[1,8,64,128]{3,2,1,0:T(8,128)(2,1)S(1)}, bf16[2048,256]{1,0:T(8,128)(2,1)S(1)}) custom-call(f32[1,128]{1,0:T(1,128)S(1)} %get-tuple-element.14.offset.offset_ref, bf16[128,1024]{1,0:T(8,128)(2,1)S(1)} %weights.1.w_ref.refs_2_, bf16[256,128]{1,0:T(8,128)(2,1)S(1)} %get-tuple-element.17.own_ref, ...), custom_call_target="tpu_custom_call" | custom-call | tf_op jit(solution)/shard_map/near/pallas_call | solution.py:408
  14.1 0.1 collective-permute-done.6.refs_2_
  14.2 1.5 %far.1 = bf16[2,8,64,128]{3,2,1,0:T(8,128)(2,1)} custom-call(f32[1,128]{1,0:T(1,128)S(1)} %get-tuple-element.14.offset.offset_ref, bf16[128,1024]{1,0:T(8,128)(2,1)S(1)} %weights.1.w_ref.refs_2_, bf16[2048,256]{1,0:T(8,128)(2,1)S(1)} %get-tuple-element.19.weights_ref, bf16[1,8,64,128]{3,2,1,0:T(8,128)(2,1)S(1)} %get-tuple-element.20.near_ref, ...), custom_call_target="tpu_custom_call" | custom-call | tf_op jit(solution)/shard_map/far/pallas_call | solution.py:421
  (4 shorter events, 0.0 us)
Async XLA Ops:
  1.6 3.2 %collective-permute-start.1 = (bf16[256,128]{1,0:T(8,128)(2,1)S(1)}, bf16[256,128]{1,0:T(8,128)(2,1)S(1)}, u32[]{:S(2)}, u32[]{:S(2)}) collective-permute-start(bf16[256,128]{1,0:T(8,128)(2,1)S(1)} %get-tuple-element.17.own_ref), channel_id=1, source_target_pairs={{0,1},{1,0},{2,3},{3,2},{4,5},{5,4},{6,7},{7,6},{8,9},{9,8},{10,11... | collective-permute-start | bytes 196616 | tf_op jit(solution)/shard_map/ppermute | solution.py:343
  2.2 7.1 %collective-permute-start = (bf16[160,128]{1,0:T(8,128)(2,1)S(1)}, bf16[160,128]{1,0:T(8,128)(2,1)S(1)}, u32[]{:S(2)}, u32[]{:S(2)}) collective-permute-start(bf16[160,128]{1,0:T(8,128)(2,1)S(1)} %get-tuple-element.16), channel_id=1, source_target_pairs={{0,4},{1,5},{2,6},{3,7},{4,8},{5,9},{6,10},{7,11},{8,12},{9,13},{1... | collective-permute-start | bytes 122888 | tf_op jit(solution)/shard_map/ppermute | solution.py:352
  4.8 7.0 %collective-permute-start.2 = (bf16[320,128]{1,0:T(8,128)(2,1)S(1)}, bf16[320,128]{1,0:T(8,128)(2,1)S(1)}, u32[]{:S(2)}, u32[]{:S(2)}) collective-permute-start(bf16[320,128]{1,0:T(8,128)(2,1)S(1)} %get-tuple-element.18), channel_id=1, source_target_pairs={{0,8},{1,13},{2,10},{3,15},{4,12},{5,1},{6,14},{7,3},{8,0},{9,5},{... | collective-permute-start | bytes 245768 | tf_op jit(solution)/shard_map/ppermute | solution.py:352
  7.5 5.5 %collective-permute-start.4 = (bf16[64,128]{1,0:T(8,128)(2,1)S(1)}, bf16[64,128]{1,0:T(8,128)(2,1)S(1)}, u32[]{:S(2)}, u32[]{:S(2)}) collective-permute-start(bf16[64,128]{1,0:T(8,128)(2,1)S(1)} %get-tuple-element.21), channel_id=1, source_target_pairs={{0,10},{1,15},{2,8},{3,13},{4,14},{5,11},{6,12},{7,9},{8,2},{9,7},... | collective-permute-start | bytes 49160 | tf_op jit(solution)/shard_map/ppermute | solution.py:352
  8.7 4.3 %collective-permute-start.5 = (bf16[64,128]{1,0:T(8,128)(2,1)S(1)}, bf16[64,128]{1,0:T(8,128)(2,1)S(1)}, u32[]{:S(2)}, u32[]{:S(2)}) collective-permute-start(bf16[64,128]{1,0:T(8,128)(2,1)S(1)} %get-tuple-element.22), channel_id=1, source_target_pairs={{0,2},{1,7},{2,0},{3,5},{4,6},{5,3},{6,4},{7,1},{8,10},{9,15},{10,... | collective-permute-start | bytes 49160 | tf_op jit(solution)/shard_map/ppermute | solution.py:352
  11.8 1.4 %collective-permute-start.3 = (bf16[432,128]{1,0:T(8,128)(2,1)S(1)}, bf16[432,128]{1,0:T(8,128)(2,1)S(1)}, u32[]{:S(2)}, u32[]{:S(2)}) collective-permute-start(bf16[432,128]{1,0:T(8,128)(2,1)S(1)} %core.4), channel_id=1, source_target_pairs={{0,1},{1,0},{2,3},{3,2},{4,5},{5,4},{6,7},{7,6},{8,9},{9,8},{10,11... | collective-permute-start | bytes 331784 | tf_op jit(solution)/shard_map/ppermute | solution.py:343
  13.0 1.2 %collective-permute-start.6 = (bf16[64,128]{1,0:T(8,128)(2,1)S(1)}, bf16[64,128]{1,0:T(8,128)(2,1)S(1)}, u32[]{:S(2)}, u32[]{:S(2)}) collective-permute-start(bf16[64,128]{1,0:T(8,128)(2,1)S(1)} %core.5), channel_id=1, source_target_pairs={{0,1},{1,0},{2,3},{3,2},{4,5},{5,4},{6,7},{7,6},{8,9},{9,8},{10,11... | collective-permute-start | bytes 49160 | tf_op jit(solution)/shard_map/ppermute | solution.py:343
